TPU v7x, 256 devices: a whole 4x4x8 slice. The times are simulated.
256 devices in a mesh: lon: 32 (over z_lo, x, core), lat: 8 (over z_hi, y).
Axes of the slice: x: 4, y: 4, z: 8 (z_hi: 2, z_lo: 4; z = z_hi * 4 + z_lo), core: 2. Of those that a mesh axis runs over, the one named last changes fastest.
Arguments:
- warmth_anomaly: float32 [16, 256, 4096], P(None, 'lat', 'lon'), may hold values from -6 to 6
- brine_anomaly: float32 [16, 256, 4096], P(None, 'lat', 'lon'), may hold values from -6 to 6
- zonal_speed: float32 [16, 256, 4096], P(None, 'lat', 'lon'), may hold values from -3 to 3
- meridional_speed: float32 [16, 256, 4096], P(None, 'lat', 'lon'), may hold values from -3 to 3
- upper_bound_stress: float32 [256, 4096], P('lat', 'lon'), may hold values from -6 to 6
- sea_indicator: int32 [16, 256, 4096], P(None, 'lat', 'lon'), may hold values 0 or 1
Outputs:
- temperature_out: float32 [16, 256, 4096], P(None, 'lat', 'lon')
- salinity_out: float32 [16, 256, 4096], P(None, 'lat', 'lon')
- zonal_out: float32 [16, 256, 4096], P(None, 'lat', 'lon')
- meridional_out: float32 [16, 256, 4096], P(None, 'lat', 'lon')
- pressure_out: float32 [16, 256, 4096], P(None, 'lat', 'lon')
All inputs are finite; a program needn't handle non-finite values. No bound on the sum of `sea_indicator` on one device may be relied on, other than what follows from the above.
Results may differ from a plain program's by a relative error of at most 0.00002.
Values sent between devices are 32-bit elements; how exact they have to be, the bound alone decides.
No kernel may reach another device: no remote copies, remote signals or barrier semaphores. Data moves between devices by JAX's collectives and lax.ppermute only.
A program may use at most 64 MiB of HBM per device.

v0:
```python
import jax
import jax.numpy as jnp
from jax import lax
from jax.sharding import PartitionSpec as P

STEPS = 2


HEAT_EXPANSION = 0.2
SALT_CONTRACTION = 0.15
GRAVITY = 0.5
TIME_STEP = 0.2
VISCOSITY = 0.25
DIFFUSIVITY = 0.2
ROTATION = 1.0


def padded_2(value, sides, width):
    for axis, dim in sides:
        count, length = (lax.axis_size(axis), value.shape[dim])
        up = [(i, (i + 1) % count) for i in range(count)]
        down = [(j, i) for i, j in up]
        last = lax.slice_in_dim(value, length - width, length, axis=dim)
        initial = lax.slice_in_dim(value, 0, width, axis=dim)
        before = lax.ppermute(last, axis, up)
        after = lax.ppermute(initial, axis, down)
        value = jnp.concatenate([before, value, after], axis=dim)
    return value


def stratum_stress(warmth_anomaly, brine_anomaly, uppermost_stratum):
    seawater_heaviness = -HEAT_EXPANSION * warmth_anomaly + SALT_CONTRACTION * brine_anomaly
    running = jnp.zeros_like(seawater_heaviness[0])
    levels = []
    for level_number in range(seawater_heaviness.shape[0]):
        layer = seawater_heaviness[level_number]
        levels.append(uppermost_stratum + GRAVITY * (running + 0.5 * layer))
        running = running + layer
    return jnp.stack(levels, axis=0)


def neighbours(field):
    return (
        field[:, 1:-1, 1:-1],
        field[:, 1:-1, 2:],
        field[:, 1:-1, :-2],
        field[:, 2:, 1:-1],
        field[:, :-2, 1:-1],
    )


def laplace(parts):
    return parts[1] + parts[2] + parts[3] + parts[4] - 4.0 * parts[0]


def march_forward(temp_wide, salt_wide, zonal_wide, merid_wide, press_wide, wet_mask, coriolis):
    zonal = neighbours(zonal_wide)
    merid = neighbours(merid_wide)
    hydro_stress = neighbours(press_wide)
    easterly_speed_current = zonal[0]
    northerly_speed_current = merid[0]
    grad_x = 0.5 * (hydro_stress[1] - hydro_stress[2])
    grad_y = 0.5 * (hydro_stress[3] - hydro_stress[4])
    zonal_next = wet_mask * (
        easterly_speed_current
        + TIME_STEP * (coriolis * northerly_speed_current - grad_x + VISCOSITY * laplace(zonal))
    )
    merid_next = wet_mask * (
        northerly_speed_current
        + TIME_STEP * (-coriolis * easterly_speed_current - grad_y + VISCOSITY * laplace(merid))
    )

    def tracer(wide_field):
        parts = neighbours(wide_field)
        transport = -0.5 * (
            easterly_speed_current * (parts[1] - parts[2])
            + northerly_speed_current * (parts[3] - parts[4])
        )
        return wet_mask * (parts[0] + TIME_STEP * (transport + DIFFUSIVITY * laplace(parts)))

    return (tracer(temp_wide), tracer(salt_wide), zonal_next, merid_next)


def fetch_fold(top_rows):
    lon_count = lax.axis_size("lon")
    row_shape = top_rows.shape
    flat = top_rows.reshape(-1)
    total = flat.shape[0]
    piece_width = -(-total // lon_count)
    padded = flat.reshape(lon_count, piece_width)
    spread = lax.all_to_all(padded, "lon", split_axis=0, concat_axis=0, tiled=True)
    returned = lax.all_to_all(spread[::-1], "lon", split_axis=0, concat_axis=0, tiled=True)
    partner = returned.reshape(-1).reshape(row_shape)
    return partner[:, ::-1]


def extend_all(stacked, flip_signs):
    lat_id = lax.axis_index("lat")
    lat_count = lax.axis_size("lat")
    widened = padded_2(stacked, (("lat", 1), ("lon", 2)), 1)
    fold_row = fetch_fold(stacked[:, -1, :]) * flip_signs[:, None]
    north_row = jnp.where(lat_id == lat_count - 1, fold_row, widened[:, -1, 1:-1])
    south_row = jnp.where(lat_id == 0, jnp.zeros_like(fold_row), widened[:, 0, 1:-1])
    north_full = jnp.concatenate(
        [widened[:, -1:, :1], north_row[:, None, :], widened[:, -1:, -1:]], axis=2
    )
    south_full = jnp.concatenate(
        [widened[:, :1, :1], south_row[:, None, :], widened[:, :1, -1:]], axis=2
    )
    return jnp.concatenate([south_full, widened[:, 1:-1, :], north_full], axis=1)


def on_device(
    warmth_anomaly, brine_anomaly, zonal_speed, meridional_speed, upper_bound_stress, sea_indicator
):
    vertical_strata, meridional_position, zonal_position = warmth_anomaly.shape
    total_rows = meridional_position * lax.axis_size("lat")
    wet_mask = sea_indicator.astype(jnp.float32)
    row_index = (
        lax.axis_index("lat") * meridional_position + jnp.arange(meridional_position)
    ).astype(jnp.float32)
    coriolis = (ROTATION * (2.0 * (row_index + 0.5) / total_rows - 1.0))[:, None]
    plus_ones = jnp.ones((vertical_strata,), jnp.float32)
    existing_warmth, existing_brine = (warmth_anomaly, brine_anomaly)
    easterly_speed_current, northerly_speed_current = (zonal_speed, meridional_speed)
    for step_index in range(STEPS):
        hydro_stress = stratum_stress(existing_warmth, existing_brine, upper_bound_stress)
        stacked = jnp.concatenate(
            [
                hydro_stress,
                existing_warmth,
                existing_brine,
                easterly_speed_current,
                northerly_speed_current,
            ],
            axis=0,
        )
        flip_signs = jnp.concatenate([plus_ones, plus_ones, plus_ones, -plus_ones, -plus_ones])
        widened = extend_all(stacked, flip_signs)
        press_wide = widened[0:vertical_strata]
        temp_wide = widened[vertical_strata : 2 * vertical_strata]
        salt_wide = widened[2 * vertical_strata : 3 * vertical_strata]
        zonal_wide = widened[3 * vertical_strata : 4 * vertical_strata]
        merid_wide = widened[4 * vertical_strata : 5 * vertical_strata]
        existing_warmth, existing_brine, easterly_speed_current, northerly_speed_current = (
            march_forward(
                temp_wide, salt_wide, zonal_wide, merid_wide, press_wide, wet_mask, coriolis
            )
        )
    ending_stress = stratum_stress(existing_warmth, existing_brine, upper_bound_stress)
    return (
        existing_warmth,
        existing_brine,
        easterly_speed_current,
        northerly_speed_current,
        ending_stress,
    )


def solution(mesh):
    in_specs = (
        P(None, "lat", "lon"),
        P(None, "lat", "lon"),
        P(None, "lat", "lon"),
        P(None, "lat", "lon"),
        P("lat", "lon"),
        P(None, "lat", "lon"),
    )
    out_specs = (
        P(None, "lat", "lon"),
        P(None, "lat", "lon"),
        P(None, "lat", "lon"),
        P(None, "lat", "lon"),
        P(None, "lat", "lon"),
    )
    return jax.shard_map(
        on_device, mesh=mesh, in_specs=in_specs, out_specs=out_specs, check_vma=False
    )
```

profile of v0, /device:TPU:1, one launch (start us, length us, event | category | flops | bytes accessed | tf_op | source)
XLA Modules:
  0.0 143.8 jit_solution(8065771772323693175)
XLA Ops:
  7.7 10.0 %all-to-all-start = ((f32[32,1,320]{2,1,0:T(1,128)}), f32[32,1,320]{2,1,0:T(1,128)S(1)}, u32[]{:S(2)}, u32[]{:S(2)}) async-start(f32[32,1,320]{2,1,0:T(1,128)} %all_to_all.38), calls=%async_computation | async-start | bytes 98304 | tf_op jit(solution)/shard_map/all_to_all | solution.py:91
  17.7 6.7 %collective-permute-start.1 = (f32[80,1,128]{2,1,0:T(1,128)S(1)}, f32[80,1,128]{2,1,0:T(1,128)S(1)}, u32[]{:S(2)}, u32[]{:S(2)}) collective-permute-start(f32[80,1,128]{2,1,0:T(1,128)S(1)} %get-tuple-element.64), channel_id=1, source_target_pairs={{1,0},{2,1},{3,2},{4,3},{5,4},{6,5},{7,6},{0,7},{9,8},{10,9},{11,1... | collective-permute-start | bytes 122888 | tf_op jit(solution)/shard_map/ppermute | solution.py:26
  25.5 7.8 %collective-permute-done = f32[80,1,128]{2,1,0:T(1,128)S(1)} collective-permute-done((f32[80,1,128]{2,1,0:T(1,128)S(1)}, f32[80,1,128]{2,1,0:T(1,128)S(1)}, u32[]{:S(2)}, u32[]{:S(2)}) %collective-permute-start) | collective-permute-done | bytes 40992 | tf_op jit(solution)/shard_map/ppermute | solution.py:25
  33.6 2.2 %fusion.115 = (f32[80,34,1]{2,1,0:T(8,128)}, f32[80,34,1]{2,1,0:T(8,128)}) fusion(f32[80,34,128]{2,1,0:T(8,128)S(1)} %pad_maximum_fusion.8), kind=kLoop, calls=%fused_computation.273 | loop fusion | bytes 43520 | tf_op jit(solution)/shard_map/slice | solution.py:23
  35.8 2.0 %copy.223 = f32[80,34,1]{0,2,1:T(1,128)S(1)} copy(f32[80,34,1]{2,1,0:T(8,128)} %get-tuple-element.58) | data formatting | bytes 21760 | tf_op jit(solution)/shard_map/slice | solution.py:23
  38.3 1.8 %collective-permute-start.2 = (f32[80,34,1]{0,2,1:T(1,128)S(1)}, f32[80,34,1]{0,2,1:T(1,128)S(1)}, u32[]{:S(2)}, u32[]{:S(2)}) collective-permute-start(f32[80,34,1]{0,2,1:T(1,128)S(1)} %copy.221), channel_id=1, source_target_pairs={{8,0},{16,8},{24,16},{32,24},{40,32},{48,40},{56,48},{64,56},{72,6... | collective-permute-start | bytes 32648 | tf_op jit(solution)/shard_map/ppermute | solution.py:26
  40.1 1.8 %collective-permute-start.3 = (f32[80,34,1]{0,2,1:T(1,128)S(1)}, f32[80,34,1]{0,2,1:T(1,128)S(1)}, u32[]{:S(2)}, u32[]{:S(2)}) collective-permute-start(f32[80,34,1]{0,2,1:T(1,128)S(1)} %copy.223), channel_id=1, source_target_pairs={{0,8},{8,16},{16,24},{24,32},{32,40},{40,48},{48,56},{56,64},{64,7... | collective-permute-start | bytes 32648 | tf_op jit(solution)/shard_map/ppermute | solution.py:25
  45.7 1.8 %copy.224 = f32[80,34,1]{2,1,0:T(8,128)} copy(f32[80,34,1]{0,2,1:T(1,128)S(1)} %collective-permute-done.3) | data formatting | bytes 21760 | tf_op jit(solution)/shard_map/ppermute | solution.py:25
  47.5 1.7 %copy.222 = f32[80,34,1]{2,1,0:T(8,128)} copy(f32[80,34,1]{0,2,1:T(1,128)S(1)} %collective-permute-done.2) | data formatting | bytes 21760 | tf_op jit(solution)/shard_map/ppermute | solution.py:26
  49.9 10.6 %all-to-all-start.1 = ((f32[32,1,320]{2,1,0:T(1,128)}), f32[32,1,320]{2,1,0:T(1,128)}, u32[]{:S(2)}, u32[]{:S(2)}) async-start(f32[32,1,320]{2,1,0:T(1,128)} %copy.228), calls=%async_computation.1 | async-start | bytes 98304 | tf_op jit(solution)/shard_map/all_to_all | solution.py:92
  60.5 3.6 %pad_maximum_fusion.4 = f32[80,32,130]{2,1,0:T(8,128)S(1)} fusion(f32[80,34,1]{2,1,0:T(8,128)} %copy.222, f32[80,34,1]{2,1,0:T(8,128)} %copy.224, f32[80,1,128]{2,1,0:T(1,128)S(1)} %collective-permute-done.1, f32[80,32,128]{2,1,0:T(8,128)} %copy-done.7, f32[80,1,128]{2,1,0:T(1,128)S(1)} %collective-permute-done), kind=kLoop, calls=%fused_computation.4 | loop fusion | flops 1331200 | bytes 2745600 | tf_op jit(solution)/shard_map/concatenate | solution.py:27
  68.9 1.5 %reduce.1 = f32[32,320]{1,0:T(8,128)} reduce(f32[32,1,320]{2,1,0:T(1,128)} %all-to-all-done.1, f32[]{:T(128)} %constant.43), dimensions={1}, to_apply=%all_to_all.32.reduce_sub_computation | reduce | bytes 81924 | tf_op jit(solution)/shard_map/all_to_all | solution.py:92
  75.3 2.9 %multiply_add_fusion.1 = (f32[16,32,128]{2,1,0:T(8,128)S(1)}, f32[16,32,128]{2,1,0:T(8,128)S(1)}, f32[16,32,128]{2,1,0:T(8,128)S(1)}) fusion(f32[16,32,128]{2,1,0:T(8,128)} %param.7, f32[16,32,128]{2,1,0:T(8,128)S(1)} %copy-done.11, f32[80,32,130]{2,1,0:T(8,128)S(1)} %pad_maximum_fusion.4, f32[80,1,1]{2,1,0:T(1,128)} %copy.233, ...), kind=kLoop, calls=%fused_computation.97 | loop fusion | flops 3670016 | bytes 4925952 | tf_op jit(solution)/shard_map/add | solution.py:32
  85.2 8.4 %all-to-all-start.2 = ((f32[32,1,320]{2,1,0:T(1,128)}), f32[32,1,320]{2,1,0:T(1,128)S(1)}, u32[]{:S(2)}, u32[]{:S(2)}) async-start(f32[32,1,320]{2,1,0:T(1,128)} %all_to_all.39), calls=%async_computation.2 | async-start | bytes 98304 | tf_op jit(solution)/shard_map/all_to_all | solution.py:91
  93.7 1.5 %pad_maximum_fusion.9 = f32[80,34,128]{2,1,0:T(8,128)S(1)} fusion(f32[80,1,128]{2,1,0:T(1,128)S(1)} %bitcast.568, f32[80,32,128]{2,1,0:T(8,128)} %copy-done.5, f32[80,1,128]{2,1,0:T(1,128)S(1)} %collective-permute-done.4), kind=kLoop, calls=%fused_computation.9 | loop fusion | flops 696320 | bytes 2785280 | tf_op jit(solution)/shard_map/concatenate | solution.py:27
  95.2 1.7 %fusion.114 = (f32[80,34,1]{2,1,0:T(8,128)}, f32[80,34,1]{2,1,0:T(8,128)S(1)}) fusion(f32[80,34,128]{2,1,0:T(8,128)S(1)} %pad_maximum_fusion.9), kind=kLoop, calls=%fused_computation.272 | loop fusion | bytes 43520 | tf_op jit(solution)/shard_map/slice | solution.py:23
  96.9 1.9 %copy.238 = f32[80,34,1]{0,2,1:T(1,128)S(1)} copy(f32[80,34,1]{2,1,0:T(8,128)} %get-tuple-element.56) | data formatting | bytes 21760 | tf_op jit(solution)/shard_map/slice | solution.py:23
  103.0 2.8 %collective-permute-done.7 = f32[80,34,1]{0,2,1:T(1,128)S(1)} collective-permute-done((f32[80,34,1]{0,2,1:T(1,128)S(1)}, f32[80,34,1]{0,2,1:T(1,128)S(1)}, u32[]{:S(2)}, u32[]{:S(2)}) %collective-permute-start.7) | collective-permute-done | bytes 10912 | tf_op jit(solution)/shard_map/ppermute | solution.py:25
  106.3 1.7 %copy.239 = f32[80,34,1]{2,1,0:T(8,128)} copy(f32[80,34,1]{0,2,1:T(1,128)S(1)} %collective-permute-done.7) | data formatting | bytes 21760 | tf_op jit(solution)/shard_map/ppermute | solution.py:25
  108.1 1.8 %copy.237 = f32[80,34,1]{2,1,0:T(8,128)} copy(f32[80,34,1]{0,2,1:T(1,128)S(1)} %collective-permute-done.6) | data formatting | bytes 21760 | tf_op jit(solution)/shard_map/ppermute | solution.py:26
  110.6 10.6 %all-to-all-start.3 = ((f32[32,1,320]{2,1,0:T(1,128)}), f32[32,1,320]{2,1,0:T(1,128)}, u32[]{:S(2)}, u32[]{:S(2)}) async-start(f32[32,1,320]{2,1,0:T(1,128)} %copy.243), calls=%async_computation.3 | async-start | bytes 98304 | tf_op jit(solution)/shard_map/all_to_all | solution.py:92
  121.1 3.6 %pad_maximum_fusion = f32[80,32,130]{2,1,0:T(8,128)S(1)} fusion(f32[80,34,1]{2,1,0:T(8,128)} %copy.237, f32[80,34,1]{2,1,0:T(8,128)} %copy.239, f32[80,1,128]{2,1,0:T(1,128)S(1)} %bitcast.569, f32[80,32,128]{2,1,0:T(8,128)} %copy-done.5, f32[80,1,128]{2,1,0:T(1,128)S(1)} %collective-permute-done.4), kind=kLoop, calls=%fused_computation | loop fusion | flops 1331200 | bytes 2745600 | tf_op jit(solution)/shard_map/concatenate | solution.py:27
  129.5 1.5 %reduce.3 = f32[32,320]{1,0:T(8,128)} reduce(f32[32,1,320]{2,1,0:T(1,128)} %all-to-all-done.3, f32[]{:T(128)} %constant.43), dimensions={1}, to_apply=%all_to_all.37.reduce_sub_computation | reduce | bytes 81924 | tf_op jit(solution)/shard_map/all_to_all | solution.py:92
  135.9 3.7 %multiply_add_fusion = (f32[16,32,128]{2,1,0:T(8,128)S(1)}, f32[16,32,128]{2,1,0:T(8,128)}, f32[16,32,128]{2,1,0:T(8,128)}) fusion(f32[16,32,128]{2,1,0:T(8,128)} %copy-done.17, f32[16,32,128]{2,1,0:T(8,128)S(1)} %get-tuple-element.26, f32[80,32,130]{2,1,0:T(8,128)S(1)} %pad_maximum_fusion, f32[80,1,1]{2,1,0:T(1,128)} %copy.248, ...), kind=kLoop, calls=%fused_computation.94 | loop fusion | flops 3670016 | bytes 4925952 | tf_op jit(solution)/shard_map/add | solution.py:32
  (170 shorter events, 48.8 us)
Async XLA Ops:
  0.6 5.9 %copy-start.15 = (f32[16,32,128]{2,1,0:T(8,128)S(1)}, f32[16,32,128]{2,1,0:T(8,128)}, u32[]{:S(2)}) copy-start(f32[16,32,128]{2,1,0:T(8,128)} %param.7) | copy-start | bytes 786436
  0.6 5.8 %copy-start.16 = (f32[16,32,128]{2,1,0:T(8,128)S(1)}, f32[16,32,128]{2,1,0:T(8,128)}, u32[]{:S(2)}) copy-start(f32[16,32,128]{2,1,0:T(8,128)} %param.6) | copy-start | bytes 786436
  0.7 5.6 %copy-start.4 = (f32[32,128]{1,0:T(8,128)S(1)}, f32[32,128]{1,0:T(8,128)}, u32[]{:S(2)}) copy-start(f32[32,128]{1,0:T(8,128)} %param.10) | copy-start | bytes 49156
  1.8 4.7 %copy-start.13 = (f32[16,32,128]{2,1,0:T(8,128)S(1)}, f32[16,32,128]{2,1,0:T(8,128)}, u32[]{:S(2)}) copy-start(f32[16,32,128]{2,1,0:T(8,128)} %param.8) | copy-start | bytes 786436
  6.6 27.0 %copy-start.7 = (f32[80,32,128]{2,1,0:T(8,128)}, f32[80,32,128]{2,1,0:T(8,128)S(1)}, u32[]{:S(2)}) copy-start(f32[80,32,128]{2,1,0:T(8,128)S(1)} %constant_dynamic-update-slice_fusion) | copy-start | bytes 3932164
  7.7 41.5 %all-to-all-start = ((f32[32,1,320]{2,1,0:T(1,128)}), f32[32,1,320]{2,1,0:T(1,128)S(1)}, u32[]{:S(2)}, u32[]{:S(2)}) async-start(f32[32,1,320]{2,1,0:T(1,128)} %all_to_all.38), calls=%async_computation | async-start | bytes 98304 | tf_op jit(solution)/shard_map/all_to_all | solution.py:91
  17.7 7.8 %collective-permute-start.1 = (f32[80,1,128]{2,1,0:T(1,128)S(1)}, f32[80,1,128]{2,1,0:T(1,128)S(1)}, u32[]{:S(2)}, u32[]{:S(2)}) collective-permute-start(f32[80,1,128]{2,1,0:T(1,128)S(1)} %get-tuple-element.64), channel_id=1, source_target_pairs={{1,0},{2,1},{3,2},{4,3},{5,4},{6,5},{7,6},{0,7},{9,8},{10,9},{11,1... | collective-permute-start | bytes 122888 | tf_op jit(solution)/shard_map/ppermute | solution.py:26
  24.4 8.9 %collective-permute-start = (f32[80,1,128]{2,1,0:T(1,128)S(1)}, f32[80,1,128]{2,1,0:T(1,128)S(1)}, u32[]{:S(2)}, u32[]{:S(2)}) collective-permute-start(f32[80,1,128]{2,1,0:T(1,128)S(1)} %get-tuple-element.65), channel_id=1, source_target_pairs={{0,1},{1,2},{2,3},{3,4},{4,5},{5,6},{6,7},{7,0},{8,9},{9,10},{10,1... | collective-permute-start | bytes 122888 | tf_op jit(solution)/shard_map/ppermute | solution.py:25
  38.3 5.0 %collective-permute-start.2 = (f32[80,34,1]{0,2,1:T(1,128)S(1)}, f32[80,34,1]{0,2,1:T(1,128)S(1)}, u32[]{:S(2)}, u32[]{:S(2)}) collective-permute-start(f32[80,34,1]{0,2,1:T(1,128)S(1)} %copy.221), channel_id=1, source_target_pairs={{8,0},{16,8},{24,16},{32,24},{40,32},{48,40},{56,48},{64,56},{72,6... | collective-permute-start | bytes 32648 | tf_op jit(solution)/shard_map/ppermute | solution.py:26
  40.1 5.1 %collective-permute-start.3 = (f32[80,34,1]{0,2,1:T(1,128)S(1)}, f32[80,34,1]{0,2,1:T(1,128)S(1)}, u32[]{:S(2)}, u32[]{:S(2)}) collective-permute-start(f32[80,34,1]{0,2,1:T(1,128)S(1)} %copy.223), channel_id=1, source_target_pairs={{0,8},{8,16},{16,24},{24,32},{32,40},{40,48},{48,56},{56,64},{64,7... | collective-permute-start | bytes 32648 | tf_op jit(solution)/shard_map/ppermute | solution.py:25
  49.9 19.0 %all-to-all-start.1 = ((f32[32,1,320]{2,1,0:T(1,128)}), f32[32,1,320]{2,1,0:T(1,128)}, u32[]{:S(2)}, u32[]{:S(2)}) async-start(f32[32,1,320]{2,1,0:T(1,128)} %copy.228), calls=%async_computation.1 | async-start | bytes 98304 | tf_op jit(solution)/shard_map/all_to_all | solution.py:92
  60.5 13.0 %copy-start.23 = (f32[80]{0:T(128)S(1)}, f32[80]{0:T(128)}, u32[]{:S(2)}) copy-start(f32[80]{0:T(128)} %constant.10.clone.1) | copy-start | bytes 964
  60.5 14.8 %copy-start.9 = (s32[16,32,128]{2,1,0:T(8,128)S(1)}, s32[16,32,128]{2,1,0:T(8,128)}, u32[]{:S(2)}) copy-start(s32[16,32,128]{2,1,0:T(8,128)} %param.11) | copy-start | bytes 786436
  75.3 3.4 %copy-start.3 = (f32[80,34,1]{2,1,0:T(8,128)S(1)}, f32[80,34,1]{2,1,0:T(8,128)}, u32[]{:S(2)}) copy-start(f32[80,34,1]{2,1,0:T(8,128)} %copy.222) | copy-start | bytes 32644
  75.3 3.4 %copy-start.8 = (f32[80,32,128]{2,1,0:T(8,128)S(1)}, f32[80,32,128]{2,1,0:T(8,128)}, u32[]{:S(2)}) copy-start(f32[80,32,128]{2,1,0:T(8,128)} %copy-done.7) | copy-start | bytes 3932164
  78.2 2.5 %copy-start.17 = (f32[16,32,128]{2,1,0:T(8,128)}, f32[16,32,128]{2,1,0:T(8,128)S(1)}, u32[]{:S(2)}) copy-start(f32[16,32,128]{2,1,0:T(8,128)S(1)} %get-tuple-element.42) | copy-start | bytes 786436
  82.8 10.9 %collective-permute-start.5 = (f32[80,1,128]{2,0,1:T(8,128)S(1)}, f32[80,1,128]{2,0,1:T(8,128)S(1)}, u32[]{:S(2)}, u32[]{:S(2)}) collective-permute-start(f32[80,1,128]{2,0,1:T(8,128)S(1)} %bitcast.578), channel_id=1, source_target_pairs={{1,0},{2,1},{3,2},{4,3},{5,4},{6,5},{7,6},{0,7},{9,8},{10,9},{11,1... | collective-permute-start | bytes 122888 | tf_op jit(solution)/shard_map/ppermute | solution.py:26
  83.1 10.6 %collective-permute-start.4 = (f32[80,1,128]{2,1,0:T(1,128)S(1)}, f32[80,1,128]{2,1,0:T(1,128)S(1)}, u32[]{:S(2)}, u32[]{:S(2)}) collective-permute-start(f32[80,1,128]{2,1,0:T(1,128)S(1)} %get-tuple-element.62), channel_id=1, source_target_pairs={{0,1},{1,2},{2,3},{3,4},{4,5},{5,6},{6,7},{7,0},{8,9},{9,10},{10,1... | collective-permute-start | bytes 122888 | tf_op jit(solution)/shard_map/ppermute | solution.py:25
  85.2 24.6 %all-to-all-start.2 = ((f32[32,1,320]{2,1,0:T(1,128)}), f32[32,1,320]{2,1,0:T(1,128)S(1)}, u32[]{:S(2)}, u32[]{:S(2)}) async-start(f32[32,1,320]{2,1,0:T(1,128)} %all_to_all.39), calls=%async_computation.2 | async-start | bytes 98304 | tf_op jit(solution)/shard_map/all_to_all | solution.py:91
  99.3 3.2 %collective-permute-start.6 = (f32[80,34,1]{0,2,1:T(1,128)S(1)}, f32[80,34,1]{0,2,1:T(1,128)S(1)}, u32[]{:S(2)}, u32[]{:S(2)}) collective-permute-start(f32[80,34,1]{0,2,1:T(1,128)S(1)} %copy.236), channel_id=1, source_target_pairs={{8,0},{16,8},{24,16},{32,24},{40,32},{48,40},{56,48},{64,56},{72,6... | collective-permute-start | bytes 32648 | tf_op jit(solution)/shard_map/ppermute | solution.py:26
  99.7 6.1 %collective-permute-start.7 = (f32[80,34,1]{0,2,1:T(1,128)S(1)}, f32[80,34,1]{0,2,1:T(1,128)S(1)}, u32[]{:S(2)}, u32[]{:S(2)}) collective-permute-start(f32[80,34,1]{0,2,1:T(1,128)S(1)} %copy.238), channel_id=1, source_target_pairs={{0,8},{8,16},{16,24},{24,32},{32,40},{40,48},{48,56},{56,64},{64,7... | collective-permute-start | bytes 32648 | tf_op jit(solution)/shard_map/ppermute | solution.py:25
  110.6 18.9 %all-to-all-start.3 = ((f32[32,1,320]{2,1,0:T(1,128)}), f32[32,1,320]{2,1,0:T(1,128)}, u32[]{:S(2)}, u32[]{:S(2)}) async-start(f32[32,1,320]{2,1,0:T(1,128)} %copy.243), calls=%async_computation.3 | async-start | bytes 98304 | tf_op jit(solution)/shard_map/all_to_all | solution.py:92
  135.8 4.0 %copy-start = (f32[80,34,1]{2,1,0:T(8,128)S(1)}, f32[80,34,1]{2,1,0:T(8,128)}, u32[]{:S(2)}) copy-start(f32[80,34,1]{2,1,0:T(8,128)} %copy.239) | copy-start | bytes 32644
  135.8 4.0 %copy-start.1 = (f32[80,34,1]{2,1,0:T(8,128)S(1)}, f32[80,34,1]{2,1,0:T(8,128)}, u32[]{:S(2)}) copy-start(f32[80,34,1]{2,1,0:T(8,128)} %copy.237) | copy-start | bytes 32644
  (17 other events, 24.7 us)
where the time goes:
time: 145 us; the launch traced here: 144 us
  starting transfers between devices  53.4 us (37%)
  local copies, waits for them, and re-layouts  40.5 us (28%)
  other arithmetic  33.2 us (23%)
  waiting for transfers between devices  15.2 us (10%)
  between operations  1.46 us (1%)
    all_to_all x2, starting transfers between devices, fetch_fold(): lax.all_to_all(spread[::-1], 'lon', split_axis=0, concat_axis=0, tiled=True)  21.1 us
    all_to_all x2, starting transfers between devices, fetch_fold(): lax.all_to_all(padded, 'lon', split_axis=0, concat_axis=0, tiled=True)  18.4 us
    ppermute x4, waiting for transfers between devices, padded_2(): before = lax.ppermute(last, axis, up)  12 us
    ppermute x4, starting transfers between devices, padded_2(): after = lax.ppermute(initial, axis, down)  9.22 us
    concatenate x4, other arithmetic, padded_2(): value = jnp.concatenate([before, value, after], axis=dim)  8.95 us
    slice x6, local copies, waits for them, and re-layouts, padded_2(): last = lax.slice_in_dim(value, length - width, length, axis=dim)  8.06 us
    add x3, other arithmetic, stratum_stress(): -HEAT_EXPANSION * warmth_anomaly + SALT_CONTRACTION * brine_anomaly  7.73 us
    unnamed x48, other arithmetic  5.66 us
  transfers between devices with their start and end apart: 12, of which 6 were waited for; matrix products, arithmetic and copies ran while one was open for 26% of the time, Pallas kernels for 0%

commit v1 on v0

v1 whole, which is shorter than its diff:
```python
import jax
import jax.numpy as jnp
from jax import lax
from jax.experimental import pallas as pl
from jax.experimental.pallas import tpu as pltpu
from jax.sharding import PartitionSpec as P

STEPS = 2
HEAT_EXPANSION = 0.2
SALT_CONTRACTION = 0.15
GRAVITY = 0.5
TIME_STEP = 0.2
VISCOSITY = 0.25
DIFFUSIVITY = 0.2
ROTATION = 1.0

LEVELS = 16
ROWS = 32
LANES = 128
BLOCKS = ROWS // 8
SLOTS = LEVELS * BLOCKS

COL_T, COL_S, COL_U, COL_V, COL_WET, COL_PS = range(6)
COL_TILE = 8
COL_ROWS = 6 * COL_TILE
ROW_WET = 4 * 2 * LEVELS
ROW_PS = ROW_WET + LEVELS
ROW_CORNER = ROW_PS + 8
ROW_ROWS = ROW_CORNER + 8

FIRST = 16
EXT_ROWS = 64
EXT_LANES = 2 * LANES

VMEM = pl.BlockSpec(memory_space=pltpu.VMEM)


def lanes_of(shape):
    return lax.broadcasted_iota(jnp.int32, shape, len(shape) - 1)


def pack_columns(t_ref, s_ref, u_ref, v_ref, ps_ref, wet_ref, near_ref, far_ref):
    even = lax.axis_index("lon") % 2 == 0
    slot = lanes_of((8, LANES)) >> 1
    masks = [slot == j for j in range(SLOTS)]

    def pack(index, tiles):
        east = jnp.zeros((8, LANES), jnp.float32)
        west = jnp.zeros((8, LANES), jnp.float32)
        for j, tile in enumerate(tiles):
            rolled = pltpu.roll(tile(), (2 * j + 2) % LANES, 1)
            east = jnp.where(masks[j], rolled, east)
            west = jnp.where(masks[(j + 1) % SLOTS], rolled, west)
        rows = pl.ds(index * COL_TILE, COL_TILE)
        near_ref[rows, :] = jnp.where(even, east, west)
        far_ref[rows, :] = jnp.where(even, west, east)

    def tiles_of(ref):
        return [
            (lambda j=j: ref[j // BLOCKS, pl.ds(8 * (j % BLOCKS), 8), :].astype(jnp.float32))
            for j in range(SLOTS)
        ]

    for index, ref in ((COL_T, t_ref), (COL_S, s_ref), (COL_U, u_ref), (COL_V, v_ref), (COL_WET, wet_ref)):
        pack(index, tiles_of(ref))
    pack(COL_PS, [(lambda r=r: ps_ref[pl.ds(8 * r, 8), :]) for r in range(BLOCKS)])


def reverse_lanes(value):
    index = LANES - 1 - lanes_of(value.shape)
    return jnp.take_along_axis(value, index, axis=1, mode="promise_in_bounds")


def pack_rows(t_ref, s_ref, u_ref, v_ref, ps_ref, wet_ref, near_ref, far_ref):
    lat = lax.axis_index("lat")
    even = lat % 2 == 0
    fold = lat == lax.axis_size("lat") - 1

    def put(first, north, south, sign):
        rows = pl.ds(first, north.shape[0])
        near_ref[rows, :] = jnp.where(even, north, south)
        far_ref[rows, :] = jnp.where(even, south, north)

        @pl.when(fold)
        def _():
            far_ref[rows, :] = sign * reverse_lanes(north)

    for index, (ref, sign) in enumerate(((t_ref, 1.0), (s_ref, 1.0), (u_ref, -1.0), (v_ref, -1.0))):
        for ring in range(2):
            put(
                (2 * index + ring) * LEVELS,
                ref[:, ROWS - 1 - ring, :],
                ref[:, ring, :],
                sign,
            )
    put(ROW_WET, wet_ref[:, ROWS - 1, :].astype(jnp.float32), wet_ref[:, 0, :].astype(jnp.float32), 1.0)
    top, bottom = ps_ref[pl.ds(ROWS - 8, 8), :], ps_ref[pl.ds(0, 8), :]
    sub = lax.broadcasted_iota(jnp.int32, (8, LANES), 0)
    north = jnp.where(sub == 0, pltpu.roll(top, 1, 0), pltpu.roll(top, 3, 0))
    put(ROW_PS, north, bottom, 1.0)
    near_ref[pl.ds(ROW_CORNER, 8), :] = jnp.zeros((8, LANES), jnp.float32)
    far_ref[pl.ds(ROW_CORNER, 8), :] = jnp.zeros((8, LANES), jnp.float32)


def halo_tiles(near, far, even_lon):
    slot = lanes_of(near.shape) >> 1
    west = jnp.where(even_lon, far, near)
    east = jnp.where(even_lon, near, far)
    return (
        jnp.where(slot % 2 == 0, west, east),
        jnp.where(slot % 2 == 0, east, west),
    )


def pack_corners(near_ref, far_ref, near_out, far_out):
    lat = lax.axis_index("lat")
    even = lat % 2 == 0
    fold = lat == lax.axis_size("lat") - 1
    even_tile, odd_tile = halo_tiles(near_ref[...], far_ref[...], lax.axis_index("lon") % 2 == 0)
    lane = lanes_of((8, LANES))
    sub = lax.broadcasted_iota(jnp.int32, (8, LANES), 0)

    def gather(tile, row):
        out = jnp.zeros((8, LANES), jnp.float32)
        for index, field in enumerate((COL_T, COL_S, COL_U, COL_V, COL_PS)):
            one = pltpu.roll(tile[field * COL_TILE : (field + 1) * COL_TILE], (index - row) % 8, 0)
            out = jnp.where(sub == index, one, out)
        return out

    north, south = gather(odd_tile, 7), gather(even_tile, 0)
    mirrored = pltpu.roll(north, LANES - 6, 1)
    mirrored = jnp.where(lane % 2 == 0, pltpu.roll(mirrored, 1, 1), pltpu.roll(mirrored, LANES - 1, 1))
    mirrored = jnp.where((sub == 2) | (sub == 3), -mirrored, mirrored)
    near_out[...] = jnp.where(even, north, south)
    far_out[...] = jnp.where(fold, mirrored, jnp.where(even, south, north))


def step_kernel(
    t_ref, s_ref, u_ref, v_ref, ps_ref, wet_ref, col_near_ref, col_far_ref, row_near_ref, row_far_ref,
    t_out, s_out, u_out, v_out, p_out,
    x_ref, w_ref, psx_ref, p_ref, y_ref,
):
    lat = lax.axis_index("lat")
    lat_count = lax.axis_size("lat")
    even = lat % 2 == 0
    even_tile, odd_tile = halo_tiles(
        col_near_ref[...], col_far_ref[...], lax.axis_index("lon") % 2 == 0
    )
    fields = (t_ref, s_ref, u_ref, v_ref)
    own = pl.ds(FIRST, ROWS)
    inner, halo = pl.ds(0, LANES), pl.ds(LANES, LANES)

    def tile_of(index, j):
        tile = (odd_tile if j % 2 else even_tile)[index * COL_TILE : (index + 1) * COL_TILE]
        return pltpu.roll(tile, (-2 * (j + 1)) % LANES, 1)

    def copy_level(k, _):
        for index, ref in enumerate(fields):
            x_ref[index, k, own, inner] = ref[k]
        w_ref[k, own, inner] = wet_ref[k].astype(jnp.float32)
        return 0

    lax.fori_loop(0, LEVELS, copy_level, 0)
    psx_ref[own, inner] = ps_ref[...]
    for j in range(SLOTS):
        k, rows = j // BLOCKS, pl.ds(FIRST + 8 * (j % BLOCKS), 8)
        for index in range(4):
            x_ref[index, k, rows, halo] = tile_of(index, j)
        w_ref[k, rows, halo] = tile_of(COL_WET, j)
        if k == 0:
            psx_ref[rows, halo] = tile_of(COL_PS, j)

    near, far = row_near_ref[...], row_far_ref[...]
    south = jnp.where(even, far, near)
    south = jnp.where(lat == 0, 0.0, south)
    north = jnp.where(even, near, far)
    for value, first, away, block in ((south, FIRST - 1, -1, BLOCKS - 1), (north, FIRST + ROWS, 1, 0)):
        for k in range(LEVELS):
            shift = (-2 * (BLOCKS * k + block + 1)) % LANES
            for index in range(4):
                for ring in range(2):
                    at = (2 * index + ring) * LEVELS + k
                    x_ref[index, k, pl.ds(first + away * ring, 1), inner] = value[at : at + 1]
                corner = value[ROW_CORNER + index : ROW_CORNER + index + 1]
                x_ref[index, k, pl.ds(first, 1), halo] = pltpu.roll(corner, shift, 1)
            w_ref[k, pl.ds(first, 1), inner] = value[ROW_WET + k : ROW_WET + k + 1]
        for ring in range(2):
            psx_ref[pl.ds(first + away * ring, 1), inner] = value[ROW_PS + ring : ROW_PS + ring + 1]
        corner = value[ROW_CORNER + 4 : ROW_CORNER + 5]
        psx_ref[pl.ds(first, 1), halo] = pltpu.roll(corner, (-2 * (block + 1)) % LANES, 1)

    def pressure(src, lo, count, lanes, put):
        rows = pl.ds(lo, count)
        psv = psx_ref[rows, lanes]

        def level(k, running):
            heavy = -HEAT_EXPANSION * src[0, k, rows, lanes] + SALT_CONTRACTION * src[1, k, rows, lanes]
            put(k, psv + GRAVITY * (running + 0.5 * heavy))
            return running + heavy

        lax.fori_loop(0, LEVELS, level, jnp.zeros_like(psv))

    def put_p(k, value):
        p_ref[k, pl.ds(8, 48), :] = value

    def march(src, k, base, wide, put):
        lanes = pl.ds(0, EXT_LANES)

        def parts(ref, *lead):
            centre = ref[(*lead, k, pl.ds(base, 8), lanes)]
            east = pltpu.roll(centre, EXT_LANES - 1, 1)
            west = pltpu.roll(centre, 1, 1)
            if not wide:
                centre, east, west = (q[:, :LANES] for q in (centre, east, west))
            across = lanes if wide else inner
            return (
                centre,
                east,
                west,
                ref[(*lead, k, pl.ds(base + 1, 8), across)],
                ref[(*lead, k, pl.ds(base - 1, 8), across)],
            )

        def laplace(q):
            return q[1] + q[2] + q[3] + q[4] - 4.0 * q[0]

        row = base - FIRST + lax.broadcasted_iota(jnp.int32, (8, EXT_LANES if wide else LANES), 0)
        row = lat * ROWS + row
        row = jnp.minimum(row, lat_count * ROWS - 1).astype(jnp.float32)
        coriolis = ROTATION * (2.0 * (row + 0.5) / (lat_count * ROWS) - 1.0)
        wet = w_ref[k, pl.ds(base, 8), lanes if wide else inner]
        u, v = parts(src, 2), parts(src, 3)
        p = parts(p_ref)
        grad_x = 0.5 * (p[1] - p[2])
        grad_y = 0.5 * (p[3] - p[4])
        put(2, wet * (u[0] + TIME_STEP * (coriolis * v[0] - grad_x + VISCOSITY * laplace(u))))
        put(3, wet * (v[0] + TIME_STEP * (-coriolis * u[0] - grad_y + VISCOSITY * laplace(v))))
        for index in range(2):
            q = parts(src, index)
            transport = -0.5 * (u[0] * (q[1] - q[2]) + v[0] * (q[3] - q[4]))
            put(index, wet * (q[0] + TIME_STEP * (transport + DIFFUSIVITY * laplace(q))))

    everywhere = pl.ds(0, EXT_LANES)
    pressure(x_ref, 8, 48, everywhere, put_p)

    def first_step(k, _):
        for base in range(8, 56, 8):
            def put(index, value, base=base):
                y_ref[index, k, pl.ds(base, 8), :] = value

            march(x_ref, k, base, True, put)
        return 0

    lax.fori_loop(0, LEVELS, first_step, 0)
    pressure(y_ref, 8, 48, everywhere, put_p)
    outs = (t_out, s_out, u_out, v_out)

    def second_step(k, _):
        for block in range(BLOCKS):
            def put(index, value, block=block):
                outs[index][k, pl.ds(8 * block, 8), :] = value

            march(y_ref, k, FIRST + 8 * block, False, put)
        return 0

    lax.fori_loop(0, LEVELS, second_step, 0)
    psv = ps_ref[...]

    def last(k, running):
        heavy = -HEAT_EXPANSION * t_out[k] + SALT_CONTRACTION * s_out[k]
        p_out[k] = psv + GRAVITY * (running + 0.5 * heavy)
        return running + heavy

    lax.fori_loop(0, LEVELS, last, jnp.zeros_like(psv))


def exchanges(lon_count, lat_count):
    def at(lat, lon):
        return (lon % lon_count) * lat_count + lat

    def lat_far(lat, lon):
        if lat == 0:
            return at(0, lon ^ 1)
        if lat == lat_count - 1:
            return at(lat, lon_count - 1 - lon)
        return at(lat + 1 if lat % 2 else lat - 1, lon)

    cells = [(lat, lon) for lat in range(lat_count) for lon in range(lon_count)]
    lon_near = [(at(a, o), at(a, o ^ 1)) for a, o in cells]
    lon_far = [(at(a, o), at(a, o + 1 if o % 2 else o - 1)) for a, o in cells]
    lat_near = [(at(a, o), at(a ^ 1, o)) for a, o in cells]
    return lon_near, lon_far, lat_near, [(at(a, o), lat_far(a, o)) for a, o in cells]


def swap(value, pairs):
    return lax.ppermute(value, ("lon", "lat"), pairs)


def on_device(t, s, u, v, ps, wet):
    lon_near, lon_far, lat_near, lat_far = exchanges(lax.axis_size("lon"), lax.axis_size("lat"))
    inputs = (t, s, u, v, ps, wet)
    cols = jax.ShapeDtypeStruct((COL_ROWS, LANES), jnp.float32)
    rows = jax.ShapeDtypeStruct((ROW_ROWS, LANES), jnp.float32)
    corners = jax.ShapeDtypeStruct((8, LANES), jnp.float32)
    big = pltpu.CompilerParams(vmem_limit_bytes=48 * 1024 * 1024)
    col_near, col_far = pl.pallas_call(
        pack_columns, out_shape=(cols, cols), in_specs=[VMEM] * 6, out_specs=(VMEM, VMEM), compiler_params=big
    )(*inputs)
    row_near, row_far = pl.pallas_call(
        pack_rows, out_shape=(rows, rows), in_specs=[VMEM] * 6, out_specs=(VMEM, VMEM), compiler_params=big
    )(*inputs)
    col_far = swap(col_far, lon_far)
    col_near = swap(col_near, lon_near)
    corner_near, corner_far = pl.pallas_call(
        pack_corners, out_shape=(corners, corners), in_specs=[VMEM] * 2, out_specs=(VMEM, VMEM)
    )(col_near, col_far)
    row_near = lax.dynamic_update_slice(row_near, corner_near, (ROW_CORNER, 0))
    row_far = lax.dynamic_update_slice(row_far, corner_far, (ROW_CORNER, 0))
    row_far = swap(row_far, lat_far)
    row_near = swap(row_near, lat_near)
    out = jax.ShapeDtypeStruct(t.shape, jnp.float32)
    wide = (LEVELS, EXT_ROWS, EXT_LANES)
    return pl.pallas_call(
        step_kernel,
        out_shape=(out,) * 5,
        in_specs=[VMEM] * 10,
        out_specs=(VMEM,) * 5,
        scratch_shapes=[
            pltpu.VMEM((4, *wide), jnp.float32),
            pltpu.VMEM(wide, jnp.float32),
            pltpu.VMEM(wide[1:], jnp.float32),
            pltpu.VMEM(wide, jnp.float32),
            pltpu.VMEM((4, *wide), jnp.float32),
        ],
        compiler_params=big,
    )(*inputs, col_near, col_far, row_near, row_far)


def solution(mesh):
    field = P(None, "lat", "lon")
    return jax.shard_map(
        on_device,
        mesh=mesh,
        in_specs=(field, field, field, field, P("lat", "lon"), field),
        out_specs=(field,) * 5,
        check_vma=False,
    )
```

time: 145 us -> 39.4 us (0.27)
  the two profiles are of different devices: /device:TPU:1 before, /device:TPU:24 now
where the time goes in v1:
time: 39.4 us; the launch traced here: 38.8 us
  starting transfers between devices  12.7 us (32%)
  Pallas kernels  10.7 us (27%)
  local copies, waits for them, and re-layouts  8.97 us (23%)
  waiting for transfers between devices  5.77 us (15%)
  between operations  0.76 us (2%)
    ppermute x4, starting transfers between devices, swap(): return lax.ppermute(value, ('lon', 'lat'), pairs)  12.7 us
    pallas_call x1, Pallas kernels, on_device(): pl.pallas_call(step_kernel, out_shape=(out,) * 5, in_specs=[VMEM] * 10, o...  8.59 us
    unnamed x32, local copies, waits for them, and re-layouts  7.58 us
    ppermute x4, waiting for transfers between devices, swap(): return lax.ppermute(value, ('lon', 'lat'), pairs)  5.77 us
    pallas_call x1, Pallas kernels, on_device(): pl.pallas_call(pack_corners, out_shape=(corners, corners), in_specs=[VMEM...  1.5 us
  transfers between devices with their start and end apart: 4, of which 3 were waited for; matrix products, arithmetic and copies ran while one was open for 2% of the time, Pallas kernels for 0%

profile of v1, /device:TPU:24, one launch (start us, length us, event | category | flops | bytes accessed | tf_op | source)
XLA Modules:
  0.0 38.8 jit_solution(6232760387089518718)
XLA Ops:
  0.6 0.0 copy-start
  0.6 0.9 %copy-done = f32[16,32,128]{2,1,0:T(8,128)S(1)} copy-done((f32[16,32,128]{2,1,0:T(8,128)S(1)}, f32[16,32,128]{2,1,0:T(8,128)}, u32[]{:S(2)}) %copy-start) | copy-done | bytes 262168
  1.6 0.9 %copy-done.2 = f32[16,32,128]{2,1,0:T(8,128)S(1)} copy-done((f32[16,32,128]{2,1,0:T(8,128)S(1)}, f32[16,32,128]{2,1,0:T(8,128)}, u32[]{:S(2)}) %copy-start.2) | copy-done | bytes 262168
  2.5 0.9 %copy-done.4 = f32[16,32,128]{2,1,0:T(8,128)S(1)} copy-done((f32[16,32,128]{2,1,0:T(8,128)S(1)}, f32[16,32,128]{2,1,0:T(8,128)}, u32[]{:S(2)}) %copy-start.4) | copy-done | bytes 262168
  3.5 0.9 %copy-done.6 = f32[16,32,128]{2,1,0:T(8,128)S(1)} copy-done((f32[16,32,128]{2,1,0:T(8,128)S(1)}, f32[16,32,128]{2,1,0:T(8,128)}, u32[]{:S(2)}) %copy-start.6) | copy-done | bytes 262168
  4.4 0.9 %copy-done.8 = s32[16,32,128]{2,1,0:T(8,128)S(1)} copy-done((s32[16,32,128]{2,1,0:T(8,128)S(1)}, s32[16,32,128]{2,1,0:T(8,128)}, u32[]{:S(2)}) %copy-start.8) | copy-done | bytes 262168
  5.4 0.7 %copy-done.10 = f32[32,128]{1,0:T(8,128)S(1)} copy-done((f32[32,128]{1,0:T(8,128)S(1)}, f32[32,128]{1,0:T(8,128)}, u32[]{:S(2)}) %copy-start.10) | copy-done | bytes 16408
  6.1 0.4 %shard_map.101 = (f32[48,128]{1,0:T(8,128)S(1)}, f32[48,128]{1,0:T(8,128)S(1)}) custom-call(f32[16,32,128]{2,1,0:T(8,128)S(1)} %copy-done, f32[16,32,128]{2,1,0:T(8,128)S(1)} %copy-done.2, f32[16,32,128]{2,1,0:T(8,128)S(1)} %copy-done.4, f32[16,32,128]{2,1,0:T(8,128)S(1)} %copy-done.6, f32[32,128]{1,0:T(8,128)S(1)} %copy-done.10, s32[16,32,128]{2,1,0:T(8,128)S(1)} %copy-done.8), custom_call_target="tpu_custom_call" | custom-call | tf_op jit(solution)/shard_map/pallas_call | solution.py:306
  6.5 0.1 collective-permute-start
  6.6 0.0 copy-start.1
  6.6 0.0 copy-start.3
  6.7 7.0 %collective-permute-start.1 = (f32[48,128]{1,0:T(8,128)S(1)}, f32[48,128]{1,0:T(8,128)S(1)}, u32[]{:S(2)}, u32[]{:S(2)}) collective-permute-start(f32[48,128]{1,0:T(8,128)S(1)} %get-tuple-element.12), channel_id=1, source_target_pairs={{0,248},{8,16},{16,8},{24,32},{32,24},{40,48},{48,40},{56,64},{64,... | collective-permute-start | bytes 73736 | tf_op jit(solution)/shard_map/ppermute | solution.py:296
  13.6 0.2 shard_map.102
  13.8 1.3 %collective-permute-done.1.far_ref.col_far_ref = f32[48,128]{1,0:T(8,128)S(1)} collective-permute-done((f32[48,128]{1,0:T(8,128)S(1)}, f32[48,128]{1,0:T(8,128)S(1)}, u32[]{:S(2)}, u32[]{:S(2)}) %collective-permute-start.1) | collective-permute-done | bytes 24608 | tf_op jit(solution)/shard_map/ppermute | solution.py:296
  15.2 0.6 %copy-done.14 = f32[48,128]{1,0:T(8,128)} copy-done((f32[48,128]{1,0:T(8,128)}, f32[48,128]{1,0:T(8,128)S(1)}, u32[]{:S(2)}) %copy-start.14) | copy-done | bytes 24600
  15.8 1.5 %shard_map.103 = (f32[8,128]{1,0:T(8,128)}, f32[8,128]{1,0:T(8,128)}) custom-call(f32[48,128]{1,0:T(8,128)} %copy-done.12, f32[48,128]{1,0:T(8,128)} %copy-done.14), custom_call_target="tpu_custom_call" | custom-call | tf_op jit(solution)/shard_map/pallas_call | solution.py:314
  17.3 0.7 %constant_dynamic-update-slice_fusion = f32[160,128]{1,0:T(8,128)S(1)} fusion(f32[160,128]{1,0:T(8,128)S(1)} %get-tuple-element.15, f32[8,128]{1,0:T(8,128)} %get-tuple-element.16), kind=kLoop, calls=%fused_computation | loop fusion | bytes 8192 | tf_op jit(solution)/shard_map/dynamic_update_slice | solution.py:318
  18.0 5.6 %collective-permute-start.3 = (f32[160,128]{1,0:T(8,128)S(1)}, f32[160,128]{1,0:T(8,128)S(1)}, u32[]{:S(2)}, u32[]{:S(2)}) collective-permute-start(f32[160,128]{1,0:T(8,128)S(1)} %constant_dynamic-update-slice_fusion), channel_id=1, source_target_pairs={{0,8},{8,0},{16,24},{24,16},{32,40},{40,32},{48,56},{56,48},{64,72... | collective-permute-start | bytes 245768 | tf_op jit(solution)/shard_map/ppermute | solution.py:296
  23.6 0.7 %constant_dynamic-update-slice_fusion.1 = f32[160,128]{1,0:T(8,128)S(1)} fusion(f32[160,128]{1,0:T(8,128)S(1)} %get-tuple-element.13, f32[8,128]{1,0:T(8,128)} %get-tuple-element.14), kind=kLoop, calls=%fused_computation.1 | loop fusion | bytes 8192 | tf_op jit(solution)/shard_map/dynamic_update_slice | solution.py:317
  24.3 4.2 %collective-permute-done.3.row_far_ref = f32[160,128]{1,0:T(8,128)S(1)} collective-permute-done((f32[160,128]{1,0:T(8,128)S(1)}, f32[160,128]{1,0:T(8,128)S(1)}, u32[]{:S(2)}, u32[]{:S(2)}) %collective-permute-start.3) | collective-permute-done | bytes 81952 | tf_op jit(solution)/shard_map/ppermute | solution.py:296
  28.4 0.3 collective-permute-done.2.row_near_ref
  28.8 0.7 %copy-done.13 = f32[48,128]{1,0:T(8,128)S(1)} copy-done((f32[48,128]{1,0:T(8,128)S(1)}, f32[48,128]{1,0:T(8,128)}, u32[]{:S(2)}) %copy-start.13) | copy-done | bytes 24600
  29.5 0.7 %copy-done.15 = f32[48,128]{1,0:T(8,128)S(1)} copy-done((f32[48,128]{1,0:T(8,128)S(1)}, f32[48,128]{1,0:T(8,128)}, u32[]{:S(2)}) %copy-start.15) | copy-done | bytes 24600
  30.2 8.6 %shard_map.104 = (f32[16,32,128]{2,1,0:T(8,128)}, f32[16,32,128]{2,1,0:T(8,128)}, f32[16,32,128]{2,1,0:T(8,128)}, f32[16,32,128]{2,1,0:T(8,128)}, f32[16,32,128]{2,1,0:T(8,128)}) custom-call(f32[16,32,128]{2,1,0:T(8,128)S(1)} %copy-done.1, f32[16,32,128]{2,1,0:T(8,128)S(1)} %copy-done.3, f32[16,32,128]{2,1,0:T(8,128)S(1)} %copy-done.5, ...), custom_call_target="tpu_custom_call" | custom-call | tf_op jit(solution)/shard_map/pallas_call | solution.py:323
  (22 shorter events, 0.1 us)
Async XLA Ops:
  0.6 1.0 %copy-start = (f32[16,32,128]{2,1,0:T(8,128)S(1)}, f32[16,32,128]{2,1,0:T(8,128)}, u32[]{:S(2)}) copy-start(f32[16,32,128]{2,1,0:T(8,128)} %t_ref.5) | copy-start | bytes 786436
  1.6 0.9 %copy-start.2 = (f32[16,32,128]{2,1,0:T(8,128)S(1)}, f32[16,32,128]{2,1,0:T(8,128)}, u32[]{:S(2)}) copy-start(f32[16,32,128]{2,1,0:T(8,128)} %s_ref.5) | copy-start | bytes 786436
  2.5 0.9 %copy-start.4 = (f32[16,32,128]{2,1,0:T(8,128)S(1)}, f32[16,32,128]{2,1,0:T(8,128)}, u32[]{:S(2)}) copy-start(f32[16,32,128]{2,1,0:T(8,128)} %u_ref.5) | copy-start | bytes 786436
  3.5 0.9 %copy-start.6 = (f32[16,32,128]{2,1,0:T(8,128)S(1)}, f32[16,32,128]{2,1,0:T(8,128)}, u32[]{:S(2)}) copy-start(f32[16,32,128]{2,1,0:T(8,128)} %v_ref.5) | copy-start | bytes 786436
  4.4 0.9 %copy-start.8 = (s32[16,32,128]{2,1,0:T(8,128)S(1)}, s32[16,32,128]{2,1,0:T(8,128)}, u32[]{:S(2)}) copy-start(s32[16,32,128]{2,1,0:T(8,128)} %wet_ref.5) | copy-start | bytes 786436
  5.4 0.7 %copy-start.10 = (f32[32,128]{1,0:T(8,128)S(1)}, f32[32,128]{1,0:T(8,128)}, u32[]{:S(2)}) copy-start(f32[32,128]{1,0:T(8,128)} %ps_ref.5) | copy-start | bytes 49156
  6.5 7.3 %collective-permute-start = (f32[48,128]{1,0:T(8,128)S(1)}, f32[48,128]{1,0:T(8,128)S(1)}, u32[]{:S(2)}, u32[]{:S(2)}) collective-permute-start(f32[48,128]{1,0:T(8,128)S(1)} %get-tuple-element.11), channel_id=1, source_target_pairs={{0,8},{8,0},{16,24},{24,16},{32,40},{40,32},{48,56},{56,48},{64,72... | collective-permute-start | bytes 73736 | tf_op jit(solution)/shard_map/ppermute | solution.py:296
  6.6 22.1 %copy-start.1 = (f32[16,32,128]{2,1,0:T(8,128)S(1)}, f32[16,32,128]{2,1,0:T(8,128)}, u32[]{:S(2)}) copy-start(f32[16,32,128]{2,1,0:T(8,128)} %t_ref.5) | copy-start | bytes 786436
  6.6 22.1 %copy-start.3 = (f32[16,32,128]{2,1,0:T(8,128)S(1)}, f32[16,32,128]{2,1,0:T(8,128)}, u32[]{:S(2)}) copy-start(f32[16,32,128]{2,1,0:T(8,128)} %s_ref.5) | copy-start | bytes 786436
  6.6 22.1 %copy-start.5 = (f32[16,32,128]{2,1,0:T(8,128)S(1)}, f32[16,32,128]{2,1,0:T(8,128)}, u32[]{:S(2)}) copy-start(f32[16,32,128]{2,1,0:T(8,128)} %u_ref.5) | copy-start | bytes 786436
  6.6 22.1 %copy-start.7 = (f32[16,32,128]{2,1,0:T(8,128)S(1)}, f32[16,32,128]{2,1,0:T(8,128)}, u32[]{:S(2)}) copy-start(f32[16,32,128]{2,1,0:T(8,128)} %v_ref.5) | copy-start | bytes 786436
  6.7 22.1 %copy-start.9 = (s32[16,32,128]{2,1,0:T(8,128)S(1)}, s32[16,32,128]{2,1,0:T(8,128)}, u32[]{:S(2)}) copy-start(s32[16,32,128]{2,1,0:T(8,128)} %wet_ref.5) | copy-start | bytes 786436
  6.7 8.5 %collective-permute-start.1 = (f32[48,128]{1,0:T(8,128)S(1)}, f32[48,128]{1,0:T(8,128)S(1)}, u32[]{:S(2)}, u32[]{:S(2)}) collective-permute-start(f32[48,128]{1,0:T(8,128)S(1)} %get-tuple-element.12), channel_id=1, source_target_pairs={{0,248},{8,16},{16,8},{24,32},{32,24},{40,48},{48,40},{56,64},{64,... | collective-permute-start | bytes 73736 | tf_op jit(solution)/shard_map/ppermute | solution.py:296
  13.8 1.3 %copy-start.12 = (f32[48,128]{1,0:T(8,128)}, f32[48,128]{1,0:T(8,128)S(1)}, u32[]{:S(2)}) copy-start(f32[48,128]{1,0:T(8,128)S(1)} %collective-permute-done.near_ref.col_near_ref) | copy-start | bytes 73732
  15.2 0.6 %copy-start.14 = (f32[48,128]{1,0:T(8,128)}, f32[48,128]{1,0:T(8,128)S(1)}, u32[]{:S(2)}) copy-start(f32[48,128]{1,0:T(8,128)S(1)} %collective-permute-done.1.far_ref.col_far_ref) | copy-start | bytes 73732
  17.3 11.5 %copy-start.11 = (f32[32,128]{1,0:T(8,128)S(1)}, f32[32,128]{1,0:T(8,128)}, u32[]{:S(2)}) copy-start(f32[32,128]{1,0:T(8,128)} %ps_ref.5) | copy-start | bytes 49156
  18.0 10.5 %collective-permute-start.3 = (f32[160,128]{1,0:T(8,128)S(1)}, f32[160,128]{1,0:T(8,128)S(1)}, u32[]{:S(2)}, u32[]{:S(2)}) collective-permute-start(f32[160,128]{1,0:T(8,128)S(1)} %constant_dynamic-update-slice_fusion), channel_id=1, source_target_pairs={{0,8},{8,0},{16,24},{24,16},{32,40},{40,32},{48,56},{56,48},{64,72... | collective-permute-start | bytes 245768 | tf_op jit(solution)/shard_map/ppermute | solution.py:296
  24.3 4.4 %collective-permute-start.2 = (f32[160,128]{1,0:T(8,128)S(1)}, f32[160,128]{1,0:T(8,128)S(1)}, u32[]{:S(2)}, u32[]{:S(2)}) collective-permute-start(f32[160,128]{1,0:T(8,128)S(1)} %constant_dynamic-update-slice_fusion.1), channel_id=1, source_target_pairs={{0,1},{8,9},{16,17},{24,25},{32,33},{40,41},{48,49},{56,57},{64,65... | collective-permute-start | bytes 245768 | tf_op jit(solution)/shard_map/ppermute | solution.py:296
  28.8 0.7 %copy-start.13 = (f32[48,128]{1,0:T(8,128)S(1)}, f32[48,128]{1,0:T(8,128)}, u32[]{:S(2)}) copy-start(f32[48,128]{1,0:T(8,128)} %copy-done.12) | copy-start | bytes 73732
  29.5 0.7 %copy-start.15 = (f32[48,128]{1,0:T(8,128)S(1)}, f32[48,128]{1,0:T(8,128)}, u32[]{:S(2)}) copy-start(f32[48,128]{1,0:T(8,128)} %copy-done.14) | copy-start | bytes 73732

commit v2 on v1

v2 whole, which is shorter than its diff:
```python
import jax
import jax.numpy as jnp
from jax import lax
from jax.experimental import pallas as pl
from jax.experimental.pallas import tpu as pltpu
from jax.sharding import PartitionSpec as P

STEPS = 2
HEAT_EXPANSION = 0.2
SALT_CONTRACTION = 0.15
GRAVITY = 0.5
TIME_STEP = 0.2
VISCOSITY = 0.25
DIFFUSIVITY = 0.2
ROTATION = 1.0

LEVELS = 16
ROWS = 32
LANES = 128
BLOCKS = ROWS // 8
SLOTS = LEVELS * BLOCKS

COL_T, COL_S, COL_U, COL_V, COL_WET, COL_PS = range(6)
COL_TILE = 8
COL_ROWS = 6 * COL_TILE
ROW_WET = 4 * 2 * LEVELS
ROW_PS = ROW_WET + LEVELS
ROW_CORNER = ROW_PS + 8
ROW_ROWS = ROW_CORNER + 8

PARTS = 4

VMEM = pl.BlockSpec(memory_space=pltpu.VMEM)
HBM = pl.BlockSpec(memory_space=pltpu.HBM)


def lanes_of(shape):
    return lax.broadcasted_iota(jnp.int32, shape, len(shape) - 1)


def fetch(pairs, sems):
    copies = [pltpu.make_async_copy(src, dst, sems.at[i]) for i, (src, dst) in enumerate(pairs)]
    for copy in copies:
        copy.start()
    return copies


def pack_columns(
    t_hbm, s_hbm, u_hbm, v_hbm, ps_hbm, wet_hbm, near_ref, far_ref,
    t_ref, s_ref, u_ref, v_ref, ps_ref, wet_ref, sems,
):
    copies = fetch(
        (
            (t_hbm, t_ref), (s_hbm, s_ref), (u_hbm, u_ref), (v_hbm, v_ref),
            (wet_hbm, wet_ref), (ps_hbm, ps_ref),
        ),
        sems,
    )
    even = lax.axis_index("lon") % 2 == 0
    slot = lanes_of((8, LANES)) >> 1
    masks = [slot == j for j in range(SLOTS)]

    def pack(index, tiles):
        east = jnp.zeros((8, LANES), jnp.float32)
        west = jnp.zeros((8, LANES), jnp.float32)
        for j, tile in enumerate(tiles):
            rolled = pltpu.roll(tile(), (2 * j + 2) % LANES, 1)
            east = jnp.where(masks[j], rolled, east)
            west = jnp.where(masks[(j + 1) % SLOTS], rolled, west)
        rows = pl.ds(index * COL_TILE, COL_TILE)
        near_ref[rows, :] = jnp.where(even, east, west)
        far_ref[rows, :] = jnp.where(even, west, east)

    def tiles_of(ref):
        return [
            (lambda j=j: ref[j // BLOCKS, pl.ds(8 * (j % BLOCKS), 8), :].astype(jnp.float32))
            for j in range(SLOTS)
        ]

    for index, ref in ((COL_T, t_ref), (COL_S, s_ref), (COL_U, u_ref), (COL_V, v_ref), (COL_WET, wet_ref)):
        copies[index].wait()
        pack(index, tiles_of(ref))
    copies[COL_PS].wait()
    pack(COL_PS, [(lambda r=r: ps_ref[pl.ds(8 * r, 8), :]) for r in range(BLOCKS)])


def reverse_lanes(value):
    index = LANES - 1 - lanes_of(value.shape)
    return jnp.take_along_axis(value, index, axis=1, mode="promise_in_bounds")


def pack_rows(
    t_hbm, s_hbm, u_hbm, v_hbm, ps_hbm, wet_hbm, near_ref, far_ref, x_ref, wet_ref, ps_ref, sems
):
    pairs = [(ps_hbm, ps_ref)]
    for side, first in ((0, 0), (1, ROWS - 8)):
        for index, src in enumerate((t_hbm, s_hbm, u_hbm, v_hbm)):
            pairs.append((src.at[:, pl.ds(first, 8), :], x_ref.at[side, index]))
        pairs.append((wet_hbm.at[:, pl.ds(first, 8), :], wet_ref.at[side]))
    copies = fetch(pairs, sems)
    lat = lax.axis_index("lat")
    even = lat % 2 == 0
    fold = lat == lax.axis_size("lat") - 1
    for copy in copies:
        copy.wait()

    def put(first, north, south, sign):
        rows = pl.ds(first, north.shape[0])
        near_ref[rows, :] = jnp.where(even, north, south)
        far_ref[rows, :] = jnp.where(even, south, north)

        @pl.when(fold)
        def _():
            far_ref[rows, :] = sign * reverse_lanes(north)

    for index, sign in enumerate((1.0, 1.0, -1.0, -1.0)):
        for ring in range(2):
            put((2 * index + ring) * LEVELS, x_ref[1, index, :, 7 - ring, :], x_ref[0, index, :, ring, :], sign)
    put(ROW_WET, wet_ref[1, :, 7, :].astype(jnp.float32), wet_ref[0, :, 0, :].astype(jnp.float32), 1.0)
    top, bottom = ps_ref[pl.ds(ROWS - 8, 8), :], ps_ref[pl.ds(0, 8), :]
    sub = lax.broadcasted_iota(jnp.int32, (8, LANES), 0)
    north = jnp.where(sub == 0, pltpu.roll(top, 1, 0), pltpu.roll(top, 3, 0))
    put(ROW_PS, north, bottom, 1.0)
    near_ref[pl.ds(ROW_CORNER, 8), :] = jnp.zeros((8, LANES), jnp.float32)
    far_ref[pl.ds(ROW_CORNER, 8), :] = jnp.zeros((8, LANES), jnp.float32)


def halo_tiles(near, far, even_lon):
    slot = lanes_of(near.shape) >> 1
    west = jnp.where(even_lon, far, near)
    east = jnp.where(even_lon, near, far)
    return (
        jnp.where(slot % 2 == 0, west, east),
        jnp.where(slot % 2 == 0, east, west),
    )


def pack_corners(far_ref, near_ref, far_in, near_in, far_out, near_out):
    lat = lax.axis_index("lat")
    even = lat % 2 == 0
    fold = lat == lax.axis_size("lat") - 1
    even_tile, odd_tile = halo_tiles(near_ref[...], far_ref[...], lax.axis_index("lon") % 2 == 0)
    lane = lanes_of((8, LANES))
    sub = lax.broadcasted_iota(jnp.int32, (8, LANES), 0)

    def gather(tile, row):
        out = jnp.zeros((8, LANES), jnp.float32)
        for index, field in enumerate((COL_T, COL_S, COL_U, COL_V, COL_PS)):
            one = pltpu.roll(tile[field * COL_TILE : (field + 1) * COL_TILE], (index - row) % 8, 0)
            out = jnp.where(sub == index, one, out)
        return out

    north, south = gather(odd_tile, 7), gather(even_tile, 0)
    mirrored = pltpu.roll(north, LANES - 6, 1)
    mirrored = jnp.where(lane % 2 == 0, pltpu.roll(mirrored, 1, 1), pltpu.roll(mirrored, LANES - 1, 1))
    mirrored = jnp.where((sub == 2) | (sub == 3), -mirrored, mirrored)
    rows = pl.ds(ROW_CORNER, 8)
    near_out[rows, :] = jnp.where(even, north, south)
    far_out[rows, :] = jnp.where(fold, mirrored, jnp.where(even, south, north))


def laplace(q):
    centre, east, west, north, south = q
    return east + west + north + south - 4.0 * centre


def march(t, s, u, v, p, wet, coriolis):
    grad_x = 0.5 * (p[1] - p[2])
    grad_y = 0.5 * (p[3] - p[4])

    def tracer(q):
        transport = -0.5 * (u[0] * (q[1] - q[2]) + v[0] * (q[3] - q[4]))
        return wet * (q[0] + TIME_STEP * (transport + DIFFUSIVITY * laplace(q)))

    return (
        tracer(t),
        tracer(s),
        wet * (u[0] + TIME_STEP * (coriolis * v[0] - grad_x + VISCOSITY * laplace(u))),
        wet * (v[0] + TIME_STEP * (-coriolis * u[0] - grad_y + VISCOSITY * laplace(v))),
    )


def heaviness(t, s):
    return -HEAT_EXPANSION * t + SALT_CONTRACTION * s


def coriolis_of(row):
    total = ROWS * lax.axis_size("lat")
    row = jnp.minimum(lax.axis_index("lat") * ROWS + row, total - 1).astype(jnp.float32)
    return ROTATION * (2.0 * (row + 0.5) / total - 1.0)


def east_of(own, halo, lane):
    return pltpu.roll(jnp.where(lane == 0, halo, own), LANES - 1, 1)


def west_of(own, halo, lane):
    return pltpu.roll(jnp.where(lane == LANES - 1, halo, own), 1, 1)


def packed_pressure(t, s, ps, order):
    heavy = heaviness(t, s)
    total = heavy
    for shift in (8, 16, 32, 64):
        total = total + jnp.where(order >= shift, pltpu.roll(total, shift, 1), 0.0)
        ps = ps + pltpu.roll(ps, shift, 1)
    return ps + GRAVITY * (total - 0.5 * heavy)


def main_kernel(
    t_ref, s_ref, u_ref, v_ref, ps_ref, wet_ref, near_ref, far_ref, own_near_ref, own_far_ref,
    t_hbm, s_hbm, u_hbm, v_hbm, p_hbm, raw_ref, rawh_ref, one_ref, oneh_ref, psh_ref,
    p_ref, y_ref, q_ref, out_ref, sems,
):
    even = lax.axis_index("lon") % 2 == 0
    near, far = near_ref[...], far_ref[...]
    own_near, own_far = own_near_ref[...], own_far_ref[...]
    own_east, own_west = jnp.where(even, own_near, own_far), jnp.where(even, own_far, own_near)
    got_west, got_east = jnp.where(even, far, near), jnp.where(even, near, far)
    odd = lanes_of(near.shape) % 2 == 1
    even_tile, odd_tile = halo_tiles(near, far, even)

    z = jnp.where(odd, got_west, got_east)
    z_east = pltpu.roll(jnp.where(odd, got_east, own_west), LANES - 1, 1)
    z_west = pltpu.roll(jnp.where(odd, own_east, got_west), 1, 1)
    lane = lanes_of((8, LANES))
    sub = lax.broadcasted_iota(jnp.int32, (8, LANES), 0)
    order = (lane + LANES - 1) % LANES

    def tile(value, index):
        return value[index * COL_TILE : (index + 1) * COL_TILE]

    def above(q):
        return jnp.where(sub == 7, pltpu.roll(pltpu.roll(q, LANES - 2, 1), 7, 0), pltpu.roll(q, 7, 0))

    def below(q):
        return jnp.where(sub == 0, pltpu.roll(pltpu.roll(q, 2, 1), 1, 0), pltpu.roll(q, 1, 0))

    zp, zp_east, zp_west = (
        packed_pressure(tile(q, COL_T), tile(q, COL_S), tile(q, COL_PS), order) for q in (z, z_east, z_west)
    )

    def around(index):
        q = tile(z, index)
        return q, tile(z_east, index), tile(z_west, index), above(q), below(q)

    z_one = march(
        around(COL_T), around(COL_S), around(COL_U), around(COL_V),
        (zp, zp_east, zp_west, above(zp), below(zp)),
        tile(z, COL_WET),
        coriolis_of(8 * ((order // 2) % BLOCKS) + sub),
    )
    zp_one = packed_pressure(z_one[0], z_one[1], tile(z, COL_PS), order)

    for side, block, tiles in ((0, 0, even_tile), (1, BLOCKS - 1, odd_tile)):
        psh_ref[side] = pltpu.roll(tile(tiles, COL_PS), LANES - 2 * (block + 1), 1)

    fields = (t_ref, s_ref, u_ref, v_ref)
    outs = (t_hbm, s_hbm, u_hbm, v_hbm, p_hbm)
    blocks = [pl.ds(8 * r, 8) for r in range(BLOCKS)]
    coriolis = [coriolis_of(8 * r + sub) for r in range(BLOCKS)]
    psv = [ps_ref[rows, :] for rows in blocks]

    def vertical(ref, lead, r, centre):
        north = ref[(*lead, pl.ds(8 * r + 1, 8))] if r < BLOCKS - 1 else pltpu.roll(centre, 7, 0)
        south = ref[(*lead, pl.ds(8 * r - 1, 8))] if r > 0 else pltpu.roll(centre, 1, 0)
        return north, south

    def level(k, running):
        run0, run1, run2 = (list(x) for x in running)
        side_of = {0: 0, BLOCKS - 1: 1}
        shifts = [LANES - 2 - 8 * k - 2 * r for r in range(BLOCKS)]
        for r, rows in enumerate(blocks):
            heavy = heaviness(t_ref[k, rows, :], s_ref[k, rows, :])
            p_ref[rows, :] = psv[r] + GRAVITY * (run0[r] + 0.5 * heavy)
            run0[r] = run0[r] + heavy
        for r, rows in enumerate(blocks):
            tiles = odd_tile if r % 2 else even_tile
            side = side_of.get(r)

            def parts(index, ref):
                own = ref[k, rows, :]
                halo = pltpu.roll(tile(tiles, index), shifts[r], 1)
                if side is not None:
                    raw_ref[side, index, k] = own
                    rawh_ref[side, index, k] = halo
                return (own, east_of(own, halo, lane), west_of(own, halo, lane), *vertical(ref, (k,), r, own))

            own = p_ref[rows, :]
            halo = pltpu.roll(zp, shifts[r], 1)
            p = (own, east_of(own, halo, lane), west_of(own, halo, lane), *vertical(p_ref, (), r, own))
            wet = wet_ref[k, rows, :].astype(jnp.float32)
            if side is not None:
                raw_ref[side, 4, k] = wet
                rawh_ref[side, 4, k] = pltpu.roll(tile(tiles, COL_WET), shifts[r], 1)
            new = march(*(parts(i, ref) for i, ref in enumerate(fields)), p, wet, coriolis[r])
            for index in range(4):
                y_ref[index, rows, :] = new[index]
            heavy = heaviness(new[0], new[1])
            q_ref[rows, :] = psv[r] + GRAVITY * (run1[r] + 0.5 * heavy)
            run1[r] = run1[r] + heavy
        for r, rows in enumerate(blocks):
            side = side_of.get(r)

            def parts(index):
                own = y_ref[index, rows, :]
                halo = pltpu.roll(z_one[index], shifts[r], 1)
                if side is not None:
                    one_ref[side, index, k] = own
                    oneh_ref[side, index, k] = halo
                return (own, east_of(own, halo, lane), west_of(own, halo, lane), *vertical(y_ref, (index,), r, own))

            own = q_ref[rows, :]
            halo = pltpu.roll(zp_one, shifts[r], 1)
            p = (own, east_of(own, halo, lane), west_of(own, halo, lane), *vertical(q_ref, (), r, own))
            wet = wet_ref[k, rows, :].astype(jnp.float32)
            new = march(*(parts(i) for i in range(4)), p, wet, coriolis[r])
            for index in range(4):
                out_ref[index, k, rows, :] = new[index]
            heavy = heaviness(new[0], new[1])
            out_ref[4, k, rows, :] = psv[r] + GRAVITY * (run2[r] + 0.5 * heavy)
            run2[r] = run2[r] + heavy
        return tuple(tuple(x) for x in (run0, run1, run2))

    zero = tuple(jnp.zeros((8, LANES), jnp.float32) for _ in range(BLOCKS))
    running = (zero, zero, zero)
    copies = []
    for part in range(PARTS):
        levels = pl.ds(part * LEVELS // PARTS, LEVELS // PARTS)
        running = lax.fori_loop(part * LEVELS // PARTS, (part + 1) * LEVELS // PARTS, level, running)
        for index, out in enumerate(outs):
            copy = pltpu.make_async_copy(out_ref.at[index, levels], out.at[levels], sems.at[part, index])
            copy.start()
            copies.append(copy)
    for copy in copies:
        copy.wait()


def patch_kernel(
    ps_ref, far_ref, near_ref, raw_ref, rawh_ref, one_ref, oneh_ref, psh_ref, t_in, s_in, u_in, v_in, p_in,
    t_hbm, s_hbm, u_hbm, v_hbm, p_hbm, block_ref, in_sems, out_sems,
):
    outs = (t_hbm, s_hbm, u_hbm, v_hbm, p_hbm)
    firsts = (0, ROWS - 8)
    loads = [
        [
            pltpu.make_async_copy(out.at[:, pl.ds(first, 8), :], block_ref.at[side, index], in_sems.at[side, index])
            for index, out in enumerate(outs)
        ]
        for side, first in enumerate(firsts)
    ]
    stores = [
        [
            pltpu.make_async_copy(block_ref.at[side, index], out.at[:, pl.ds(first, 8), :], out_sems.at[side, index])
            for index, out in enumerate(outs)
        ]
        for side, first in enumerate(firsts)
    ]
    for copy in loads[0] + loads[1]:
        copy.start()
    lat = lax.axis_index("lat")
    even = lat % 2 == 0
    lane = lanes_of((LEVELS, LANES))
    depth = lax.broadcasted_iota(jnp.int32, (LEVELS, LANES), 0)
    near, far = near_ref[...], far_ref[...]
    south = jnp.where(lat == 0, 0.0, jnp.where(even, far, near))
    north = jnp.where(even, near, far)

    def pressure(t, s, ps):
        heavy = heaviness(t, s)
        total = heavy
        for shift in (1, 2, 4, 8):
            total = total + jnp.where(depth >= shift, pltpu.roll(total, shift, 0), 0.0)
        return ps + GRAVITY * (total - 0.5 * heavy)

    def side_rows(side, value):
        rows = (0, 1, 2) if side == 0 else (7, 6, 5)
        at = [firsts[side] + r for r in rows]
        block = BLOCKS - 1 if side == 0 else 0

        def unfold(row):
            row = jnp.broadcast_to(pltpu.roll(row, LANES - 2 * (block + 1), 1), (LEVELS, LANES))
            for bit in (1, 2, 4, 8):
                row = jnp.where(depth & bit != 0, pltpu.roll(row, LANES - 8 * bit, 1), row)
            return row

        def five(own, halo, out, inn):
            ns = (inn, out) if side == 0 else (out, inn)
            return (own, east_of(own, halo, lane), west_of(own, halo, lane), *ns)

        def five_halo(own, halo, out, inn):
            ns = (inn, out) if side == 0 else (out, inn)
            return (halo, east_of(halo, own, lane), west_of(halo, own, lane), *ns)

        ring2 = [value[(2 * i + 1) * LEVELS : (2 * i + 2) * LEVELS] for i in range(4)]
        ring1 = [value[2 * i * LEVELS : (2 * i + 1) * LEVELS] for i in range(4)]
        corner = [unfold(value[ROW_CORNER + i : ROW_CORNER + i + 1]) for i in range(5)]
        edge0 = [raw_ref[side, i, :, rows[0], :] for i in range(5)]
        edge0h = [rawh_ref[side, i, :, rows[0], :] for i in range(5)]
        edge1 = [raw_ref[side, i, :, rows[1], :] for i in range(5)]
        edge1h = [rawh_ref[side, i, :, rows[1], :] for i in range(4)]
        one1 = [one_ref[side, i, :, rows[1], :] for i in range(4)]
        one1h = [oneh_ref[side, i, :, rows[1], :] for i in range(4)]
        one2 = [one_ref[side, i, :, rows[2], :] for i in range(4)]
        wet_ring = value[ROW_WET : ROW_WET + LEVELS]
        ps_ring2, ps_ring1 = value[ROW_PS + 1 : ROW_PS + 2], value[ROW_PS : ROW_PS + 1]
        ps_corner = corner[4][0:1]
        ps0, ps1, ps2 = (ps_ref[pl.ds(a, 1), :] for a in at)
        ps0h, ps1h = (psh_ref[side, pl.ds(r, 1), :] for r in rows[:2])
        step = -1 if side == 0 else 1
        cor_ring, cor0, cor1 = (coriolis_of(jnp.int32(at[0] + d)) for d in (step, 0, -step))

        p_ring2 = pressure(ring2[0], ring2[1], ps_ring2)
        p_ring1 = pressure(ring1[0], ring1[1], ps_ring1)
        p_corner = pressure(corner[0], corner[1], ps_corner)
        p0 = pressure(edge0[0], edge0[1], ps0)
        p0h = pressure(edge0h[0], edge0h[1], ps0h)
        p1 = pressure(edge1[0], edge1[1], ps1)
        p1h = pressure(edge1h[0], edge1h[1], ps1h)
        first_ring = march(
            *(five(ring1[i], corner[i], ring2[i], edge0[i]) for i in range(4)),
            five(p_ring1, p_corner, p_ring2, p0), wet_ring, cor_ring,
        )
        first0 = march(
            *(five(edge0[i], edge0h[i], ring1[i], edge1[i]) for i in range(4)),
            five(p0, p0h, p_ring1, p1), edge0[4], cor0,
        )
        first0h = march(
            *(five_halo(edge0[i], edge0h[i], corner[i], edge1h[i]) for i in range(4)),
            five_halo(p0, p0h, p_corner, p1h), edge0h[4], cor0,
        )
        p_ring1 = pressure(first_ring[0], first_ring[1], ps_ring1)
        p0 = pressure(first0[0], first0[1], ps0)
        p0h = pressure(first0h[0], first0h[1], ps0h)
        p1 = pressure(one1[0], one1[1], ps1)
        p1h = pressure(one1h[0], one1h[1], ps1h)
        p2 = pressure(one2[0], one2[1], ps2)
        second0 = march(
            *(five(first0[i], first0h[i], first_ring[i], one1[i]) for i in range(4)),
            five(p0, p0h, p_ring1, p1), edge0[4], cor0,
        )
        second1 = march(
            *(five(one1[i], one1h[i], first0[i], one2[i]) for i in range(4)),
            five(p1, p1h, p0, p2), edge1[4], cor1,
        )
        second0 = (*second0, pressure(second0[0], second0[1], ps0))
        second1 = (*second1, pressure(second1[0], second1[1], ps1))
        for index in range(5):
            loads[side][index].wait()
            block_ref[side, index, :, rows[0], :] = second0[index]
            block_ref[side, index, :, rows[1], :] = second1[index]
            stores[side][index].start()

    side_rows(0, south)
    side_rows(1, north)
    for copy in stores[0] + stores[1]:
        copy.wait()


def exchanges(lon_count, lat_count):
    def at(lat, lon):
        return (lon % lon_count) * lat_count + lat

    def lat_far(lat, lon):
        if lat == 0:
            return at(0, lon ^ 1)
        if lat == lat_count - 1:
            return at(lat, lon_count - 1 - lon)
        return at(lat + 1 if lat % 2 else lat - 1, lon)

    cells = [(lat, lon) for lat in range(lat_count) for lon in range(lon_count)]
    lon_near = [(at(a, o), at(a, o ^ 1)) for a, o in cells]
    lon_far = [(at(a, o), at(a, o + 1 if o % 2 else o - 1)) for a, o in cells]
    lat_near = [(at(a, o), at(a ^ 1, o)) for a, o in cells]
    return lon_near, lon_far, lat_near, [(at(a, o), lat_far(a, o)) for a, o in cells]


def swap(value, pairs):
    return lax.ppermute(value, ("lon", "lat"), pairs)


def on_device(t, s, u, v, ps, wet):
    lon_near, lon_far, lat_near, lat_far = exchanges(lax.axis_size("lon"), lax.axis_size("lat"))
    inputs = (t, s, u, v, ps, wet)
    kept = [pltpu.with_memory_space_constraint(x, pltpu.HBM) for x in inputs]
    cols = jax.ShapeDtypeStruct((COL_ROWS, LANES), jnp.float32)
    rows = jax.ShapeDtypeStruct((ROW_ROWS, LANES), jnp.float32)

    def grant(mib):
        return pltpu.CompilerParams(vmem_limit_bytes=int(mib * 1024 * 1024))

    col_near, col_far = pl.pallas_call(
        pack_columns,
        out_shape=(cols, cols),
        in_specs=[HBM] * 6,
        out_specs=(VMEM, VMEM),
        scratch_shapes=[pltpu.VMEM(x.shape, x.dtype) for x in inputs] + [pltpu.SemaphoreType.DMA((6,))],
        compiler_params=grant(6),
    )(*kept)
    block = (LEVELS, 8, LANES)
    row_near, row_far = pl.pallas_call(
        pack_rows,
        out_shape=(rows, rows),
        in_specs=[HBM] * 6,
        out_specs=(VMEM, VMEM),
        scratch_shapes=[
            pltpu.VMEM((2, 4, *block), jnp.float32),
            pltpu.VMEM((2, *block), jnp.int32),
            pltpu.VMEM((ROWS, LANES), jnp.float32),
            pltpu.SemaphoreType.DMA((11,)),
        ],
        compiler_params=grant(4),
    )(*kept)
    got_far = swap(col_far, lon_far)
    got_near = swap(col_near, lon_near)
    row_far, row_near = pl.pallas_call(
        pack_corners,
        out_shape=(rows, rows),
        in_specs=[VMEM] * 4,
        out_specs=(VMEM, VMEM),
        input_output_aliases={2: 0, 3: 1},
        compiler_params=grant(2),
    )(got_far, got_near, row_far, row_near)
    row_far = swap(row_far, lat_far)
    row_near = swap(row_near, lat_near)
    out = jax.ShapeDtypeStruct(t.shape, jnp.float32)

    def blocks(count):
        return jax.ShapeDtypeStruct((2, count, *block), jnp.float32)

    plane = pltpu.VMEM((ROWS, LANES), jnp.float32)
    *outs, raw, raw_halo, one, one_halo, ps_halo = pl.pallas_call(
        main_kernel,
        out_shape=(out,) * 5 + (blocks(5), blocks(5), blocks(4), blocks(4), jax.ShapeDtypeStruct((2, 8, LANES), jnp.float32)),
        in_specs=[VMEM] * 10,
        out_specs=(HBM,) * 5 + (VMEM,) * 5,
        scratch_shapes=[
            plane,
            pltpu.VMEM((4, ROWS, LANES), jnp.float32),
            plane,
            pltpu.VMEM((5, *t.shape), jnp.float32),
            pltpu.SemaphoreType.DMA((PARTS, 5)),
        ],
        compiler_params=grant(12),
    )(*inputs, got_near, got_far, col_near, col_far)
    return pl.pallas_call(
        patch_kernel,
        out_shape=(out,) * 5,
        in_specs=[VMEM] * 8 + [HBM] * 5,
        out_specs=(HBM,) * 5,
        scratch_shapes=[
            pltpu.VMEM((2, 5, *block), jnp.float32),
            pltpu.SemaphoreType.DMA((2, 5)),
            pltpu.SemaphoreType.DMA((2, 5)),
        ],
        input_output_aliases={8 + i: i for i in range(5)},
        compiler_params=grant(8),
    )(ps, row_far, row_near, raw, raw_halo, one, one_halo, ps_halo, *outs)


def solution(mesh):
    field = P(None, "lat", "lon")
    return jax.shard_map(
        on_device,
        mesh=mesh,
        in_specs=(field, field, field, field, P("lat", "lon"), field),
        out_specs=(field,) * 5,
        check_vma=False,
    )
```

time: 39.4 us -> 27.3 us (0.69)
  the two profiles are of different devices: /device:TPU:24 before, /device:TPU:16 now
where the time goes in v2:
time: 27.3 us; the launch traced here: 27.1 us
  starting transfers between devices  13.8 us (51%)
  Pallas kernels  12.5 us (46%)
  between operations  0.74 us (3%)
    ppermute x4, starting transfers between devices, swap(): return lax.ppermute(value, ('lon', 'lat'), pairs)  13.8 us
    pallas_call x1, Pallas kernels, on_device(): pl.pallas_call(main_kernel, out_shape=(out,) * 5 + (blocks(5), blocks(5),...  6.08 us
    pallas_call x1, Pallas kernels, on_device(): pl.pallas_call(patch_kernel, out_shape=(out,) * 5, in_specs=[VMEM] * 8 +...  3.04 us
    pallas_call x1, Pallas kernels, on_device(): pl.pallas_call(pack_columns, out_shape=(cols, cols), in_specs=[HBM] * 6,...  1.76 us
    pallas_call x1, Pallas kernels, on_device(): pl.pallas_call(pack_rows, out_shape=(rows, rows), in_specs=[HBM] * 6, out...  1.49 us
  transfers between devices with their start and end apart: 4, of which 0 were waited for; matrix products, arithmetic and copies ran while one was open for 0% of the time, Pallas kernels for 28%

profile of v2, /device:TPU:16, one launch (start us, length us, event | category | flops | bytes accessed | tf_op | source)
XLA Modules:
  0.0 27.1 jit_solution(6370320725816384081)
XLA Ops:
  0.6 1.8 %shard_map.101 = (f32[48,128]{1,0:T(8,128)S(1)}, f32[48,128]{1,0:T(8,128)S(1)}) custom-call(f32[16,32,128]{2,1,0:T(8,128)} %t_ref.1, f32[16,32,128]{2,1,0:T(8,128)} %s_ref.1, f32[16,32,128]{2,1,0:T(8,128)} %u_ref.1, f32[16,32,128]{2,1,0:T(8,128)} %v_ref.1, f32[32,128]{1,0:T(8,128)} %ps_ref.3, s32[16,32,128]{2,1,0:T(8,128)} %wet_ref.1), custom_call_target="tpu_custom_call" | custom-call | tf_op jit(solution)/shard_map/pallas_call | solution.py:492
  2.4 6.3 %collective-permute-start = (f32[48,128]{1,0:T(8,128)S(1)}, f32[48,128]{1,0:T(8,128)S(1)}, u32[]{:S(2)}, u32[]{:S(2)}) collective-permute-start(f32[48,128]{1,0:T(8,128)S(1)} %get-tuple-element.21.own_far_ref), channel_id=1, source_target_pairs={{0,248},{8,16},{16,8},{24,32},{32,24},{40,48},{48,40},{56,64},{64,... | collective-permute-start | bytes 73736 | tf_op jit(solution)/shard_map/ppermute | solution.py:479
  8.7 0.0 collective-permute-start.1
  8.8 0.0 copy-start
  8.8 0.0 copy-start.1
  8.8 0.0 copy-start.3
  8.8 0.0 copy-start.4
  8.8 1.5 %shard_map.102 = (f32[160,128]{1,0:T(8,128)S(1)}, f32[160,128]{1,0:T(8,128)S(1)}) custom-call(f32[16,32,128]{2,1,0:T(8,128)} %t_ref.1, f32[16,32,128]{2,1,0:T(8,128)} %s_ref.1, f32[16,32,128]{2,1,0:T(8,128)} %u_ref.1, f32[16,32,128]{2,1,0:T(8,128)} %v_ref.1, f32[32,128]{1,0:T(8,128)} %ps_ref.3, s32[16,32,128]{2,1,0:T(8,128)} %wet_ref.1), custom_call_target="tpu_custom_call" | custom-call | tf_op jit(solution)/shard_map/pallas_call | solution.py:501
  10.3 0.0 collective-permute-done.far_ref
  10.3 0.0 collective-permute-done.1.near_ref
  10.3 0.0 copy-start.5
  10.3 0.2 shard_map.103
  10.5 0.4 %collective-permute-start.2 = (f32[160,128]{1,0:T(8,128)S(1)}, f32[160,128]{1,0:T(8,128)S(1)}, u32[]{:S(2)}, u32[]{:S(2)}) collective-permute-start(f32[160,128]{1,0:T(8,128)S(1)} %get-tuple-element.25), channel_id=1, source_target_pairs={{0,8},{8,0},{16,24},{24,16},{32,40},{40,32},{48,56},{56,48},{64,72... | collective-permute-start | bytes 245768 | tf_op jit(solution)/shard_map/ppermute | solution.py:479
  10.9 7.0 %collective-permute-start.3 = (f32[160,128]{1,0:T(8,128)S(1)}, f32[160,128]{1,0:T(8,128)S(1)}, u32[]{:S(2)}, u32[]{:S(2)}) collective-permute-start(f32[160,128]{1,0:T(8,128)S(1)} %get-tuple-element.26), channel_id=1, source_target_pairs={{0,1},{8,9},{16,17},{24,25},{32,33},{40,41},{48,49},{56,57},{64,65... | collective-permute-start | bytes 245768 | tf_op jit(solution)/shard_map/ppermute | solution.py:479
  17.9 0.0 copy-done
  17.9 0.0 copy-done.1
  18.0 0.0 copy-done.2
  18.0 0.0 copy-done.3
  18.0 0.0 copy-done.4
  18.0 0.0 copy-done.5
  18.0 6.1 %shard_map.104 = (f32[16,32,128]{2,1,0:T(8,128)}, f32[16,32,128]{2,1,0:T(8,128)}, f32[16,32,128]{2,1,0:T(8,128)}, f32[16,32,128]{2,1,0:T(8,128)}, f32[16,32,128]...) custom-call(f32[16,32,128]{2,1,0:T(8,128)S(1)} %copy-done, ...), custom_call_target="tpu_custom_call" | custom-call | tf_op jit(solution)/shard_map/pallas_call | solution.py:532
  24.1 0.0 collective-permute-done.2.far_ref
  24.1 0.0 collective-permute-done.3.near_ref
  24.1 3.0 %shard_map.105 = (f32[16,32,128]{2,1,0:T(8,128)}, f32[16,32,128]{2,1,0:T(8,128)}, f32[16,32,128]{2,1,0:T(8,128)}, f32[16,32,128]{2,1,0:T(8,128)}, f32[16,32,128]{2,1,0:T(8,128)}) custom-call(f32[32,128]{1,0:T(8,128)S(1)} %copy-done.5, ...), custom_call_target="tpu_custom_call", output_to_operand_aliasing={{0}: (8, {}), {1}: (9, {}), {2}: (10, {}), {3}: (11, {}), {... | custom-call | tf_op jit(solution)/shard_map/pallas_call | solution.py:546
  (1 shorter events, 0.0 us)
Async XLA Ops:
  2.4 7.9 %collective-permute-start = (f32[48,128]{1,0:T(8,128)S(1)}, f32[48,128]{1,0:T(8,128)S(1)}, u32[]{:S(2)}, u32[]{:S(2)}) collective-permute-start(f32[48,128]{1,0:T(8,128)S(1)} %get-tuple-element.21.own_far_ref), channel_id=1, source_target_pairs={{0,248},{8,16},{16,8},{24,32},{32,24},{40,48},{48,40},{56,64},{64,... | collective-permute-start | bytes 73736 | tf_op jit(solution)/shard_map/ppermute | solution.py:479
  8.7 1.5 %collective-permute-start.1 = (f32[48,128]{1,0:T(8,128)S(1)}, f32[48,128]{1,0:T(8,128)S(1)}, u32[]{:S(2)}, u32[]{:S(2)}) collective-permute-start(f32[48,128]{1,0:T(8,128)S(1)} %get-tuple-element.22.own_near_ref), channel_id=1, source_target_pairs={{0,8},{8,0},{16,24},{24,16},{32,40},{40,32},{48,56},{56,48},{64,72... | collective-permute-start | bytes 73736 | tf_op jit(solution)/shard_map/ppermute | solution.py:479
  8.8 9.2 %copy-start = (f32[16,32,128]{2,1,0:T(8,128)S(1)}, f32[16,32,128]{2,1,0:T(8,128)}, u32[]{:S(2)}) copy-start(f32[16,32,128]{2,1,0:T(8,128)} %t_ref.1) | copy-start | bytes 786436
  8.8 9.2 %copy-start.1 = (f32[16,32,128]{2,1,0:T(8,128)S(1)}, f32[16,32,128]{2,1,0:T(8,128)}, u32[]{:S(2)}) copy-start(f32[16,32,128]{2,1,0:T(8,128)} %s_ref.1) | copy-start | bytes 786436
  8.8 9.2 %copy-start.2 = (f32[16,32,128]{2,1,0:T(8,128)S(1)}, f32[16,32,128]{2,1,0:T(8,128)}, u32[]{:S(2)}) copy-start(f32[16,32,128]{2,1,0:T(8,128)} %u_ref.1) | copy-start | bytes 786436
  8.8 9.2 %copy-start.3 = (f32[16,32,128]{2,1,0:T(8,128)S(1)}, f32[16,32,128]{2,1,0:T(8,128)}, u32[]{:S(2)}) copy-start(f32[16,32,128]{2,1,0:T(8,128)} %v_ref.1) | copy-start | bytes 786436
  8.8 9.2 %copy-start.4 = (s32[16,32,128]{2,1,0:T(8,128)S(1)}, s32[16,32,128]{2,1,0:T(8,128)}, u32[]{:S(2)}) copy-start(s32[16,32,128]{2,1,0:T(8,128)} %wet_ref.1) | copy-start | bytes 786436
  10.3 7.7 %copy-start.5 = (f32[32,128]{1,0:T(8,128)S(1)}, f32[32,128]{1,0:T(8,128)}, u32[]{:S(2)}) copy-start(f32[32,128]{1,0:T(8,128)} %ps_ref.3) | copy-start | bytes 49156
  10.5 13.6 %collective-permute-start.2 = (f32[160,128]{1,0:T(8,128)S(1)}, f32[160,128]{1,0:T(8,128)S(1)}, u32[]{:S(2)}, u32[]{:S(2)}) collective-permute-start(f32[160,128]{1,0:T(8,128)S(1)} %get-tuple-element.25), channel_id=1, source_target_pairs={{0,8},{8,0},{16,24},{24,16},{32,40},{40,32},{48,56},{56,48},{64,72... | collective-permute-start | bytes 245768 | tf_op jit(solution)/shard_map/ppermute | solution.py:479
  10.9 13.2 %collective-permute-start.3 = (f32[160,128]{1,0:T(8,128)S(1)}, f32[160,128]{1,0:T(8,128)S(1)}, u32[]{:S(2)}, u32[]{:S(2)}) collective-permute-start(f32[160,128]{1,0:T(8,128)S(1)} %get-tuple-element.26), channel_id=1, source_target_pairs={{0,1},{8,9},{16,17},{24,25},{32,33},{40,41},{48,49},{56,57},{64,65... | collective-permute-start | bytes 245768 | tf_op jit(solution)/shard_map/ppermute | solution.py:479

commit v3 on v2

--- a/solution.py
+++ b/solution.py
@@ -38,24 +38,17 @@
     return lax.broadcasted_iota(jnp.int32, shape, len(shape) - 1)
 
 
-def fetch(pairs, sems):
-    copies = [pltpu.make_async_copy(src, dst, sems.at[i]) for i, (src, dst) in enumerate(pairs)]
-    for copy in copies:
+def pack_columns(
+    t_hbm, s_hbm, u_hbm, v_hbm, ps_hbm, wet_hbm, near_ref, far_ref, x_ref, wet_ref, ps_ref, sems
+):
+    for index, src in enumerate((t_hbm, s_hbm, u_hbm, v_hbm)):
+        pltpu.make_async_copy(src, x_ref.at[index], sems.at[0]).start()
+    rest = (
+        pltpu.make_async_copy(wet_hbm, wet_ref, sems.at[1]),
+        pltpu.make_async_copy(ps_hbm, ps_ref, sems.at[2]),
+    )
+    for copy in rest:
         copy.start()
-    return copies
-
-
-def pack_columns(
-    t_hbm, s_hbm, u_hbm, v_hbm, ps_hbm, wet_hbm, near_ref, far_ref,
-    t_ref, s_ref, u_ref, v_ref, ps_ref, wet_ref, sems,
-):
-    copies = fetch(
-        (
-            (t_hbm, t_ref), (s_hbm, s_ref), (u_hbm, u_ref), (v_hbm, v_ref),
-            (wet_hbm, wet_ref), (ps_hbm, ps_ref),
-        ),
-        sems,
-    )
     even = lax.axis_index("lon") % 2 == 0
     slot = lanes_of((8, LANES)) >> 1
     masks = [slot == j for j in range(SLOTS)]
@@ -77,10 +70,12 @@
             for j in range(SLOTS)
         ]
 
-    for index, ref in ((COL_T, t_ref), (COL_S, s_ref), (COL_U, u_ref), (COL_V, v_ref), (COL_WET, wet_ref)):
-        copies[index].wait()
-        pack(index, tiles_of(ref))
-    copies[COL_PS].wait()
+    pltpu.make_async_copy(x_ref, x_ref, sems.at[0]).wait()
+    for index in range(4):
+        pack(index, tiles_of(x_ref.at[index]))
+    for copy in rest:
+        copy.wait()
+    pack(COL_WET, tiles_of(wet_ref))
     pack(COL_PS, [(lambda r=r: ps_ref[pl.ds(8 * r, 8), :]) for r in range(BLOCKS)])
 
 
@@ -92,17 +87,18 @@
 def pack_rows(
     t_hbm, s_hbm, u_hbm, v_hbm, ps_hbm, wet_hbm, near_ref, far_ref, x_ref, wet_ref, ps_ref, sems
 ):
-    pairs = [(ps_hbm, ps_ref)]
+    rest = pltpu.make_async_copy(ps_hbm, ps_ref, sems.at[2])
+    rest.start()
     for side, first in ((0, 0), (1, ROWS - 8)):
         for index, src in enumerate((t_hbm, s_hbm, u_hbm, v_hbm)):
-            pairs.append((src.at[:, pl.ds(first, 8), :], x_ref.at[side, index]))
-        pairs.append((wet_hbm.at[:, pl.ds(first, 8), :], wet_ref.at[side]))
-    copies = fetch(pairs, sems)
+            pltpu.make_async_copy(src.at[:, pl.ds(first, 8), :], x_ref.at[side, index], sems.at[0]).start()
+        pltpu.make_async_copy(wet_hbm.at[:, pl.ds(first, 8), :], wet_ref.at[side], sems.at[1]).start()
     lat = lax.axis_index("lat")
     even = lat % 2 == 0
     fold = lat == lax.axis_size("lat") - 1
-    for copy in copies:
-        copy.wait()
+    for ref, sem in ((x_ref, 0), (wet_ref, 1)):
+        pltpu.make_async_copy(ref, ref, sems.at[sem]).wait()
+    rest.wait()
 
     def put(first, north, south, sign):
         rows = pl.ds(first, north.shape[0])
@@ -164,18 +160,22 @@
     return east + west + north + south - 4.0 * centre
 
 
-def march(t, s, u, v, p, wet, coriolis):
-    grad_x = 0.5 * (p[1] - p[2])
-    grad_y = 0.5 * (p[3] - p[4])
+def slopes(u, p):
+    return VISCOSITY * u - 0.5 * p, VISCOSITY * u + 0.5 * p
+
+
+def march(t, s, u, v, p, sides, wet, coriolis):
+    grad_y = 0.5 * (p[0] - p[1])
 
     def tracer(q):
         transport = -0.5 * (u[0] * (q[1] - q[2]) + v[0] * (q[3] - q[4]))
         return wet * (q[0] + TIME_STEP * (transport + DIFFUSIVITY * laplace(q)))
 
+    push = sides[0] + sides[1] + VISCOSITY * (u[1] + u[2]) - 4.0 * VISCOSITY * u[0]
     return (
         tracer(t),
         tracer(s),
-        wet * (u[0] + TIME_STEP * (coriolis * v[0] - grad_x + VISCOSITY * laplace(u))),
+        wet * (u[0] + TIME_STEP * (coriolis * v[0] + push)),
         wet * (v[0] + TIME_STEP * (-coriolis * u[0] - grad_y + VISCOSITY * laplace(v))),
     )
 
@@ -240,22 +240,32 @@
         packed_pressure(tile(q, COL_T), tile(q, COL_S), tile(q, COL_PS), order) for q in (z, z_east, z_west)
     )
 
+    def centred(q):
+        return q, above(q), below(q)
+
     def around(index):
         q = tile(z, index)
         return q, tile(z_east, index), tile(z_west, index), above(q), below(q)
 
     z_one = march(
-        around(COL_T), around(COL_S), around(COL_U), around(COL_V),
-        (zp, zp_east, zp_west, above(zp), below(zp)),
+        around(COL_T), around(COL_S), centred(tile(z, COL_U)), around(COL_V),
+        (above(zp), below(zp)),
+        (slopes(tile(z_east, COL_U), zp_east)[0], slopes(tile(z_west, COL_U), zp_west)[1]),
         tile(z, COL_WET),
         coriolis_of(8 * ((order // 2) % BLOCKS) + sub),
     )
     zp_one = packed_pressure(z_one[0], z_one[1], tile(z, COL_PS), order)
 
+    def packed_slopes(u, p):
+        to_west, to_east = slopes(u, p)
+        return jnp.where(lane % 2 == 1, to_east, to_west)
+
+    z_slopes = packed_slopes(tile(z, COL_U), zp)
+    z_one_slopes = packed_slopes(z_one[2], zp_one)
+
     for side, block, tiles in ((0, 0, even_tile), (1, BLOCKS - 1, odd_tile)):
         psh_ref[side] = pltpu.roll(tile(tiles, COL_PS), LANES - 2 * (block + 1), 1)
 
-    fields = (t_ref, s_ref, u_ref, v_ref)
     outs = (t_hbm, s_hbm, u_hbm, v_hbm, p_hbm)
     blocks = [pl.ds(8 * r, 8) for r in range(BLOCKS)]
     coriolis = [coriolis_of(8 * r + sub) for r in range(BLOCKS)]
@@ -278,22 +288,31 @@
             tiles = odd_tile if r % 2 else even_tile
             side = side_of.get(r)
 
+            def unpack(index):
+                return pltpu.roll(tile(tiles, index), shifts[r], 1)
+
             def parts(index, ref):
-                own = ref[k, rows, :]
-                halo = pltpu.roll(tile(tiles, index), shifts[r], 1)
+                own, halo = ref[k, rows, :], unpack(index)
                 if side is not None:
                     raw_ref[side, index, k] = own
                     rawh_ref[side, index, k] = halo
                 return (own, east_of(own, halo, lane), west_of(own, halo, lane), *vertical(ref, (k,), r, own))
 
-            own = p_ref[rows, :]
-            halo = pltpu.roll(zp, shifts[r], 1)
-            p = (own, east_of(own, halo, lane), west_of(own, halo, lane), *vertical(p_ref, (), r, own))
+            p, u = p_ref[rows, :], u_ref[k, rows, :]
+            halo = pltpu.roll(z_slopes, shifts[r], 1)
+            to_west, to_east = slopes(u, p)
             wet = wet_ref[k, rows, :].astype(jnp.float32)
             if side is not None:
+                raw_ref[side, 2, k] = u
+                rawh_ref[side, 2, k] = unpack(COL_U)
                 raw_ref[side, 4, k] = wet
-                rawh_ref[side, 4, k] = pltpu.roll(tile(tiles, COL_WET), shifts[r], 1)
-            new = march(*(parts(i, ref) for i, ref in enumerate(fields)), p, wet, coriolis[r])
+                rawh_ref[side, 4, k] = unpack(COL_WET)
+            new = march(
+                parts(0, t_ref), parts(1, s_ref), (u, *vertical(u_ref, (k,), r, u)), parts(3, v_ref),
+                vertical(p_ref, (), r, p),
+                (east_of(to_west, halo, lane), west_of(to_east, halo, lane)),
+                wet, coriolis[r],
+            )
             for index in range(4):
                 y_ref[index, rows, :] = new[index]
             heavy = heaviness(new[0], new[1])
@@ -310,11 +329,19 @@
                     oneh_ref[side, index, k] = halo
                 return (own, east_of(own, halo, lane), west_of(own, halo, lane), *vertical(y_ref, (index,), r, own))
 
-            own = q_ref[rows, :]
-            halo = pltpu.roll(zp_one, shifts[r], 1)
-            p = (own, east_of(own, halo, lane), west_of(own, halo, lane), *vertical(q_ref, (), r, own))
+            p, u = q_ref[rows, :], y_ref[2, rows, :]
+            halo = pltpu.roll(z_one_slopes, shifts[r], 1)
+            to_west, to_east = slopes(u, p)
+            if side is not None:
+                one_ref[side, 2, k] = u
+                oneh_ref[side, 2, k] = pltpu.roll(z_one[2], shifts[r], 1)
             wet = wet_ref[k, rows, :].astype(jnp.float32)
-            new = march(*(parts(i) for i in range(4)), p, wet, coriolis[r])
+            new = march(
+                parts(0), parts(1), (u, *vertical(y_ref, (2,), r, u)), parts(3),
+                vertical(q_ref, (), r, p),
+                (east_of(to_west, halo, lane), west_of(to_east, halo, lane)),
+                wet, coriolis[r],
+            )
             for index in range(4):
                 out_ref[index, k, rows, :] = new[index]
             heavy = heaviness(new[0], new[1])
@@ -324,40 +351,20 @@
 
     zero = tuple(jnp.zeros((8, LANES), jnp.float32) for _ in range(BLOCKS))
     running = (zero, zero, zero)
-    copies = []
-    for part in range(PARTS):
-        levels = pl.ds(part * LEVELS // PARTS, LEVELS // PARTS)
+    parts_of = [pl.ds(part * LEVELS // PARTS, LEVELS // PARTS) for part in range(PARTS)]
+    for part, levels in enumerate(parts_of):
         running = lax.fori_loop(part * LEVELS // PARTS, (part + 1) * LEVELS // PARTS, level, running)
         for index, out in enumerate(outs):
-            copy = pltpu.make_async_copy(out_ref.at[index, levels], out.at[levels], sems.at[part, index])
-            copy.start()
-            copies.append(copy)
-    for copy in copies:
-        copy.wait()
+            pltpu.make_async_copy(out_ref.at[index, levels], out.at[levels], sems.at[part]).start()
+    for part, levels in enumerate(parts_of):
+        pltpu.make_async_copy(out_ref.at[:, levels], out_ref.at[:, levels], sems.at[part]).wait()
 
 
 def patch_kernel(
     ps_ref, far_ref, near_ref, raw_ref, rawh_ref, one_ref, oneh_ref, psh_ref, t_in, s_in, u_in, v_in, p_in,
-    t_hbm, s_hbm, u_hbm, v_hbm, p_hbm, block_ref, in_sems, out_sems,
+    t_hbm, s_hbm, u_hbm, v_hbm, p_hbm, block_ref, sems,
 ):
     outs = (t_hbm, s_hbm, u_hbm, v_hbm, p_hbm)
-    firsts = (0, ROWS - 8)
-    loads = [
-        [
-            pltpu.make_async_copy(out.at[:, pl.ds(first, 8), :], block_ref.at[side, index], in_sems.at[side, index])
-            for index, out in enumerate(outs)
-        ]
-        for side, first in enumerate(firsts)
-    ]
-    stores = [
-        [
-            pltpu.make_async_copy(block_ref.at[side, index], out.at[:, pl.ds(first, 8), :], out_sems.at[side, index])
-            for index, out in enumerate(outs)
-        ]
-        for side, first in enumerate(firsts)
-    ]
-    for copy in loads[0] + loads[1]:
-        copy.start()
     lat = lax.axis_index("lat")
     even = lat % 2 == 0
     lane = lanes_of((LEVELS, LANES))
@@ -375,7 +382,7 @@
 
     def side_rows(side, value):
         rows = (0, 1, 2) if side == 0 else (7, 6, 5)
-        at = [firsts[side] + r for r in rows]
+        at = [side * (ROWS - 8) + r for r in rows]
         block = BLOCKS - 1 if side == 0 else 0
 
         def unfold(row):
@@ -417,17 +424,37 @@
         p0h = pressure(edge0h[0], edge0h[1], ps0h)
         p1 = pressure(edge1[0], edge1[1], ps1)
         p1h = pressure(edge1h[0], edge1h[1], ps1h)
+
+        def sides_of(u, uh, p, ph):
+            west, east = slopes(u, p)
+            west_halo, east_halo = slopes(uh, ph)
+            return (
+                (east_of(west, west_halo, lane), west_of(east, east_halo, lane)),
+                (east_of(west_halo, west, lane), west_of(east_halo, east, lane)),
+            )
+
+        def ns(out, inn):
+            return (inn, out) if side == 0 else (out, inn)
+
+        sides_ring, _ = sides_of(ring1[2], corner[2], p_ring1, p_corner)
+        sides0, sides0h = sides_of(edge0[2], edge0h[2], p0, p0h)
         first_ring = march(
-            *(five(ring1[i], corner[i], ring2[i], edge0[i]) for i in range(4)),
-            five(p_ring1, p_corner, p_ring2, p0), wet_ring, cor_ring,
+            *(five(ring1[i], corner[i], ring2[i], edge0[i]) for i in range(2)),
+            (ring1[2], *ns(ring2[2], edge0[2])),
+            five(ring1[3], corner[3], ring2[3], edge0[3]),
+            ns(p_ring2, p0), sides_ring, wet_ring, cor_ring,
         )
         first0 = march(
-            *(five(edge0[i], edge0h[i], ring1[i], edge1[i]) for i in range(4)),
-            five(p0, p0h, p_ring1, p1), edge0[4], cor0,
+            *(five(edge0[i], edge0h[i], ring1[i], edge1[i]) for i in range(2)),
+            (edge0[2], *ns(ring1[2], edge1[2])),
+            five(edge0[3], edge0h[3], ring1[3], edge1[3]),
+            ns(p_ring1, p1), sides0, edge0[4], cor0,
         )
         first0h = march(
-            *(five_halo(edge0[i], edge0h[i], corner[i], edge1h[i]) for i in range(4)),
-            five_halo(p0, p0h, p_corner, p1h), edge0h[4], cor0,
+            *(five_halo(edge0[i], edge0h[i], corner[i], edge1h[i]) for i in range(2)),
+            (edge0h[2], *ns(corner[2], edge1h[2])),
+            five_halo(edge0[3], edge0h[3], corner[3], edge1h[3]),
+            ns(p_corner, p1h), sides0h, edge0h[4], cor0,
         )
         p_ring1 = pressure(first_ring[0], first_ring[1], ps_ring1)
         p0 = pressure(first0[0], first0[1], ps0)
@@ -435,26 +462,32 @@
         p1 = pressure(one1[0], one1[1], ps1)
         p1h = pressure(one1h[0], one1h[1], ps1h)
         p2 = pressure(one2[0], one2[1], ps2)
+        sides0, _ = sides_of(first0[2], first0h[2], p0, p0h)
+        sides1, _ = sides_of(one1[2], one1h[2], p1, p1h)
         second0 = march(
-            *(five(first0[i], first0h[i], first_ring[i], one1[i]) for i in range(4)),
-            five(p0, p0h, p_ring1, p1), edge0[4], cor0,
+            *(five(first0[i], first0h[i], first_ring[i], one1[i]) for i in range(2)),
+            (first0[2], *ns(first_ring[2], one1[2])),
+            five(first0[3], first0h[3], first_ring[3], one1[3]),
+            ns(p_ring1, p1), sides0, edge0[4], cor0,
         )
         second1 = march(
-            *(five(one1[i], one1h[i], first0[i], one2[i]) for i in range(4)),
-            five(p1, p1h, p0, p2), edge1[4], cor1,
+            *(five(one1[i], one1h[i], first0[i], one2[i]) for i in range(2)),
+            (one1[2], *ns(first0[2], one2[2])),
+            five(one1[3], one1h[3], first0[3], one2[3]),
+            ns(p0, p2), sides1, edge1[4], cor1,
         )
         second0 = (*second0, pressure(second0[0], second0[1], ps0))
         second1 = (*second1, pressure(second1[0], second1[1], ps1))
-        for index in range(5):
-            loads[side][index].wait()
-            block_ref[side, index, :, rows[0], :] = second0[index]
-            block_ref[side, index, :, rows[1], :] = second1[index]
-            stores[side][index].start()
+        for index, out in enumerate(outs):
+            block_ref[side, index, :, side, :] = second0[index]
+            block_ref[side, index, :, 1 - side, :] = second1[index]
+            pltpu.make_async_copy(
+                block_ref.at[side, index], out.at[:, pl.ds(side * (ROWS - 2), 2), :], sems.at[0]
+            ).start()
 
     side_rows(0, south)
     side_rows(1, north)
-    for copy in stores[0] + stores[1]:
-        copy.wait()
+    pltpu.make_async_copy(block_ref, block_ref, sems.at[0]).wait()
 
 
 def exchanges(lon_count, lat_count):
@@ -494,7 +527,12 @@
         out_shape=(cols, cols),
         in_specs=[HBM] * 6,
         out_specs=(VMEM, VMEM),
-        scratch_shapes=[pltpu.VMEM(x.shape, x.dtype) for x in inputs] + [pltpu.SemaphoreType.DMA((6,))],
+        scratch_shapes=[
+            pltpu.VMEM((4, *t.shape), jnp.float32),
+            pltpu.VMEM(wet.shape, wet.dtype),
+            pltpu.VMEM(ps.shape, jnp.float32),
+            pltpu.SemaphoreType.DMA((3,)),
+        ],
         compiler_params=grant(6),
     )(*kept)
     block = (LEVELS, 8, LANES)
@@ -507,7 +545,7 @@
             pltpu.VMEM((2, 4, *block), jnp.float32),
             pltpu.VMEM((2, *block), jnp.int32),
             pltpu.VMEM((ROWS, LANES), jnp.float32),
-            pltpu.SemaphoreType.DMA((11,)),
+            pltpu.SemaphoreType.DMA((3,)),
         ],
         compiler_params=grant(4),
     )(*kept)
@@ -539,7 +577,7 @@
             pltpu.VMEM((4, ROWS, LANES), jnp.float32),
             plane,
             pltpu.VMEM((5, *t.shape), jnp.float32),
-            pltpu.SemaphoreType.DMA((PARTS, 5)),
+            pltpu.SemaphoreType.DMA((PARTS,)),
         ],
         compiler_params=grant(12),
     )(*inputs, got_near, got_far, col_near, col_far)
@@ -549,9 +587,8 @@
         in_specs=[VMEM] * 8 + [HBM] * 5,
         out_specs=(HBM,) * 5,
         scratch_shapes=[
-            pltpu.VMEM((2, 5, *block), jnp.float32),
-            pltpu.SemaphoreType.DMA((2, 5)),
-            pltpu.SemaphoreType.DMA((2, 5)),
+            pltpu.VMEM((2, 5, LEVELS, 2, LANES), jnp.float32),
+            pltpu.SemaphoreType.DMA((1,)),
         ],
         input_output_aliases={8 + i: i for i in range(5)},
         compiler_params=grant(8),

time: 27.3 us -> 25.4 us (0.930)
  Pallas kernels: 12.5 us -> 10.6 us
    pallas_call x1, Pallas kernels: 3.04 us -> 1.82 us  [on_device(): pl.pallas_call(patch_kernel, out_shape=(out,) * 5, in_specs=[VMEM] * 8 +...]
    pallas_call x1, Pallas kernels: 6.08 us -> 5.55 us  [on_device(): pl.pallas_call(main_kernel, out_shape=(out,) * 5 + (blocks(5), blocks(5),...]
  transfers between devices with their start and end apart: 4 -> 4, of which waited for: 0 -> 1; matrix products, arithmetic and copies ran while one was open for 0% -> 0% of each run, Pallas kernels for 28% -> 28%
where the time goes in v3:
time: 25.4 us; the launch traced here: 25.3 us
  starting transfers between devices  13.9 us (55%)
  Pallas kernels  10.6 us (42%)
  between operations  0.72 us (3%)
    ppermute x4, starting transfers between devices, swap(): return lax.ppermute(value, ('lon', 'lat'), pairs)  13.9 us
    pallas_call x1, Pallas kernels, on_device(): pl.pallas_call(main_kernel, out_shape=(out,) * 5 + (blocks(5), blocks(5),...  5.55 us
    pallas_call x1, Pallas kernels, on_device(): pl.pallas_call(patch_kernel, out_shape=(out,) * 5, in_specs=[VMEM] * 8 +...  1.82 us
    pallas_call x1, Pallas kernels, on_device(): pl.pallas_call(pack_columns, out_shape=(cols, cols), in_specs=[HBM] * 6,...  1.69 us
    pallas_call x1, Pallas kernels, on_device(): pl.pallas_call(pack_rows, out_shape=(rows, rows), in_specs=[HBM] * 6, out...  1.42 us
  transfers between devices with their start and end apart: 4, of which 1 were waited for; matrix products, arithmetic and copies ran while one was open for 0% of the time, Pallas kernels for 28%

profile of v3, /device:TPU:16, one launch (start us, length us, event | category | flops | bytes accessed | tf_op | source)
XLA Modules:
  0.0 25.3 jit_solution(10307876674660001629)
XLA Ops:
  0.6 1.7 %shard_map.101 = (f32[48,128]{1,0:T(8,128)S(1)}, f32[48,128]{1,0:T(8,128)S(1)}) custom-call(f32[16,32,128]{2,1,0:T(8,128)} %t_ref.1, f32[16,32,128]{2,1,0:T(8,128)} %s_ref.1, f32[16,32,128]{2,1,0:T(8,128)} %u_ref.1, f32[16,32,128]{2,1,0:T(8,128)} %v_ref.1, f32[32,128]{1,0:T(8,128)} %ps_ref.3, s32[16,32,128]{2,1,0:T(8,128)} %wet_ref.1), custom_call_target="tpu_custom_call" | custom-call | tf_op jit(solution)/shard_map/pallas_call | solution.py:525
  2.3 6.3 %collective-permute-start = (f32[48,128]{1,0:T(8,128)S(1)}, f32[48,128]{1,0:T(8,128)S(1)}, u32[]{:S(2)}, u32[]{:S(2)}) collective-permute-start(f32[48,128]{1,0:T(8,128)S(1)} %get-tuple-element.21.own_far_ref), channel_id=1, source_target_pairs={{0,248},{8,16},{16,8},{24,32},{32,24},{40,48},{48,40},{56,64},{64,... | collective-permute-start | bytes 73736 | tf_op jit(solution)/shard_map/ppermute | solution.py:512
  8.7 0.0 collective-permute-start.1
  8.7 0.0 copy-start
  8.7 0.0 copy-start.1
  8.7 0.0 copy-start.2
  8.7 0.0 copy-start.3
  8.7 0.0 copy-start.4
  8.7 1.4 %shard_map.102 = (f32[160,128]{1,0:T(8,128)S(1)}, f32[160,128]{1,0:T(8,128)S(1)}) custom-call(f32[16,32,128]{2,1,0:T(8,128)} %t_ref.1, f32[16,32,128]{2,1,0:T(8,128)} %s_ref.1, f32[16,32,128]{2,1,0:T(8,128)} %u_ref.1, f32[16,32,128]{2,1,0:T(8,128)} %v_ref.1, f32[32,128]{1,0:T(8,128)} %ps_ref.3, s32[16,32,128]{2,1,0:T(8,128)} %wet_ref.1), custom_call_target="tpu_custom_call" | custom-call | tf_op jit(solution)/shard_map/pallas_call | solution.py:539
  10.1 0.1 collective-permute-done.far_ref
  10.2 0.0 collective-permute-done.1.near_ref
  10.2 0.2 shard_map.103
  10.4 0.5 %collective-permute-start.2 = (f32[160,128]{1,0:T(8,128)S(1)}, f32[160,128]{1,0:T(8,128)S(1)}, u32[]{:S(2)}, u32[]{:S(2)}) collective-permute-start(f32[160,128]{1,0:T(8,128)S(1)} %get-tuple-element.25), channel_id=1, source_target_pairs={{0,8},{8,0},{16,24},{24,16},{32,40},{40,32},{48,56},{56,48},{64,72... | collective-permute-start | bytes 245768 | tf_op jit(solution)/shard_map/ppermute | solution.py:512
  10.8 7.1 %collective-permute-start.3 = (f32[160,128]{1,0:T(8,128)S(1)}, f32[160,128]{1,0:T(8,128)S(1)}, u32[]{:S(2)}, u32[]{:S(2)}) collective-permute-start(f32[160,128]{1,0:T(8,128)S(1)} %get-tuple-element.26), channel_id=1, source_target_pairs={{0,1},{8,9},{16,17},{24,25},{32,33},{40,41},{48,49},{56,57},{64,65... | collective-permute-start | bytes 245768 | tf_op jit(solution)/shard_map/ppermute | solution.py:512
  17.9 0.0 copy-done
  17.9 0.0 copy-done.1
  17.9 0.0 copy-done.2
  17.9 0.0 copy-done.3
  17.9 0.0 copy-done.4
  17.9 0.0 copy-done.5
  17.9 5.6 %shard_map.104 = (f32[16,32,128]{2,1,0:T(8,128)}, f32[16,32,128]{2,1,0:T(8,128)}, f32[16,32,128]{2,1,0:T(8,128)}, f32[16,32,128]{2,1,0:T(8,128)}, f32[16,32,128]...) custom-call(f32[16,32,128]{2,1,0:T(8,128)S(1)} %copy-done, ...), custom_call_target="tpu_custom_call" | custom-call | tf_op jit(solution)/shard_map/pallas_call | solution.py:570
  23.5 0.0 collective-permute-done.2.far_ref
  23.5 0.0 collective-permute-done.3.near_ref
  23.5 1.8 %shard_map.105 = (f32[16,32,128]{2,1,0:T(8,128)}, f32[16,32,128]{2,1,0:T(8,128)}, f32[16,32,128]{2,1,0:T(8,128)}, f32[16,32,128]{2,1,0:T(8,128)}, f32[16,32,128]{2,1,0:T(8,128)}) custom-call(f32[32,128]{1,0:T(8,128)S(1)} %copy-done.5, ...), custom_call_target="tpu_custom_call", output_to_operand_aliasing={{0}: (8, {}), {1}: (9, {}), {2}: (10, {}), {3}: (11, {}), {... | custom-call | tf_op jit(solution)/shard_map/pallas_call | solution.py:584
  (1 shorter events, 0.0 us)
Async XLA Ops:
  2.3 7.9 %collective-permute-start = (f32[48,128]{1,0:T(8,128)S(1)}, f32[48,128]{1,0:T(8,128)S(1)}, u32[]{:S(2)}, u32[]{:S(2)}) collective-permute-start(f32[48,128]{1,0:T(8,128)S(1)} %get-tuple-element.21.own_far_ref), channel_id=1, source_target_pairs={{0,248},{8,16},{16,8},{24,32},{32,24},{40,48},{48,40},{56,64},{64,... | collective-permute-start | bytes 73736 | tf_op jit(solution)/shard_map/ppermute | solution.py:512
  8.7 1.5 %collective-permute-start.1 = (f32[48,128]{1,0:T(8,128)S(1)}, f32[48,128]{1,0:T(8,128)S(1)}, u32[]{:S(2)}, u32[]{:S(2)}) collective-permute-start(f32[48,128]{1,0:T(8,128)S(1)} %get-tuple-element.22.own_near_ref), channel_id=1, source_target_pairs={{0,8},{8,0},{16,24},{24,16},{32,40},{40,32},{48,56},{56,48},{64,72... | collective-permute-start | bytes 73736 | tf_op jit(solution)/shard_map/ppermute | solution.py:512
  8.7 9.2 %copy-start = (f32[16,32,128]{2,1,0:T(8,128)S(1)}, f32[16,32,128]{2,1,0:T(8,128)}, u32[]{:S(2)}) copy-start(f32[16,32,128]{2,1,0:T(8,128)} %t_ref.1) | copy-start | bytes 786436
  8.7 9.2 %copy-start.1 = (f32[16,32,128]{2,1,0:T(8,128)S(1)}, f32[16,32,128]{2,1,0:T(8,128)}, u32[]{:S(2)}) copy-start(f32[16,32,128]{2,1,0:T(8,128)} %s_ref.1) | copy-start | bytes 786436
  8.7 9.2 %copy-start.2 = (f32[16,32,128]{2,1,0:T(8,128)S(1)}, f32[16,32,128]{2,1,0:T(8,128)}, u32[]{:S(2)}) copy-start(f32[16,32,128]{2,1,0:T(8,128)} %u_ref.1) | copy-start | bytes 786436
  8.7 9.2 %copy-start.3 = (f32[16,32,128]{2,1,0:T(8,128)S(1)}, f32[16,32,128]{2,1,0:T(8,128)}, u32[]{:S(2)}) copy-start(f32[16,32,128]{2,1,0:T(8,128)} %v_ref.1) | copy-start | bytes 786436
  8.7 9.2 %copy-start.4 = (s32[16,32,128]{2,1,0:T(8,128)S(1)}, s32[16,32,128]{2,1,0:T(8,128)}, u32[]{:S(2)}) copy-start(s32[16,32,128]{2,1,0:T(8,128)} %wet_ref.1) | copy-start | bytes 786436
  10.2 7.7 %copy-start.5 = (f32[32,128]{1,0:T(8,128)S(1)}, f32[32,128]{1,0:T(8,128)}, u32[]{:S(2)}) copy-start(f32[32,128]{1,0:T(8,128)} %ps_ref.3) | copy-start | bytes 49156
  10.4 13.1 %collective-permute-start.2 = (f32[160,128]{1,0:T(8,128)S(1)}, f32[160,128]{1,0:T(8,128)S(1)}, u32[]{:S(2)}, u32[]{:S(2)}) collective-permute-start(f32[160,128]{1,0:T(8,128)S(1)} %get-tuple-element.25), channel_id=1, source_target_pairs={{0,8},{8,0},{16,24},{24,16},{32,40},{40,32},{48,56},{56,48},{64,72... | collective-permute-start | bytes 245768 | tf_op jit(solution)/shard_map/ppermute | solution.py:512
  10.8 12.7 %collective-permute-start.3 = (f32[160,128]{1,0:T(8,128)S(1)}, f32[160,128]{1,0:T(8,128)S(1)}, u32[]{:S(2)}, u32[]{:S(2)}) collective-permute-start(f32[160,128]{1,0:T(8,128)S(1)} %get-tuple-element.26), channel_id=1, source_target_pairs={{0,1},{8,9},{16,17},{24,25},{32,33},{40,41},{48,49},{56,57},{64,65... | collective-permute-start | bytes 245768 | tf_op jit(solution)/shard_map/ppermute | solution.py:512

commit v4 on v3

--- a/solution.py
+++ b/solution.py
@@ -28,7 +28,7 @@
 ROW_CORNER = ROW_PS + 8
 ROW_ROWS = ROW_CORNER + 8
 
-PARTS = 4
+PARTS = ((0, 8), (8, 14), (14, 16))
 
 VMEM = pl.BlockSpec(memory_space=pltpu.VMEM)
 HBM = pl.BlockSpec(memory_space=pltpu.HBM)
@@ -276,13 +276,13 @@
         south = ref[(*lead, pl.ds(8 * r - 1, 8))] if r > 0 else pltpu.roll(centre, 1, 0)
         return north, south
 
-    def level(k, running):
+    def level(k, running, half=0):
         run0, run1, run2 = (list(x) for x in running)
         side_of = {0: 0, BLOCKS - 1: 1}
         shifts = [LANES - 2 - 8 * k - 2 * r for r in range(BLOCKS)]
         for r, rows in enumerate(blocks):
             heavy = heaviness(t_ref[k, rows, :], s_ref[k, rows, :])
-            p_ref[rows, :] = psv[r] + GRAVITY * (run0[r] + 0.5 * heavy)
+            p_ref[half, rows, :] = psv[r] + GRAVITY * (run0[r] + 0.5 * heavy)
             run0[r] = run0[r] + heavy
         for r, rows in enumerate(blocks):
             tiles = odd_tile if r % 2 else even_tile
@@ -298,7 +298,7 @@
                     rawh_ref[side, index, k] = halo
                 return (own, east_of(own, halo, lane), west_of(own, halo, lane), *vertical(ref, (k,), r, own))
 
-            p, u = p_ref[rows, :], u_ref[k, rows, :]
+            p, u = p_ref[half, rows, :], u_ref[k, rows, :]
             halo = pltpu.roll(z_slopes, shifts[r], 1)
             to_west, to_east = slopes(u, p)
             wet = wet_ref[k, rows, :].astype(jnp.float32)
@@ -309,27 +309,27 @@
                 rawh_ref[side, 4, k] = unpack(COL_WET)
             new = march(
                 parts(0, t_ref), parts(1, s_ref), (u, *vertical(u_ref, (k,), r, u)), parts(3, v_ref),
-                vertical(p_ref, (), r, p),
+                vertical(p_ref, (half,), r, p),
                 (east_of(to_west, halo, lane), west_of(to_east, halo, lane)),
                 wet, coriolis[r],
             )
             for index in range(4):
-                y_ref[index, rows, :] = new[index]
+                y_ref[half, index, rows, :] = new[index]
             heavy = heaviness(new[0], new[1])
-            q_ref[rows, :] = psv[r] + GRAVITY * (run1[r] + 0.5 * heavy)
+            q_ref[half, rows, :] = psv[r] + GRAVITY * (run1[r] + 0.5 * heavy)
             run1[r] = run1[r] + heavy
         for r, rows in enumerate(blocks):
             side = side_of.get(r)
 
             def parts(index):
-                own = y_ref[index, rows, :]
+                own = y_ref[half, index, rows, :]
                 halo = pltpu.roll(z_one[index], shifts[r], 1)
                 if side is not None:
                     one_ref[side, index, k] = own
                     oneh_ref[side, index, k] = halo
-                return (own, east_of(own, halo, lane), west_of(own, halo, lane), *vertical(y_ref, (index,), r, own))
-
-            p, u = q_ref[rows, :], y_ref[2, rows, :]
+                return (own, east_of(own, halo, lane), west_of(own, halo, lane), *vertical(y_ref, (half, index), r, own))
+
+            p, u = q_ref[half, rows, :], y_ref[half, 2, rows, :]
             halo = pltpu.roll(z_one_slopes, shifts[r], 1)
             to_west, to_east = slopes(u, p)
             if side is not None:
@@ -337,8 +337,8 @@
                 oneh_ref[side, 2, k] = pltpu.roll(z_one[2], shifts[r], 1)
             wet = wet_ref[k, rows, :].astype(jnp.float32)
             new = march(
-                parts(0), parts(1), (u, *vertical(y_ref, (2,), r, u)), parts(3),
-                vertical(q_ref, (), r, p),
+                parts(0), parts(1), (u, *vertical(y_ref, (half, 2), r, u)), parts(3),
+                vertical(q_ref, (half,), r, p),
                 (east_of(to_west, halo, lane), west_of(to_east, halo, lane)),
                 wet, coriolis[r],
             )
@@ -351,13 +351,17 @@
 
     zero = tuple(jnp.zeros((8, LANES), jnp.float32) for _ in range(BLOCKS))
     running = (zero, zero, zero)
-    parts_of = [pl.ds(part * LEVELS // PARTS, LEVELS // PARTS) for part in range(PARTS)]
-    for part, levels in enumerate(parts_of):
-        running = lax.fori_loop(part * LEVELS // PARTS, (part + 1) * LEVELS // PARTS, level, running)
+    def pair(k, running):
+        return level(2 * k + 1, level(2 * k, running, 0), 1)
+
+    for part, (first, last) in enumerate(PARTS):
+        running = lax.fori_loop(first // 2, last // 2, pair, running)
         for index, out in enumerate(outs):
+            levels = pl.ds(first, last - first)
             pltpu.make_async_copy(out_ref.at[index, levels], out.at[levels], sems.at[part]).start()
-    for part, levels in enumerate(parts_of):
-        pltpu.make_async_copy(out_ref.at[:, levels], out_ref.at[:, levels], sems.at[part]).wait()
+    for part, (first, last) in enumerate(PARTS):
+        whole = out_ref.at[:, pl.ds(first, last - first)]
+        pltpu.make_async_copy(whole, whole, sems.at[part]).wait()
 
 
 def patch_kernel(
@@ -566,7 +570,7 @@
     def blocks(count):
         return jax.ShapeDtypeStruct((2, count, *block), jnp.float32)
 
-    plane = pltpu.VMEM((ROWS, LANES), jnp.float32)
+    plane = pltpu.VMEM((2, ROWS, LANES), jnp.float32)
     *outs, raw, raw_halo, one, one_halo, ps_halo = pl.pallas_call(
         main_kernel,
         out_shape=(out,) * 5 + (blocks(5), blocks(5), blocks(4), blocks(4), jax.ShapeDtypeStruct((2, 8, LANES), jnp.float32)),
@@ -574,10 +578,10 @@
         out_specs=(HBM,) * 5 + (VMEM,) * 5,
         scratch_shapes=[
             plane,
-            pltpu.VMEM((4, ROWS, LANES), jnp.float32),
+            pltpu.VMEM((2, 4, ROWS, LANES), jnp.float32),
             plane,
             pltpu.VMEM((5, *t.shape), jnp.float32),
-            pltpu.SemaphoreType.DMA((PARTS,)),
+            pltpu.SemaphoreType.DMA((len(PARTS),)),
         ],
         compiler_params=grant(12),
     )(*inputs, got_near, got_far, col_near, col_far)

time: 25.4 us -> 24.2 us (0.953)
  Pallas kernels: 10.6 us -> 9.36 us
    pallas_call x1, Pallas kernels: 5.55 us -> 4.27 us  [on_device(): pl.pallas_call(main_kernel, out_shape=(out,) * 5 + (blocks(5), blocks(5),...]
  transfers between devices with their start and end apart: 4 -> 4, of which waited for: 1 -> 1; matrix products, arithmetic and copies ran while one was open for 0% -> 0% of each run, Pallas kernels for 28% -> 24%
where the time goes in v4:
time: 24.2 us; the launch traced here: 24 us
  starting transfers between devices  13.9 us (57%)
  Pallas kernels  9.36 us (39%)
  between operations  0.72 us (3%)
    ppermute x4, starting transfers between devices, swap(): return lax.ppermute(value, ('lon', 'lat'), pairs)  13.9 us
    pallas_call x1, Pallas kernels, on_device(): pl.pallas_call(main_kernel, out_shape=(out,) * 5 + (blocks(5), blocks(5),...  4.27 us
    pallas_call x1, Pallas kernels, on_device(): pl.pallas_call(patch_kernel, out_shape=(out,) * 5, in_specs=[VMEM] * 8 +...  1.82 us
    pallas_call x1, Pallas kernels, on_device(): pl.pallas_call(pack_columns, out_shape=(cols, cols), in_specs=[HBM] * 6,...  1.69 us
    pallas_call x1, Pallas kernels, on_device(): pl.pallas_call(pack_rows, out_shape=(rows, rows), in_specs=[HBM] * 6, out...  1.42 us
  transfers between devices with their start and end apart: 4, of which 1 were waited for; matrix products, arithmetic and copies ran while one was open for 0% of the time, Pallas kernels for 24%

profile of v4, /device:TPU:16, one launch (start us, length us, event | category | flops | bytes accessed | tf_op | source)
XLA Modules:
  0.0 24.0 jit_solution(17813440594142988777)
XLA Ops:
  0.6 1.7 %shard_map.101 = (f32[48,128]{1,0:T(8,128)S(1)}, f32[48,128]{1,0:T(8,128)S(1)}) custom-call(f32[16,32,128]{2,1,0:T(8,128)} %t_ref.1, f32[16,32,128]{2,1,0:T(8,128)} %s_ref.1, f32[16,32,128]{2,1,0:T(8,128)} %u_ref.1, f32[16,32,128]{2,1,0:T(8,128)} %v_ref.1, f32[32,128]{1,0:T(8,128)} %ps_ref.3, s32[16,32,128]{2,1,0:T(8,128)} %wet_ref.1), custom_call_target="tpu_custom_call" | custom-call | tf_op jit(solution)/shard_map/pallas_call | solution.py:529
  2.3 6.3 %collective-permute-start = (f32[48,128]{1,0:T(8,128)S(1)}, f32[48,128]{1,0:T(8,128)S(1)}, u32[]{:S(2)}, u32[]{:S(2)}) collective-permute-start(f32[48,128]{1,0:T(8,128)S(1)} %get-tuple-element.21.own_far_ref), channel_id=1, source_target_pairs={{0,248},{8,16},{16,8},{24,32},{32,24},{40,48},{48,40},{56,64},{64,... | collective-permute-start | bytes 73736 | tf_op jit(solution)/shard_map/ppermute | solution.py:516
  8.7 0.0 collective-permute-start.1
  8.7 0.0 copy-start
  8.7 0.0 copy-start.1
  8.7 0.0 copy-start.2
  8.7 0.0 copy-start.3
  8.7 0.0 copy-start.4
  8.7 1.4 %shard_map.102 = (f32[160,128]{1,0:T(8,128)S(1)}, f32[160,128]{1,0:T(8,128)S(1)}) custom-call(f32[16,32,128]{2,1,0:T(8,128)} %t_ref.1, f32[16,32,128]{2,1,0:T(8,128)} %s_ref.1, f32[16,32,128]{2,1,0:T(8,128)} %u_ref.1, f32[16,32,128]{2,1,0:T(8,128)} %v_ref.1, f32[32,128]{1,0:T(8,128)} %ps_ref.3, s32[16,32,128]{2,1,0:T(8,128)} %wet_ref.1), custom_call_target="tpu_custom_call" | custom-call | tf_op jit(solution)/shard_map/pallas_call | solution.py:543
  10.1 0.1 collective-permute-done.far_ref
  10.2 0.0 collective-permute-done.1.near_ref
  10.2 0.2 shard_map.103
  10.4 0.5 %collective-permute-start.2 = (f32[160,128]{1,0:T(8,128)S(1)}, f32[160,128]{1,0:T(8,128)S(1)}, u32[]{:S(2)}, u32[]{:S(2)}) collective-permute-start(f32[160,128]{1,0:T(8,128)S(1)} %get-tuple-element.25), channel_id=1, source_target_pairs={{0,8},{8,0},{16,24},{24,16},{32,40},{40,32},{48,56},{56,48},{64,72... | collective-permute-start | bytes 245768 | tf_op jit(solution)/shard_map/ppermute | solution.py:516
  10.8 7.1 %collective-permute-start.3 = (f32[160,128]{1,0:T(8,128)S(1)}, f32[160,128]{1,0:T(8,128)S(1)}, u32[]{:S(2)}, u32[]{:S(2)}) collective-permute-start(f32[160,128]{1,0:T(8,128)S(1)} %get-tuple-element.26), channel_id=1, source_target_pairs={{0,1},{8,9},{16,17},{24,25},{32,33},{40,41},{48,49},{56,57},{64,65... | collective-permute-start | bytes 245768 | tf_op jit(solution)/shard_map/ppermute | solution.py:516
  17.9 0.0 copy-done
  17.9 0.0 copy-done.1
  17.9 0.0 copy-done.2
  17.9 0.0 copy-done.3
  17.9 0.0 copy-done.4
  17.9 0.0 copy-done.5
  17.9 4.3 %shard_map.104 = (f32[16,32,128]{2,1,0:T(8,128)}, f32[16,32,128]{2,1,0:T(8,128)}, f32[16,32,128]{2,1,0:T(8,128)}, f32[16,32,128]{2,1,0:T(8,128)}, f32[16,32,128]...) custom-call(f32[16,32,128]{2,1,0:T(8,128)S(1)} %copy-done, ...), custom_call_target="tpu_custom_call" | custom-call | tf_op jit(solution)/shard_map/pallas_call | solution.py:574
  22.2 0.0 collective-permute-done.2.far_ref
  22.2 0.0 collective-permute-done.3.near_ref
  22.2 1.8 %shard_map.105 = (f32[16,32,128]{2,1,0:T(8,128)}, f32[16,32,128]{2,1,0:T(8,128)}, f32[16,32,128]{2,1,0:T(8,128)}, f32[16,32,128]{2,1,0:T(8,128)}, f32[16,32,128]{2,1,0:T(8,128)}) custom-call(f32[32,128]{1,0:T(8,128)S(1)} %copy-done.5, ...), custom_call_target="tpu_custom_call", output_to_operand_aliasing={{0}: (8, {}), {1}: (9, {}), {2}: (10, {}), {3}: (11, {}), {... | custom-call | tf_op jit(solution)/shard_map/pallas_call | solution.py:588
  (1 shorter events, 0.0 us)
Async XLA Ops:
  2.3 7.9 %collective-permute-start = (f32[48,128]{1,0:T(8,128)S(1)}, f32[48,128]{1,0:T(8,128)S(1)}, u32[]{:S(2)}, u32[]{:S(2)}) collective-permute-start(f32[48,128]{1,0:T(8,128)S(1)} %get-tuple-element.21.own_far_ref), channel_id=1, source_target_pairs={{0,248},{8,16},{16,8},{24,32},{32,24},{40,48},{48,40},{56,64},{64,... | collective-permute-start | bytes 73736 | tf_op jit(solution)/shard_map/ppermute | solution.py:516
  8.7 1.5 %collective-permute-start.1 = (f32[48,128]{1,0:T(8,128)S(1)}, f32[48,128]{1,0:T(8,128)S(1)}, u32[]{:S(2)}, u32[]{:S(2)}) collective-permute-start(f32[48,128]{1,0:T(8,128)S(1)} %get-tuple-element.22.own_near_ref), channel_id=1, source_target_pairs={{0,8},{8,0},{16,24},{24,16},{32,40},{40,32},{48,56},{56,48},{64,72... | collective-permute-start | bytes 73736 | tf_op jit(solution)/shard_map/ppermute | solution.py:516
  8.7 9.2 %copy-start = (f32[16,32,128]{2,1,0:T(8,128)S(1)}, f32[16,32,128]{2,1,0:T(8,128)}, u32[]{:S(2)}) copy-start(f32[16,32,128]{2,1,0:T(8,128)} %t_ref.1) | copy-start | bytes 786436
  8.7 9.2 %copy-start.1 = (f32[16,32,128]{2,1,0:T(8,128)S(1)}, f32[16,32,128]{2,1,0:T(8,128)}, u32[]{:S(2)}) copy-start(f32[16,32,128]{2,1,0:T(8,128)} %s_ref.1) | copy-start | bytes 786436
  8.7 9.2 %copy-start.2 = (f32[16,32,128]{2,1,0:T(8,128)S(1)}, f32[16,32,128]{2,1,0:T(8,128)}, u32[]{:S(2)}) copy-start(f32[16,32,128]{2,1,0:T(8,128)} %u_ref.1) | copy-start | bytes 786436
  8.7 9.2 %copy-start.3 = (f32[16,32,128]{2,1,0:T(8,128)S(1)}, f32[16,32,128]{2,1,0:T(8,128)}, u32[]{:S(2)}) copy-start(f32[16,32,128]{2,1,0:T(8,128)} %v_ref.1) | copy-start | bytes 786436
  8.7 9.2 %copy-start.4 = (s32[16,32,128]{2,1,0:T(8,128)S(1)}, s32[16,32,128]{2,1,0:T(8,128)}, u32[]{:S(2)}) copy-start(s32[16,32,128]{2,1,0:T(8,128)} %wet_ref.1) | copy-start | bytes 786436
  10.2 7.7 %copy-start.5 = (f32[32,128]{1,0:T(8,128)S(1)}, f32[32,128]{1,0:T(8,128)}, u32[]{:S(2)}) copy-start(f32[32,128]{1,0:T(8,128)} %ps_ref.3) | copy-start | bytes 49156
  10.4 11.8 %collective-permute-start.2 = (f32[160,128]{1,0:T(8,128)S(1)}, f32[160,128]{1,0:T(8,128)S(1)}, u32[]{:S(2)}, u32[]{:S(2)}) collective-permute-start(f32[160,128]{1,0:T(8,128)S(1)} %get-tuple-element.25), channel_id=1, source_target_pairs={{0,8},{8,0},{16,24},{24,16},{32,40},{40,32},{48,56},{56,48},{64,72... | collective-permute-start | bytes 245768 | tf_op jit(solution)/shard_map/ppermute | solution.py:516
  10.8 11.4 %collective-permute-start.3 = (f32[160,128]{1,0:T(8,128)S(1)}, f32[160,128]{1,0:T(8,128)S(1)}, u32[]{:S(2)}, u32[]{:S(2)}) collective-permute-start(f32[160,128]{1,0:T(8,128)S(1)} %get-tuple-element.26), channel_id=1, source_target_pairs={{0,1},{8,9},{16,17},{24,25},{32,33},{40,41},{48,49},{56,57},{64,65... | collective-permute-start | bytes 245768 | tf_op jit(solution)/shard_map/ppermute | solution.py:516

commit v5 on v4

--- a/solution.py
+++ b/solution.py
@@ -28,7 +28,8 @@
 ROW_CORNER = ROW_PS + 8
 ROW_ROWS = ROW_CORNER + 8
 
-PARTS = ((0, 8), (8, 14), (14, 16))
+PARTS = ((0, 8),)
+LATE = 8
 
 VMEM = pl.BlockSpec(memory_space=pltpu.VMEM)
 HBM = pl.BlockSpec(memory_space=pltpu.HBM)
@@ -209,7 +210,7 @@
 
 def main_kernel(
     t_ref, s_ref, u_ref, v_ref, ps_ref, wet_ref, near_ref, far_ref, own_near_ref, own_far_ref,
-    t_hbm, s_hbm, u_hbm, v_hbm, p_hbm, raw_ref, rawh_ref, one_ref, oneh_ref, psh_ref,
+    t_hbm, s_hbm, u_hbm, v_hbm, p_hbm, raw_ref, rawh_ref, one_ref, oneh_ref, psh_ref, late_ref,
     p_ref, y_ref, q_ref, out_ref, sems,
 ):
     even = lax.axis_index("lon") % 2 == 0
@@ -276,7 +277,7 @@
         south = ref[(*lead, pl.ds(8 * r - 1, 8))] if r > 0 else pltpu.roll(centre, 1, 0)
         return north, south
 
-    def level(k, running, half=0):
+    def level(k, running, half=0, done_ref=None, base=0):
         run0, run1, run2 = (list(x) for x in running)
         side_of = {0: 0, BLOCKS - 1: 1}
         shifts = [LANES - 2 - 8 * k - 2 * r for r in range(BLOCKS)]
@@ -343,32 +344,42 @@
                 wet, coriolis[r],
             )
             for index in range(4):
-                out_ref[index, k, rows, :] = new[index]
+                done_ref[index, k - base, rows, :] = new[index]
             heavy = heaviness(new[0], new[1])
-            out_ref[4, k, rows, :] = psv[r] + GRAVITY * (run2[r] + 0.5 * heavy)
+            done_ref[4, k - base, rows, :] = psv[r] + GRAVITY * (run2[r] + 0.5 * heavy)
             run2[r] = run2[r] + heavy
         return tuple(tuple(x) for x in (run0, run1, run2))
 
     zero = tuple(jnp.zeros((8, LANES), jnp.float32) for _ in range(BLOCKS))
     running = (zero, zero, zero)
-    def pair(k, running):
-        return level(2 * k + 1, level(2 * k, running, 0), 1)
+    def pair(done_ref, base):
+        def run(k, running):
+            running = level(2 * k, running, 0, done_ref, base)
+            return level(2 * k + 1, running, 1, done_ref, base)
+
+        return run
 
     for part, (first, last) in enumerate(PARTS):
-        running = lax.fori_loop(first // 2, last // 2, pair, running)
+        running = lax.fori_loop(first // 2, last // 2, pair(out_ref, 0), running)
         for index, out in enumerate(outs):
             levels = pl.ds(first, last - first)
             pltpu.make_async_copy(out_ref.at[index, levels], out.at[levels], sems.at[part]).start()
+    lax.fori_loop(LATE // 2, LEVELS // 2, pair(late_ref, LATE), running)
     for part, (first, last) in enumerate(PARTS):
         whole = out_ref.at[:, pl.ds(first, last - first)]
         pltpu.make_async_copy(whole, whole, sems.at[part]).wait()
 
 
 def patch_kernel(
-    ps_ref, far_ref, near_ref, raw_ref, rawh_ref, one_ref, oneh_ref, psh_ref, t_in, s_in, u_in, v_in, p_in,
+    ps_ref, far_ref, near_ref, raw_ref, rawh_ref, one_ref, oneh_ref, psh_ref, late_ref, t_in, s_in, u_in, v_in, p_in,
     t_hbm, s_hbm, u_hbm, v_hbm, p_hbm, block_ref, sems,
 ):
     outs = (t_hbm, s_hbm, u_hbm, v_hbm, p_hbm)
+    inner = pl.ds(2, ROWS - 4)
+    for index, out in enumerate(outs):
+        pltpu.make_async_copy(
+            late_ref.at[index, :, inner], out.at[pl.ds(LATE, LEVELS - LATE), inner], sems.at[1]
+        ).start()
     lat = lax.axis_index("lat")
     even = lat % 2 == 0
     lane = lanes_of((LEVELS, LANES))
@@ -492,6 +503,8 @@
     side_rows(0, south)
     side_rows(1, north)
     pltpu.make_async_copy(block_ref, block_ref, sems.at[0]).wait()
+    whole = late_ref.at[:, :, inner]
+    pltpu.make_async_copy(whole, whole, sems.at[1]).wait()
 
 
 def exchanges(lon_count, lat_count):
@@ -570,12 +583,13 @@
     def blocks(count):
         return jax.ShapeDtypeStruct((2, count, *block), jnp.float32)
 
+    left = jax.ShapeDtypeStruct((5, LEVELS - LATE, ROWS, LANES), jnp.float32)
     plane = pltpu.VMEM((2, ROWS, LANES), jnp.float32)
-    *outs, raw, raw_halo, one, one_halo, ps_halo = pl.pallas_call(
+    *outs, raw, raw_halo, one, one_halo, ps_halo, late = pl.pallas_call(
         main_kernel,
-        out_shape=(out,) * 5 + (blocks(5), blocks(5), blocks(4), blocks(4), jax.ShapeDtypeStruct((2, 8, LANES), jnp.float32)),
+        out_shape=(out,) * 5 + (blocks(5), blocks(5), blocks(4), blocks(4), jax.ShapeDtypeStruct((2, 8, LANES), jnp.float32), left),
         in_specs=[VMEM] * 10,
-        out_specs=(HBM,) * 5 + (VMEM,) * 5,
+        out_specs=(HBM,) * 5 + (VMEM,) * 6,
         scratch_shapes=[
             plane,
             pltpu.VMEM((2, 4, ROWS, LANES), jnp.float32),
@@ -588,15 +602,15 @@
     return pl.pallas_call(
         patch_kernel,
         out_shape=(out,) * 5,
-        in_specs=[VMEM] * 8 + [HBM] * 5,
+        in_specs=[VMEM] * 9 + [HBM] * 5,
         out_specs=(HBM,) * 5,
         scratch_shapes=[
             pltpu.VMEM((2, 5, LEVELS, 2, LANES), jnp.float32),
-            pltpu.SemaphoreType.DMA((1,)),
+            pltpu.SemaphoreType.DMA((2,)),
         ],
-        input_output_aliases={8 + i: i for i in range(5)},
+        input_output_aliases={9 + i: i for i in range(5)},
         compiler_params=grant(8),
-    )(ps, row_far, row_near, raw, raw_halo, one, one_halo, ps_halo, *outs)
+    )(ps, row_far, row_near, raw, raw_halo, one, one_halo, ps_halo, late, *outs)
 
 
 def solution(mesh):

time: 24.2 us -> 23.5 us (0.971)
  Pallas kernels: 9.36 us -> 8.71 us
    pallas_call x1, Pallas kernels: 4.27 us -> 3.58 us  [on_device(): pl.pallas_call(main_kernel, out_shape=(out,) * 5 + (blocks(5), blocks(5),...]
  transfers between devices with their start and end apart: 4 -> 4, of which waited for: 1 -> 1; matrix products, arithmetic and copies ran while one was open for 0% -> 0% of each run, Pallas kernels for 24% -> 21%
where the time goes in v5:
time: 23.5 us; the launch traced here: 23.4 us
  starting transfers between devices  13.9 us (59%)
  Pallas kernels  8.71 us (37%)
  between operations  0.72 us (3%)
    ppermute x4, starting transfers between devices, swap(): return lax.ppermute(value, ('lon', 'lat'), pairs)  13.9 us
    pallas_call x1, Pallas kernels, on_device(): pl.pallas_call(main_kernel, out_shape=(out,) * 5 + (blocks(5), blocks(5),...  3.58 us
    pallas_call x1, Pallas kernels, on_device(): pl.pallas_call(patch_kernel, out_shape=(out,) * 5, in_specs=[VMEM] * 9 +...  1.86 us
    pallas_call x1, Pallas kernels, on_device(): pl.pallas_call(pack_columns, out_shape=(cols, cols), in_specs=[HBM] * 6,...  1.69 us
    pallas_call x1, Pallas kernels, on_device(): pl.pallas_call(pack_rows, out_shape=(rows, rows), in_specs=[HBM] * 6, out...  1.42 us
  transfers between devices with their start and end apart: 4, of which 1 were waited for; matrix products, arithmetic and copies ran while one was open for 0% of the time, Pallas kernels for 21%

profile of v5, /device:TPU:16, one launch (start us, length us, event | category | flops | bytes accessed | tf_op | source)
XLA Modules:
  0.0 23.4 jit_solution(537025979248711396)
XLA Ops:
  0.6 1.7 %shard_map.101 = (f32[48,128]{1,0:T(8,128)S(1)}, f32[48,128]{1,0:T(8,128)S(1)}) custom-call(f32[16,32,128]{2,1,0:T(8,128)} %t_ref.1, f32[16,32,128]{2,1,0:T(8,128)} %s_ref.1, f32[16,32,128]{2,1,0:T(8,128)} %u_ref.1, f32[16,32,128]{2,1,0:T(8,128)} %v_ref.1, f32[32,128]{1,0:T(8,128)} %ps_ref.3, s32[16,32,128]{2,1,0:T(8,128)} %wet_ref.1), custom_call_target="tpu_custom_call" | custom-call | tf_op jit(solution)/shard_map/pallas_call | solution.py:542
  2.3 6.3 %collective-permute-start = (f32[48,128]{1,0:T(8,128)S(1)}, f32[48,128]{1,0:T(8,128)S(1)}, u32[]{:S(2)}, u32[]{:S(2)}) collective-permute-start(f32[48,128]{1,0:T(8,128)S(1)} %get-tuple-element.22.own_far_ref), channel_id=1, source_target_pairs={{0,248},{8,16},{16,8},{24,32},{32,24},{40,48},{48,40},{56,64},{64,... | collective-permute-start | bytes 73736 | tf_op jit(solution)/shard_map/ppermute | solution.py:529
  8.7 0.0 collective-permute-start.1
  8.7 0.0 copy-start
  8.7 0.0 copy-start.1
  8.7 0.0 copy-start.2
  8.7 0.0 copy-start.3
  8.7 0.0 copy-start.4
  8.7 1.4 %shard_map.102 = (f32[160,128]{1,0:T(8,128)S(1)}, f32[160,128]{1,0:T(8,128)S(1)}) custom-call(f32[16,32,128]{2,1,0:T(8,128)} %t_ref.1, f32[16,32,128]{2,1,0:T(8,128)} %s_ref.1, f32[16,32,128]{2,1,0:T(8,128)} %u_ref.1, f32[16,32,128]{2,1,0:T(8,128)} %v_ref.1, f32[32,128]{1,0:T(8,128)} %ps_ref.3, s32[16,32,128]{2,1,0:T(8,128)} %wet_ref.1), custom_call_target="tpu_custom_call" | custom-call | tf_op jit(solution)/shard_map/pallas_call | solution.py:556
  10.1 0.1 collective-permute-done.far_ref
  10.2 0.0 collective-permute-done.1.near_ref
  10.2 0.2 shard_map.103
  10.4 0.5 %collective-permute-start.2 = (f32[160,128]{1,0:T(8,128)S(1)}, f32[160,128]{1,0:T(8,128)S(1)}, u32[]{:S(2)}, u32[]{:S(2)}) collective-permute-start(f32[160,128]{1,0:T(8,128)S(1)} %get-tuple-element.26), channel_id=1, source_target_pairs={{0,8},{8,0},{16,24},{24,16},{32,40},{40,32},{48,56},{56,48},{64,72... | collective-permute-start | bytes 245768 | tf_op jit(solution)/shard_map/ppermute | solution.py:529
  10.8 7.1 %collective-permute-start.3 = (f32[160,128]{1,0:T(8,128)S(1)}, f32[160,128]{1,0:T(8,128)S(1)}, u32[]{:S(2)}, u32[]{:S(2)}) collective-permute-start(f32[160,128]{1,0:T(8,128)S(1)} %get-tuple-element.27), channel_id=1, source_target_pairs={{0,1},{8,9},{16,17},{24,25},{32,33},{40,41},{48,49},{56,57},{64,65... | collective-permute-start | bytes 245768 | tf_op jit(solution)/shard_map/ppermute | solution.py:529
  17.9 0.0 copy-done
  17.9 0.0 copy-done.1
  17.9 0.0 copy-done.2
  17.9 0.0 copy-done.3
  17.9 0.0 copy-done.4
  17.9 0.0 copy-done.5
  17.9 3.6 %shard_map.104 = (f32[16,32,128]{2,1,0:T(8,128)}, f32[16,32,128]{2,1,0:T(8,128)}, f32[16,32,128]{2,1,0:T(8,128)}, f32[16,32,128]{2,1,0:T(8,128)}, f32[16,32,128]...) custom-call(f32[16,32,128]{2,1,0:T(8,128)S(1)} %copy-done, ...), custom_call_target="tpu_custom_call" | custom-call | tf_op jit(solution)/shard_map/pallas_call | solution.py:588
  21.5 0.0 collective-permute-done.2.far_ref
  21.5 0.0 collective-permute-done.3.near_ref
  21.5 1.9 %shard_map.105 = (f32[16,32,128]{2,1,0:T(8,128)}, f32[16,32,128]{2,1,0:T(8,128)}, f32[16,32,128]{2,1,0:T(8,128)}, f32[16,32,128]{2,1,0:T(8,128)}, f32[16,32,128]{2,1,0:T(8,128)}) custom-call(f32[32,128]{1,0:T(8,128)S(1)} %copy-done.5, ...), custom_call_target="tpu_custom_call", output_to_operand_aliasing={{0}: (9, {}), {1}: (10, {}), {2}: (11, {}), {3}: (12, {}), ... | custom-call | tf_op jit(solution)/shard_map/pallas_call | solution.py:602
  (1 shorter events, 0.0 us)
Async XLA Ops:
  2.3 7.9 %collective-permute-start = (f32[48,128]{1,0:T(8,128)S(1)}, f32[48,128]{1,0:T(8,128)S(1)}, u32[]{:S(2)}, u32[]{:S(2)}) collective-permute-start(f32[48,128]{1,0:T(8,128)S(1)} %get-tuple-element.22.own_far_ref), channel_id=1, source_target_pairs={{0,248},{8,16},{16,8},{24,32},{32,24},{40,48},{48,40},{56,64},{64,... | collective-permute-start | bytes 73736 | tf_op jit(solution)/shard_map/ppermute | solution.py:529
  8.7 1.5 %collective-permute-start.1 = (f32[48,128]{1,0:T(8,128)S(1)}, f32[48,128]{1,0:T(8,128)S(1)}, u32[]{:S(2)}, u32[]{:S(2)}) collective-permute-start(f32[48,128]{1,0:T(8,128)S(1)} %get-tuple-element.23.own_near_ref), channel_id=1, source_target_pairs={{0,8},{8,0},{16,24},{24,16},{32,40},{40,32},{48,56},{56,48},{64,72... | collective-permute-start | bytes 73736 | tf_op jit(solution)/shard_map/ppermute | solution.py:529
  8.7 9.2 %copy-start = (f32[16,32,128]{2,1,0:T(8,128)S(1)}, f32[16,32,128]{2,1,0:T(8,128)}, u32[]{:S(2)}) copy-start(f32[16,32,128]{2,1,0:T(8,128)} %t_ref.1) | copy-start | bytes 786436
  8.7 9.2 %copy-start.1 = (f32[16,32,128]{2,1,0:T(8,128)S(1)}, f32[16,32,128]{2,1,0:T(8,128)}, u32[]{:S(2)}) copy-start(f32[16,32,128]{2,1,0:T(8,128)} %s_ref.1) | copy-start | bytes 786436
  8.7 9.2 %copy-start.2 = (f32[16,32,128]{2,1,0:T(8,128)S(1)}, f32[16,32,128]{2,1,0:T(8,128)}, u32[]{:S(2)}) copy-start(f32[16,32,128]{2,1,0:T(8,128)} %u_ref.1) | copy-start | bytes 786436
  8.7 9.2 %copy-start.3 = (f32[16,32,128]{2,1,0:T(8,128)S(1)}, f32[16,32,128]{2,1,0:T(8,128)}, u32[]{:S(2)}) copy-start(f32[16,32,128]{2,1,0:T(8,128)} %v_ref.1) | copy-start | bytes 786436
  8.7 9.2 %copy-start.4 = (s32[16,32,128]{2,1,0:T(8,128)S(1)}, s32[16,32,128]{2,1,0:T(8,128)}, u32[]{:S(2)}) copy-start(s32[16,32,128]{2,1,0:T(8,128)} %wet_ref.1) | copy-start | bytes 786436
  10.2 7.7 %copy-start.5 = (f32[32,128]{1,0:T(8,128)S(1)}, f32[32,128]{1,0:T(8,128)}, u32[]{:S(2)}) copy-start(f32[32,128]{1,0:T(8,128)} %ps_ref.3) | copy-start | bytes 49156
  10.4 11.1 %collective-permute-start.2 = (f32[160,128]{1,0:T(8,128)S(1)}, f32[160,128]{1,0:T(8,128)S(1)}, u32[]{:S(2)}, u32[]{:S(2)}) collective-permute-start(f32[160,128]{1,0:T(8,128)S(1)} %get-tuple-element.26), channel_id=1, source_target_pairs={{0,8},{8,0},{16,24},{24,16},{32,40},{40,32},{48,56},{56,48},{64,72... | collective-permute-start | bytes 245768 | tf_op jit(solution)/shard_map/ppermute | solution.py:529
  10.8 10.7 %collective-permute-start.3 = (f32[160,128]{1,0:T(8,128)S(1)}, f32[160,128]{1,0:T(8,128)S(1)}, u32[]{:S(2)}, u32[]{:S(2)}) collective-permute-start(f32[160,128]{1,0:T(8,128)S(1)} %get-tuple-element.27), channel_id=1, source_target_pairs={{0,1},{8,9},{16,17},{24,25},{32,33},{40,41},{48,49},{56,57},{64,65... | collective-permute-start | bytes 245768 | tf_op jit(solution)/shard_map/ppermute | solution.py:529

commit v6 on v5

--- a/solution.py
+++ b/solution.py
@@ -210,7 +210,7 @@
 
 def main_kernel(
     t_ref, s_ref, u_ref, v_ref, ps_ref, wet_ref, near_ref, far_ref, own_near_ref, own_far_ref,
-    t_hbm, s_hbm, u_hbm, v_hbm, p_hbm, raw_ref, rawh_ref, one_ref, oneh_ref, psh_ref, late_ref,
+    t_hbm, s_hbm, u_hbm, v_hbm, p_hbm, raw_ref, rawh_ref, one_ref, oneh_ref, two_ref, psh_ref, late_ref,
     p_ref, y_ref, q_ref, out_ref, sems,
 ):
     even = lax.axis_index("lon") % 2 == 0
@@ -219,7 +219,6 @@
     own_east, own_west = jnp.where(even, own_near, own_far), jnp.where(even, own_far, own_near)
     got_west, got_east = jnp.where(even, far, near), jnp.where(even, near, far)
     odd = lanes_of(near.shape) % 2 == 1
-    even_tile, odd_tile = halo_tiles(near, far, even)
 
     z = jnp.where(odd, got_west, got_east)
     z_east = pltpu.roll(jnp.where(odd, got_east, own_west), LANES - 1, 1)
@@ -231,11 +230,15 @@
     def tile(value, index):
         return value[index * COL_TILE : (index + 1) * COL_TILE]
 
+    block = (order // 2) % BLOCKS
+
     def above(q):
-        return jnp.where(sub == 7, pltpu.roll(pltpu.roll(q, LANES - 2, 1), 7, 0), pltpu.roll(q, 7, 0))
+        beyond = jnp.where(block == BLOCKS - 1, 0.0, pltpu.roll(pltpu.roll(q, LANES - 2, 1), 7, 0))
+        return jnp.where(sub == 7, beyond, pltpu.roll(q, 7, 0))
 
     def below(q):
-        return jnp.where(sub == 0, pltpu.roll(pltpu.roll(q, 2, 1), 1, 0), pltpu.roll(q, 1, 0))
+        beyond = jnp.where(block == 0, 0.0, pltpu.roll(pltpu.roll(q, 2, 1), 1, 0))
+        return jnp.where(sub == 0, beyond, pltpu.roll(q, 1, 0))
 
     zp, zp_east, zp_west = (
         packed_pressure(tile(q, COL_T), tile(q, COL_S), tile(q, COL_PS), order) for q in (z, z_east, z_west)
@@ -253,7 +256,7 @@
         (above(zp), below(zp)),
         (slopes(tile(z_east, COL_U), zp_east)[0], slopes(tile(z_west, COL_U), zp_west)[1]),
         tile(z, COL_WET),
-        coriolis_of(8 * ((order // 2) % BLOCKS) + sub),
+        coriolis_of(8 * block + sub),
     )
     zp_one = packed_pressure(z_one[0], z_one[1], tile(z, COL_PS), order)
 
@@ -264,8 +267,8 @@
     z_slopes = packed_slopes(tile(z, COL_U), zp)
     z_one_slopes = packed_slopes(z_one[2], zp_one)
 
-    for side, block, tiles in ((0, 0, even_tile), (1, BLOCKS - 1, odd_tile)):
-        psh_ref[side] = pltpu.roll(tile(tiles, COL_PS), LANES - 2 * (block + 1), 1)
+    for side, r in ((0, 0), (1, BLOCKS - 1)):
+        psh_ref[side] = pltpu.roll(tile(z, COL_PS), LANES - 2 * (r + 1), 1)
 
     outs = (t_hbm, s_hbm, u_hbm, v_hbm, p_hbm)
     blocks = [pl.ds(8 * r, 8) for r in range(BLOCKS)]
@@ -273,8 +276,16 @@
     psv = [ps_ref[rows, :] for rows in blocks]
 
     def vertical(ref, lead, r, centre):
-        north = ref[(*lead, pl.ds(8 * r + 1, 8))] if r < BLOCKS - 1 else pltpu.roll(centre, 7, 0)
-        south = ref[(*lead, pl.ds(8 * r - 1, 8))] if r > 0 else pltpu.roll(centre, 1, 0)
+        north = (
+            ref[(*lead, pl.ds(8 * r + 1, 8))]
+            if r < BLOCKS - 1
+            else jnp.where(sub == 7, 0.0, pltpu.roll(centre, 7, 0))
+        )
+        south = (
+            ref[(*lead, pl.ds(8 * r - 1, 8))]
+            if r > 0
+            else jnp.where(sub == 0, 0.0, pltpu.roll(centre, 1, 0))
+        )
         return north, south
 
     def level(k, running, half=0, done_ref=None, base=0):
@@ -286,17 +297,17 @@
             p_ref[half, rows, :] = psv[r] + GRAVITY * (run0[r] + 0.5 * heavy)
             run0[r] = run0[r] + heavy
         for r, rows in enumerate(blocks):
-            tiles = odd_tile if r % 2 else even_tile
             side = side_of.get(r)
 
             def unpack(index):
-                return pltpu.roll(tile(tiles, index), shifts[r], 1)
+                return pltpu.roll(tile(z, index), shifts[r], 1)
 
             def parts(index, ref):
                 own, halo = ref[k, rows, :], unpack(index)
                 if side is not None:
                     raw_ref[side, index, k] = own
-                    rawh_ref[side, index, k] = halo
+                    if index == 3:
+                        rawh_ref[side, 0, k] = halo
                 return (own, east_of(own, halo, lane), west_of(own, halo, lane), *vertical(ref, (k,), r, own))
 
             p, u = p_ref[half, rows, :], u_ref[k, rows, :]
@@ -305,9 +316,9 @@
             wet = wet_ref[k, rows, :].astype(jnp.float32)
             if side is not None:
                 raw_ref[side, 2, k] = u
-                rawh_ref[side, 2, k] = unpack(COL_U)
                 raw_ref[side, 4, k] = wet
-                rawh_ref[side, 4, k] = unpack(COL_WET)
+                raw_ref[side, 5, k] = p
+                rawh_ref[side, 1, k] = unpack(COL_WET)
             new = march(
                 parts(0, t_ref), parts(1, s_ref), (u, *vertical(u_ref, (k,), r, u)), parts(3, v_ref),
                 vertical(p_ref, (half,), r, p),
@@ -335,6 +346,7 @@
             to_west, to_east = slopes(u, p)
             if side is not None:
                 one_ref[side, 2, k] = u
+                one_ref[side, 4, k] = p
                 oneh_ref[side, 2, k] = pltpu.roll(z_one[2], shifts[r], 1)
             wet = wet_ref[k, rows, :].astype(jnp.float32)
             new = march(
@@ -345,6 +357,8 @@
             )
             for index in range(4):
                 done_ref[index, k - base, rows, :] = new[index]
+                if side is not None:
+                    two_ref[side, index, k] = new[index]
             heavy = heaviness(new[0], new[1])
             done_ref[4, k - base, rows, :] = psv[r] + GRAVITY * (run2[r] + 0.5 * heavy)
             run2[r] = run2[r] + heavy
@@ -371,7 +385,7 @@
 
 
 def patch_kernel(
-    ps_ref, far_ref, near_ref, raw_ref, rawh_ref, one_ref, oneh_ref, psh_ref, late_ref, t_in, s_in, u_in, v_in, p_in,
+    ps_ref, far_ref, near_ref, raw_ref, rawh_ref, one_ref, oneh_ref, two_ref, psh_ref, late_ref, t_in, s_in, u_in, v_in, p_in,
     t_hbm, s_hbm, u_hbm, v_hbm, p_hbm, block_ref, sems,
 ):
     outs = (t_hbm, s_hbm, u_hbm, v_hbm, p_hbm)
@@ -396,9 +410,10 @@
         return ps + GRAVITY * (total - 0.5 * heavy)
 
     def side_rows(side, value):
-        rows = (0, 1, 2) if side == 0 else (7, 6, 5)
-        at = [side * (ROWS - 8) + r for r in rows]
+        row0, row1 = (0, 1) if side == 0 else (7, 6)
+        first = side * (ROWS - 8)
         block = BLOCKS - 1 if side == 0 else 0
+        toward = 0.5 if side == 0 else -0.5
 
         def unfold(row):
             row = jnp.broadcast_to(pltpu.roll(row, LANES - 2 * (block + 1), 1), (LEVELS, LANES))
@@ -406,90 +421,73 @@
                 row = jnp.where(depth & bit != 0, pltpu.roll(row, LANES - 8 * bit, 1), row)
             return row
 
+        def ns(out, inn):
+            return (inn, out) if side == 0 else (out, inn)
+
         def five(own, halo, out, inn):
-            ns = (inn, out) if side == 0 else (out, inn)
-            return (own, east_of(own, halo, lane), west_of(own, halo, lane), *ns)
-
-        def five_halo(own, halo, out, inn):
-            ns = (inn, out) if side == 0 else (out, inn)
-            return (halo, east_of(halo, own, lane), west_of(halo, own, lane), *ns)
+            return (own, east_of(own, halo, lane), west_of(own, halo, lane), *ns(out, inn))
+
+        def sides_of(u, uh, p, ph):
+            west, east = slopes(u, p)
+            west_halo, east_halo = slopes(uh, ph)
+            return east_of(west, west_halo, lane), west_of(east, east_halo, lane)
+
+        def share(v, wet, beyond, p):
+            wet = TIME_STEP * wet
+            weight = wet * (DIFFUSIVITY + toward * v)
+            return (
+                weight * beyond[0],
+                weight * beyond[1],
+                wet * (VISCOSITY * beyond[2]),
+                wet * (VISCOSITY * beyond[3] + toward * p),
+            )
+
+        def plus(a, b):
+            return [x + y for x, y in zip(a, b)]
 
         ring2 = [value[(2 * i + 1) * LEVELS : (2 * i + 2) * LEVELS] for i in range(4)]
         ring1 = [value[2 * i * LEVELS : (2 * i + 1) * LEVELS] for i in range(4)]
         corner = [unfold(value[ROW_CORNER + i : ROW_CORNER + i + 1]) for i in range(5)]
-        edge0 = [raw_ref[side, i, :, rows[0], :] for i in range(5)]
-        edge0h = [rawh_ref[side, i, :, rows[0], :] for i in range(5)]
-        edge1 = [raw_ref[side, i, :, rows[1], :] for i in range(5)]
-        edge1h = [rawh_ref[side, i, :, rows[1], :] for i in range(4)]
-        one1 = [one_ref[side, i, :, rows[1], :] for i in range(4)]
-        one1h = [oneh_ref[side, i, :, rows[1], :] for i in range(4)]
-        one2 = [one_ref[side, i, :, rows[2], :] for i in range(4)]
+        edge = [raw_ref[side, i, :, row0, :] for i in range(4)]
+        wet0, wet1 = raw_ref[side, 4, :, row0, :], raw_ref[side, 4, :, row1, :]
+        p_edge = raw_ref[side, 5, :, row0, :]
+        v_halo, wet_halo = (rawh_ref[side, i, :, row0, :] for i in range(2))
+        one1 = [one_ref[side, i, :, row1, :] for i in range(4)]
+        p_one1 = one_ref[side, 4, :, row1, :]
         wet_ring = value[ROW_WET : ROW_WET + LEVELS]
         ps_ring2, ps_ring1 = value[ROW_PS + 1 : ROW_PS + 2], value[ROW_PS : ROW_PS + 1]
-        ps_corner = corner[4][0:1]
-        ps0, ps1, ps2 = (ps_ref[pl.ds(a, 1), :] for a in at)
-        ps0h, ps1h = (psh_ref[side, pl.ds(r, 1), :] for r in rows[:2])
-        step = -1 if side == 0 else 1
-        cor_ring, cor0, cor1 = (coriolis_of(jnp.int32(at[0] + d)) for d in (step, 0, -step))
+        ps0, ps1 = (ps_ref[pl.ds(first + row, 1), :] for row in (row0, row1))
+        ps_halo = psh_ref[side, pl.ds(row0, 1), :]
+        cor0 = coriolis_of(jnp.int32(first + row0))
+        cor_ring = coriolis_of(jnp.int32(first + row0 + (-1 if side == 0 else 1)))
 
         p_ring2 = pressure(ring2[0], ring2[1], ps_ring2)
         p_ring1 = pressure(ring1[0], ring1[1], ps_ring1)
-        p_corner = pressure(corner[0], corner[1], ps_corner)
-        p0 = pressure(edge0[0], edge0[1], ps0)
-        p0h = pressure(edge0h[0], edge0h[1], ps0h)
-        p1 = pressure(edge1[0], edge1[1], ps1)
-        p1h = pressure(edge1h[0], edge1h[1], ps1h)
-
-        def sides_of(u, uh, p, ph):
-            west, east = slopes(u, p)
-            west_halo, east_halo = slopes(uh, ph)
-            return (
-                (east_of(west, west_halo, lane), west_of(east, east_halo, lane)),
-                (east_of(west_halo, west, lane), west_of(east_halo, east, lane)),
-            )
-
-        def ns(out, inn):
-            return (inn, out) if side == 0 else (out, inn)
-
-        sides_ring, _ = sides_of(ring1[2], corner[2], p_ring1, p_corner)
-        sides0, sides0h = sides_of(edge0[2], edge0h[2], p0, p0h)
-        first_ring = march(
-            *(five(ring1[i], corner[i], ring2[i], edge0[i]) for i in range(2)),
-            (ring1[2], *ns(ring2[2], edge0[2])),
-            five(ring1[3], corner[3], ring2[3], edge0[3]),
-            ns(p_ring2, p0), sides_ring, wet_ring, cor_ring,
+        p_corner = pressure(corner[0], corner[1], corner[4][0:1])
+        ring = march(
+            *(five(ring1[i], corner[i], ring2[i], edge[i]) for i in range(2)),
+            (ring1[2], *ns(ring2[2], edge[2])),
+            five(ring1[3], corner[3], ring2[3], edge[3]),
+            ns(p_ring2, p_edge),
+            sides_of(ring1[2], corner[2], p_ring1, p_corner),
+            wet_ring, cor_ring,
         )
-        first0 = march(
-            *(five(edge0[i], edge0h[i], ring1[i], edge1[i]) for i in range(2)),
-            (edge0[2], *ns(ring1[2], edge1[2])),
-            five(edge0[3], edge0h[3], ring1[3], edge1[3]),
-            ns(p_ring1, p1), sides0, edge0[4], cor0,
+        added = share(edge[3], wet0, ring1, p_ring1)
+        one0 = plus([one_ref[side, i, :, row0, :] for i in range(4)], added)
+        one0h = plus(
+            [oneh_ref[side, i, :, row0, :] for i in range(4)], share(v_halo, wet_halo, corner, p_corner)
         )
-        first0h = march(
-            *(five_halo(edge0[i], edge0h[i], corner[i], edge1h[i]) for i in range(2)),
-            (edge0h[2], *ns(corner[2], edge1h[2])),
-            five_halo(edge0[3], edge0h[3], corner[3], edge1h[3]),
-            ns(p_corner, p1h), sides0h, edge0h[4], cor0,
+        second0 = march(
+            *(five(one0[i], one0h[i], ring[i], one1[i]) for i in range(2)),
+            (one0[2], *ns(ring[2], one1[2])),
+            five(one0[3], one0h[3], ring[3], one1[3]),
+            ns(pressure(ring[0], ring[1], ps_ring1), p_one1),
+            sides_of(one0[2], one0h[2], pressure(one0[0], one0[1], ps0), pressure(one0h[0], one0h[1], ps_halo)),
+            wet0, cor0,
         )
-        p_ring1 = pressure(first_ring[0], first_ring[1], ps_ring1)
-        p0 = pressure(first0[0], first0[1], ps0)
-        p0h = pressure(first0h[0], first0h[1], ps0h)
-        p1 = pressure(one1[0], one1[1], ps1)
-        p1h = pressure(one1h[0], one1h[1], ps1h)
-        p2 = pressure(one2[0], one2[1], ps2)
-        sides0, _ = sides_of(first0[2], first0h[2], p0, p0h)
-        sides1, _ = sides_of(one1[2], one1h[2], p1, p1h)
-        second0 = march(
-            *(five(first0[i], first0h[i], first_ring[i], one1[i]) for i in range(2)),
-            (first0[2], *ns(first_ring[2], one1[2])),
-            five(first0[3], first0h[3], first_ring[3], one1[3]),
-            ns(p_ring1, p1), sides0, edge0[4], cor0,
-        )
-        second1 = march(
-            *(five(one1[i], one1h[i], first0[i], one2[i]) for i in range(2)),
-            (one1[2], *ns(first0[2], one2[2])),
-            five(one1[3], one1h[3], first0[3], one2[3]),
-            ns(p0, p2), sides1, edge1[4], cor1,
+        second1 = plus(
+            [two_ref[side, i, :, row1, :] for i in range(4)],
+            share(one1[3], wet1, added, pressure(added[0], added[1], 0.0)),
         )
         second0 = (*second0, pressure(second0[0], second0[1], ps0))
         second1 = (*second1, pressure(second1[0], second1[1], ps1))
@@ -585,11 +583,11 @@
 
     left = jax.ShapeDtypeStruct((5, LEVELS - LATE, ROWS, LANES), jnp.float32)
     plane = pltpu.VMEM((2, ROWS, LANES), jnp.float32)
-    *outs, raw, raw_halo, one, one_halo, ps_halo, late = pl.pallas_call(
+    *outs, raw, raw_halo, one, one_halo, two, ps_halo, late = pl.pallas_call(
         main_kernel,
-        out_shape=(out,) * 5 + (blocks(5), blocks(5), blocks(4), blocks(4), jax.ShapeDtypeStruct((2, 8, LANES), jnp.float32), left),
+        out_shape=(out,) * 5 + (blocks(6), blocks(2), blocks(5), blocks(4), blocks(4), jax.ShapeDtypeStruct((2, 8, LANES), jnp.float32), left),
         in_specs=[VMEM] * 10,
-        out_specs=(HBM,) * 5 + (VMEM,) * 6,
+        out_specs=(HBM,) * 5 + (VMEM,) * 7,
         scratch_shapes=[
             plane,
             pltpu.VMEM((2, 4, ROWS, LANES), jnp.float32),
@@ -602,15 +600,15 @@
     return pl.pallas_call(
         patch_kernel,
         out_shape=(out,) * 5,
-        in_specs=[VMEM] * 9 + [HBM] * 5,
+        in_specs=[VMEM] * 10 + [HBM] * 5,
         out_specs=(HBM,) * 5,
         scratch_shapes=[
             pltpu.VMEM((2, 5, LEVELS, 2, LANES), jnp.float32),
             pltpu.SemaphoreType.DMA((2,)),
         ],
-        input_output_aliases={9 + i: i for i in range(5)},
+        input_output_aliases={10 + i: i for i in range(5)},
         compiler_params=grant(8),
-    )(ps, row_far, row_near, raw, raw_halo, one, one_halo, ps_halo, late, *outs)
+    )(ps, row_far, row_near, raw, raw_halo, one, one_halo, two, ps_halo, late, *outs)
 
 
 def solution(mesh):

time: 23.5 us -> 23.2 us (0.987)
  Pallas kernels: 8.71 us -> 8.37 us
    pallas_call x2, Pallas kernels: 5.45 us -> 5.1 us  [the longest x1 3.56 us: on_device(): pl.pallas_call(main_kernel, out_shape=(out,) * 5 + (blocks(6), blocks(2),...]
  transfers between devices with their start and end apart: 4 -> 4, of which waited for: 1 -> 1; matrix products, arithmetic and copies ran while one was open for 0% -> 0% of each run, Pallas kernels for 21% -> 22%
where the time goes in v6:
time: 23.2 us; the launch traced here: 23 us
  starting transfers between devices  13.9 us (60%)
  Pallas kernels  8.37 us (36%)
  between operations  0.72 us (3%)
    ppermute x4, starting transfers between devices, swap(): return lax.ppermute(value, ('lon', 'lat'), pairs)  13.9 us
    pallas_call x1, Pallas kernels, on_device(): pl.pallas_call(main_kernel, out_shape=(out,) * 5 + (blocks(6), blocks(2),...  3.56 us
    pallas_call x1, Pallas kernels, on_device(): pl.pallas_call(pack_columns, out_shape=(cols, cols), in_specs=[HBM] * 6,...  1.69 us
    pallas_call x1, Pallas kernels, on_device(): pl.pallas_call(patch_kernel, out_shape=(out,) * 5, in_specs=[VMEM] * 10 +...  1.55 us
    pallas_call x1, Pallas kernels, on_device(): pl.pallas_call(pack_rows, out_shape=(rows, rows), in_specs=[HBM] * 6, out...  1.42 us
  transfers between devices with their start and end apart: 4, of which 1 were waited for; matrix products, arithmetic and copies ran while one was open for 0% of the time, Pallas kernels for 22%

profile of v6, /device:TPU:16, one launch (start us, length us, event | category | flops | bytes accessed | tf_op | source)
XLA Modules:
  0.0 23.0 jit_solution(5713516159298999120)
XLA Ops:
  0.6 1.7 %shard_map.101 = (f32[48,128]{1,0:T(8,128)S(1)}, f32[48,128]{1,0:T(8,128)S(1)}) custom-call(f32[16,32,128]{2,1,0:T(8,128)} %t_ref.1, f32[16,32,128]{2,1,0:T(8,128)} %s_ref.1, f32[16,32,128]{2,1,0:T(8,128)} %u_ref.1, f32[16,32,128]{2,1,0:T(8,128)} %v_ref.1, f32[32,128]{1,0:T(8,128)} %ps_ref.3, s32[16,32,128]{2,1,0:T(8,128)} %wet_ref.1), custom_call_target="tpu_custom_call" | custom-call | tf_op jit(solution)/shard_map/pallas_call | solution.py:540
  2.3 6.3 %collective-permute-start = (f32[48,128]{1,0:T(8,128)S(1)}, f32[48,128]{1,0:T(8,128)S(1)}, u32[]{:S(2)}, u32[]{:S(2)}) collective-permute-start(f32[48,128]{1,0:T(8,128)S(1)} %get-tuple-element.23.own_far_ref), channel_id=1, source_target_pairs={{0,248},{8,16},{16,8},{24,32},{32,24},{40,48},{48,40},{56,64},{64,... | collective-permute-start | bytes 73736 | tf_op jit(solution)/shard_map/ppermute | solution.py:527
  8.7 0.0 collective-permute-start.1
  8.7 0.0 copy-start
  8.7 0.0 copy-start.1
  8.7 0.0 copy-start.2
  8.7 0.0 copy-start.3
  8.7 0.0 copy-start.4
  8.7 1.4 %shard_map.102 = (f32[160,128]{1,0:T(8,128)S(1)}, f32[160,128]{1,0:T(8,128)S(1)}) custom-call(f32[16,32,128]{2,1,0:T(8,128)} %t_ref.1, f32[16,32,128]{2,1,0:T(8,128)} %s_ref.1, f32[16,32,128]{2,1,0:T(8,128)} %u_ref.1, f32[16,32,128]{2,1,0:T(8,128)} %v_ref.1, f32[32,128]{1,0:T(8,128)} %ps_ref.3, s32[16,32,128]{2,1,0:T(8,128)} %wet_ref.1), custom_call_target="tpu_custom_call" | custom-call | tf_op jit(solution)/shard_map/pallas_call | solution.py:554
  10.1 0.1 collective-permute-done.far_ref
  10.2 0.0 collective-permute-done.1.near_ref
  10.2 0.2 shard_map.103
  10.4 0.5 %collective-permute-start.2 = (f32[160,128]{1,0:T(8,128)S(1)}, f32[160,128]{1,0:T(8,128)S(1)}, u32[]{:S(2)}, u32[]{:S(2)}) collective-permute-start(f32[160,128]{1,0:T(8,128)S(1)} %get-tuple-element.27), channel_id=1, source_target_pairs={{0,8},{8,0},{16,24},{24,16},{32,40},{40,32},{48,56},{56,48},{64,72... | collective-permute-start | bytes 245768 | tf_op jit(solution)/shard_map/ppermute | solution.py:527
  10.8 7.1 %collective-permute-start.3 = (f32[160,128]{1,0:T(8,128)S(1)}, f32[160,128]{1,0:T(8,128)S(1)}, u32[]{:S(2)}, u32[]{:S(2)}) collective-permute-start(f32[160,128]{1,0:T(8,128)S(1)} %get-tuple-element.28), channel_id=1, source_target_pairs={{0,1},{8,9},{16,17},{24,25},{32,33},{40,41},{48,49},{56,57},{64,65... | collective-permute-start | bytes 245768 | tf_op jit(solution)/shard_map/ppermute | solution.py:527
  17.9 0.0 copy-done
  17.9 0.0 copy-done.1
  17.9 0.0 copy-done.2
  17.9 0.0 copy-done.3
  17.9 0.0 copy-done.4
  17.9 0.0 copy-done.5
  17.9 3.6 %shard_map.104 = (f32[16,32,128]{2,1,0:T(8,128)}, f32[16,32,128]{2,1,0:T(8,128)}, f32[16,32,128]{2,1,0:T(8,128)}, f32[16,32,128]{2,1,0:T(8,128)}, f32[16,32,128]...) custom-call(f32[16,32,128]{2,1,0:T(8,128)S(1)} %copy-done, ...), custom_call_target="tpu_custom_call" | custom-call | tf_op jit(solution)/shard_map/pallas_call | solution.py:586
  21.5 0.0 collective-permute-done.2.far_ref
  21.5 0.0 collective-permute-done.3.near_ref
  21.5 1.5 %shard_map.105 = (f32[16,32,128]{2,1,0:T(8,128)}, f32[16,32,128]{2,1,0:T(8,128)}, f32[16,32,128]{2,1,0:T(8,128)}, f32[16,32,128]{2,1,0:T(8,128)}, f32[16,32,128]{2,1,0:T(8,128)}) custom-call(f32[32,128]{1,0:T(8,128)S(1)} %copy-done.5, ...), custom_call_target="tpu_custom_call", output_to_operand_aliasing={{0}: (10, {}), {1}: (11, {}), {2}: (12, {}), {3}: (13, {}),... | custom-call | tf_op jit(solution)/shard_map/pallas_call | solution.py:600
  (1 shorter events, 0.0 us)
Async XLA Ops:
  2.3 7.9 %collective-permute-start = (f32[48,128]{1,0:T(8,128)S(1)}, f32[48,128]{1,0:T(8,128)S(1)}, u32[]{:S(2)}, u32[]{:S(2)}) collective-permute-start(f32[48,128]{1,0:T(8,128)S(1)} %get-tuple-element.23.own_far_ref), channel_id=1, source_target_pairs={{0,248},{8,16},{16,8},{24,32},{32,24},{40,48},{48,40},{56,64},{64,... | collective-permute-start | bytes 73736 | tf_op jit(solution)/shard_map/ppermute | solution.py:527
  8.7 1.5 %collective-permute-start.1 = (f32[48,128]{1,0:T(8,128)S(1)}, f32[48,128]{1,0:T(8,128)S(1)}, u32[]{:S(2)}, u32[]{:S(2)}) collective-permute-start(f32[48,128]{1,0:T(8,128)S(1)} %get-tuple-element.24.own_near_ref), channel_id=1, source_target_pairs={{0,8},{8,0},{16,24},{24,16},{32,40},{40,32},{48,56},{56,48},{64,72... | collective-permute-start | bytes 73736 | tf_op jit(solution)/shard_map/ppermute | solution.py:527
  8.7 9.2 %copy-start = (f32[16,32,128]{2,1,0:T(8,128)S(1)}, f32[16,32,128]{2,1,0:T(8,128)}, u32[]{:S(2)}) copy-start(f32[16,32,128]{2,1,0:T(8,128)} %t_ref.1) | copy-start | bytes 786436
  8.7 9.2 %copy-start.1 = (f32[16,32,128]{2,1,0:T(8,128)S(1)}, f32[16,32,128]{2,1,0:T(8,128)}, u32[]{:S(2)}) copy-start(f32[16,32,128]{2,1,0:T(8,128)} %s_ref.1) | copy-start | bytes 786436
  8.7 9.2 %copy-start.2 = (f32[16,32,128]{2,1,0:T(8,128)S(1)}, f32[16,32,128]{2,1,0:T(8,128)}, u32[]{:S(2)}) copy-start(f32[16,32,128]{2,1,0:T(8,128)} %u_ref.1) | copy-start | bytes 786436
  8.7 9.2 %copy-start.3 = (f32[16,32,128]{2,1,0:T(8,128)S(1)}, f32[16,32,128]{2,1,0:T(8,128)}, u32[]{:S(2)}) copy-start(f32[16,32,128]{2,1,0:T(8,128)} %v_ref.1) | copy-start | bytes 786436
  8.7 9.2 %copy-start.4 = (s32[16,32,128]{2,1,0:T(8,128)S(1)}, s32[16,32,128]{2,1,0:T(8,128)}, u32[]{:S(2)}) copy-start(s32[16,32,128]{2,1,0:T(8,128)} %wet_ref.1) | copy-start | bytes 786436
  10.2 7.7 %copy-start.5 = (f32[32,128]{1,0:T(8,128)S(1)}, f32[32,128]{1,0:T(8,128)}, u32[]{:S(2)}) copy-start(f32[32,128]{1,0:T(8,128)} %ps_ref.3) | copy-start | bytes 49156
  10.4 11.1 %collective-permute-start.2 = (f32[160,128]{1,0:T(8,128)S(1)}, f32[160,128]{1,0:T(8,128)S(1)}, u32[]{:S(2)}, u32[]{:S(2)}) collective-permute-start(f32[160,128]{1,0:T(8,128)S(1)} %get-tuple-element.27), channel_id=1, source_target_pairs={{0,8},{8,0},{16,24},{24,16},{32,40},{40,32},{48,56},{56,48},{64,72... | collective-permute-start | bytes 245768 | tf_op jit(solution)/shard_map/ppermute | solution.py:527
  10.8 10.7 %collective-permute-start.3 = (f32[160,128]{1,0:T(8,128)S(1)}, f32[160,128]{1,0:T(8,128)S(1)}, u32[]{:S(2)}, u32[]{:S(2)}) collective-permute-start(f32[160,128]{1,0:T(8,128)S(1)} %get-tuple-element.28), channel_id=1, source_target_pairs={{0,1},{8,9},{16,17},{24,25},{32,33},{40,41},{48,49},{56,57},{64,65... | collective-permute-start | bytes 245768 | tf_op jit(solution)/shard_map/ppermute | solution.py:527

commit v7 on v6

--- a/solution.py
+++ b/solution.py
@@ -28,8 +28,8 @@
 ROW_CORNER = ROW_PS + 8
 ROW_ROWS = ROW_CORNER + 8
 
-PARTS = ((0, 8),)
-LATE = 8
+PARTS = ((0, 10),)
+LATE = 10
 
 VMEM = pl.BlockSpec(memory_space=pltpu.VMEM)
 HBM = pl.BlockSpec(memory_space=pltpu.HBM)
@@ -52,15 +52,17 @@
         copy.start()
     even = lax.axis_index("lon") % 2 == 0
     slot = lanes_of((8, LANES)) >> 1
-    masks = [slot == j for j in range(SLOTS)]
+    pair = slot >> 1
+    odd_pair = ((slot + SLOTS - 1) & (SLOTS - 1)) >> 1
+    split = slot & 1 == 0
 
     def pack(index, tiles):
-        east = jnp.zeros((8, LANES), jnp.float32)
-        west = jnp.zeros((8, LANES), jnp.float32)
+        merged = [jnp.zeros((8, LANES), jnp.float32)] * 2
         for j, tile in enumerate(tiles):
             rolled = pltpu.roll(tile(), (2 * j + 2) % LANES, 1)
-            east = jnp.where(masks[j], rolled, east)
-            west = jnp.where(masks[(j + 1) % SLOTS], rolled, west)
+            merged[j % 2] = jnp.where((odd_pair if j % 2 else pair) == j // 2, rolled, merged[j % 2])
+        east = jnp.where(split, merged[0], merged[1])
+        west = jnp.where(split, merged[1], merged[0])
         rows = pl.ds(index * COL_TILE, COL_TILE)
         near_ref[rows, :] = jnp.where(even, east, west)
         far_ref[rows, :] = jnp.where(even, west, east)
@@ -275,6 +277,18 @@
     coriolis = [coriolis_of(8 * r + sub) for r in range(BLOCKS)]
     psv = [ps_ref[rows, :] for rows in blocks]
 
+    padded = [pl.ds(8 * r + 8, 8) for r in range(BLOCKS)]
+    blank = jnp.zeros((8, LANES), jnp.float32)
+    for half in range(2):
+        for pad in (pl.ds(0, 8), pl.ds(ROWS + 8, 8)):
+            p_ref[half, pad, :] = blank
+            q_ref[half, pad, :] = blank
+            for index in range(4):
+                y_ref[half, index, pad, :] = blank
+
+    def beside(ref, lead, r):
+        return ref[(*lead, pl.ds(8 * r + 9, 8))], ref[(*lead, pl.ds(8 * r + 7, 8))]
+
     def vertical(ref, lead, r, centre):
         north = (
             ref[(*lead, pl.ds(8 * r + 1, 8))]
@@ -294,7 +308,7 @@
         shifts = [LANES - 2 - 8 * k - 2 * r for r in range(BLOCKS)]
         for r, rows in enumerate(blocks):
             heavy = heaviness(t_ref[k, rows, :], s_ref[k, rows, :])
-            p_ref[half, rows, :] = psv[r] + GRAVITY * (run0[r] + 0.5 * heavy)
+            p_ref[half, padded[r], :] = psv[r] + GRAVITY * (run0[r] + 0.5 * heavy)
             run0[r] = run0[r] + heavy
         for r, rows in enumerate(blocks):
             side = side_of.get(r)
@@ -310,7 +324,7 @@
                         rawh_ref[side, 0, k] = halo
                 return (own, east_of(own, halo, lane), west_of(own, halo, lane), *vertical(ref, (k,), r, own))
 
-            p, u = p_ref[half, rows, :], u_ref[k, rows, :]
+            p, u = p_ref[half, padded[r], :], u_ref[k, rows, :]
             halo = pltpu.roll(z_slopes, shifts[r], 1)
             to_west, to_east = slopes(u, p)
             wet = wet_ref[k, rows, :].astype(jnp.float32)
@@ -321,27 +335,27 @@
                 rawh_ref[side, 1, k] = unpack(COL_WET)
             new = march(
                 parts(0, t_ref), parts(1, s_ref), (u, *vertical(u_ref, (k,), r, u)), parts(3, v_ref),
-                vertical(p_ref, (half,), r, p),
+                beside(p_ref, (half,), r),
                 (east_of(to_west, halo, lane), west_of(to_east, halo, lane)),
                 wet, coriolis[r],
             )
             for index in range(4):
-                y_ref[half, index, rows, :] = new[index]
+                y_ref[half, index, padded[r], :] = new[index]
             heavy = heaviness(new[0], new[1])
-            q_ref[half, rows, :] = psv[r] + GRAVITY * (run1[r] + 0.5 * heavy)
+            q_ref[half, padded[r], :] = psv[r] + GRAVITY * (run1[r] + 0.5 * heavy)
             run1[r] = run1[r] + heavy
         for r, rows in enumerate(blocks):
             side = side_of.get(r)
 
             def parts(index):
-                own = y_ref[half, index, rows, :]
+                own = y_ref[half, index, padded[r], :]
                 halo = pltpu.roll(z_one[index], shifts[r], 1)
                 if side is not None:
                     one_ref[side, index, k] = own
                     oneh_ref[side, index, k] = halo
-                return (own, east_of(own, halo, lane), west_of(own, halo, lane), *vertical(y_ref, (half, index), r, own))
-
-            p, u = q_ref[half, rows, :], y_ref[half, 2, rows, :]
+                return (own, east_of(own, halo, lane), west_of(own, halo, lane), *beside(y_ref, (half, index), r))
+
+            p, u = q_ref[half, padded[r], :], y_ref[half, 2, padded[r], :]
             halo = pltpu.roll(z_one_slopes, shifts[r], 1)
             to_west, to_east = slopes(u, p)
             if side is not None:
@@ -350,8 +364,8 @@
                 oneh_ref[side, 2, k] = pltpu.roll(z_one[2], shifts[r], 1)
             wet = wet_ref[k, rows, :].astype(jnp.float32)
             new = march(
-                parts(0), parts(1), (u, *vertical(y_ref, (half, 2), r, u)), parts(3),
-                vertical(q_ref, (half,), r, p),
+                parts(0), parts(1), (u, *beside(y_ref, (half, 2), r)), parts(3),
+                beside(q_ref, (half,), r),
                 (east_of(to_west, halo, lane), west_of(to_east, halo, lane)),
                 wet, coriolis[r],
             )
@@ -582,7 +596,7 @@
         return jax.ShapeDtypeStruct((2, count, *block), jnp.float32)
 
     left = jax.ShapeDtypeStruct((5, LEVELS - LATE, ROWS, LANES), jnp.float32)
-    plane = pltpu.VMEM((2, ROWS, LANES), jnp.float32)
+    plane = pltpu.VMEM((2, ROWS + 16, LANES), jnp.float32)
     *outs, raw, raw_halo, one, one_halo, two, ps_halo, late = pl.pallas_call(
         main_kernel,
         out_shape=(out,) * 5 + (blocks(6), blocks(2), blocks(5), blocks(4), blocks(4), jax.ShapeDtypeStruct((2, 8, LANES), jnp.float32), left),
@@ -590,7 +604,7 @@
         out_specs=(HBM,) * 5 + (VMEM,) * 7,
         scratch_shapes=[
             plane,
-            pltpu.VMEM((2, 4, ROWS, LANES), jnp.float32),
+            pltpu.VMEM((2, 4, ROWS + 16, LANES), jnp.float32),
             plane,
             pltpu.VMEM((5, *t.shape), jnp.float32),
             pltpu.SemaphoreType.DMA((len(PARTS),)),

time: 23.2 us -> 23.2 us (level)
  no operation moved by 1% of the time
where the time goes in v7:
time: 23.2 us; the launch traced here: 23 us
  starting transfers between devices  13.9 us (60%)
  Pallas kernels  8.36 us (36%)
  between operations  0.72 us (3%)
    ppermute x4, starting transfers between devices, swap(): return lax.ppermute(value, ('lon', 'lat'), pairs)  13.9 us
    pallas_call x1, Pallas kernels, on_device(): pl.pallas_call(main_kernel, out_shape=(out,) * 5 + (blocks(6), blocks(2),...  3.55 us
    pallas_call x1, Pallas kernels, on_device(): pl.pallas_call(pack_columns, out_shape=(cols, cols), in_specs=[HBM] * 6,...  1.69 us
    pallas_call x1, Pallas kernels, on_device(): pl.pallas_call(patch_kernel, out_shape=(out,) * 5, in_specs=[VMEM] * 10 +...  1.55 us
    pallas_call x1, Pallas kernels, on_device(): pl.pallas_call(pack_rows, out_shape=(rows, rows), in_specs=[HBM] * 6, out...  1.42 us
  transfers between devices with their start and end apart: 4, of which 1 were waited for; matrix products, arithmetic and copies ran while one was open for 0% of the time, Pallas kernels for 22%

profile of v7, /device:TPU:16, one launch (start us, length us, event | category | flops | bytes accessed | tf_op | source)
XLA Modules:
  0.0 23.0 jit_solution(5128285611975653844)
XLA Ops:
  0.6 1.7 %shard_map.101 = (f32[48,128]{1,0:T(8,128)S(1)}, f32[48,128]{1,0:T(8,128)S(1)}) custom-call(f32[16,32,128]{2,1,0:T(8,128)} %t_ref.1, f32[16,32,128]{2,1,0:T(8,128)} %s_ref.1, f32[16,32,128]{2,1,0:T(8,128)} %u_ref.1, f32[16,32,128]{2,1,0:T(8,128)} %v_ref.1, f32[32,128]{1,0:T(8,128)} %ps_ref.3, s32[16,32,128]{2,1,0:T(8,128)} %wet_ref.1), custom_call_target="tpu_custom_call" | custom-call | tf_op jit(solution)/shard_map/pallas_call | solution.py:554
  2.3 6.3 %collective-permute-start = (f32[48,128]{1,0:T(8,128)S(1)}, f32[48,128]{1,0:T(8,128)S(1)}, u32[]{:S(2)}, u32[]{:S(2)}) collective-permute-start(f32[48,128]{1,0:T(8,128)S(1)} %get-tuple-element.23.own_far_ref), channel_id=1, source_target_pairs={{0,248},{8,16},{16,8},{24,32},{32,24},{40,48},{48,40},{56,64},{64,... | collective-permute-start | bytes 73736 | tf_op jit(solution)/shard_map/ppermute | solution.py:541
  8.7 0.0 collective-permute-start.1
  8.7 0.0 copy-start
  8.7 0.0 copy-start.1
  8.7 0.0 copy-start.2
  8.7 0.0 copy-start.3
  8.7 0.0 copy-start.4
  8.7 1.4 %shard_map.102 = (f32[160,128]{1,0:T(8,128)S(1)}, f32[160,128]{1,0:T(8,128)S(1)}) custom-call(f32[16,32,128]{2,1,0:T(8,128)} %t_ref.1, f32[16,32,128]{2,1,0:T(8,128)} %s_ref.1, f32[16,32,128]{2,1,0:T(8,128)} %u_ref.1, f32[16,32,128]{2,1,0:T(8,128)} %v_ref.1, f32[32,128]{1,0:T(8,128)} %ps_ref.3, s32[16,32,128]{2,1,0:T(8,128)} %wet_ref.1), custom_call_target="tpu_custom_call" | custom-call | tf_op jit(solution)/shard_map/pallas_call | solution.py:568
  10.1 0.1 collective-permute-done.far_ref
  10.2 0.0 collective-permute-done.1.near_ref
  10.2 0.2 shard_map.103
  10.4 0.5 %collective-permute-start.2 = (f32[160,128]{1,0:T(8,128)S(1)}, f32[160,128]{1,0:T(8,128)S(1)}, u32[]{:S(2)}, u32[]{:S(2)}) collective-permute-start(f32[160,128]{1,0:T(8,128)S(1)} %get-tuple-element.27), channel_id=1, source_target_pairs={{0,8},{8,0},{16,24},{24,16},{32,40},{40,32},{48,56},{56,48},{64,72... | collective-permute-start | bytes 245768 | tf_op jit(solution)/shard_map/ppermute | solution.py:541
  10.8 7.1 %collective-permute-start.3 = (f32[160,128]{1,0:T(8,128)S(1)}, f32[160,128]{1,0:T(8,128)S(1)}, u32[]{:S(2)}, u32[]{:S(2)}) collective-permute-start(f32[160,128]{1,0:T(8,128)S(1)} %get-tuple-element.28), channel_id=1, source_target_pairs={{0,1},{8,9},{16,17},{24,25},{32,33},{40,41},{48,49},{56,57},{64,65... | collective-permute-start | bytes 245768 | tf_op jit(solution)/shard_map/ppermute | solution.py:541
  17.9 0.0 copy-done
  17.9 0.0 copy-done.1
  17.9 0.0 copy-done.2
  17.9 0.0 copy-done.3
  17.9 0.0 copy-done.4
  17.9 0.0 copy-done.5
  17.9 3.5 %shard_map.104 = (f32[16,32,128]{2,1,0:T(8,128)}, f32[16,32,128]{2,1,0:T(8,128)}, f32[16,32,128]{2,1,0:T(8,128)}, f32[16,32,128]{2,1,0:T(8,128)}, f32[16,32,128]...) custom-call(f32[16,32,128]{2,1,0:T(8,128)S(1)} %copy-done, ...), custom_call_target="tpu_custom_call" | custom-call | tf_op jit(solution)/shard_map/pallas_call | solution.py:600
  21.5 0.0 collective-permute-done.2.far_ref
  21.5 0.0 collective-permute-done.3.near_ref
  21.5 1.5 %shard_map.105 = (f32[16,32,128]{2,1,0:T(8,128)}, f32[16,32,128]{2,1,0:T(8,128)}, f32[16,32,128]{2,1,0:T(8,128)}, f32[16,32,128]{2,1,0:T(8,128)}, f32[16,32,128]{2,1,0:T(8,128)}) custom-call(f32[32,128]{1,0:T(8,128)S(1)} %copy-done.5, ...), custom_call_target="tpu_custom_call", output_to_operand_aliasing={{0}: (10, {}), {1}: (11, {}), {2}: (12, {}), {3}: (13, {}),... | custom-call | tf_op jit(solution)/shard_map/pallas_call | solution.py:614
  (1 shorter events, 0.0 us)
Async XLA Ops:
  2.3 7.9 %collective-permute-start = (f32[48,128]{1,0:T(8,128)S(1)}, f32[48,128]{1,0:T(8,128)S(1)}, u32[]{:S(2)}, u32[]{:S(2)}) collective-permute-start(f32[48,128]{1,0:T(8,128)S(1)} %get-tuple-element.23.own_far_ref), channel_id=1, source_target_pairs={{0,248},{8,16},{16,8},{24,32},{32,24},{40,48},{48,40},{56,64},{64,... | collective-permute-start | bytes 73736 | tf_op jit(solution)/shard_map/ppermute | solution.py:541
  8.7 1.5 %collective-permute-start.1 = (f32[48,128]{1,0:T(8,128)S(1)}, f32[48,128]{1,0:T(8,128)S(1)}, u32[]{:S(2)}, u32[]{:S(2)}) collective-permute-start(f32[48,128]{1,0:T(8,128)S(1)} %get-tuple-element.24.own_near_ref), channel_id=1, source_target_pairs={{0,8},{8,0},{16,24},{24,16},{32,40},{40,32},{48,56},{56,48},{64,72... | collective-permute-start | bytes 73736 | tf_op jit(solution)/shard_map/ppermute | solution.py:541
  8.7 9.2 %copy-start = (f32[16,32,128]{2,1,0:T(8,128)S(1)}, f32[16,32,128]{2,1,0:T(8,128)}, u32[]{:S(2)}) copy-start(f32[16,32,128]{2,1,0:T(8,128)} %t_ref.1) | copy-start | bytes 786436
  8.7 9.2 %copy-start.1 = (f32[16,32,128]{2,1,0:T(8,128)S(1)}, f32[16,32,128]{2,1,0:T(8,128)}, u32[]{:S(2)}) copy-start(f32[16,32,128]{2,1,0:T(8,128)} %s_ref.1) | copy-start | bytes 786436
  8.7 9.2 %copy-start.2 = (f32[16,32,128]{2,1,0:T(8,128)S(1)}, f32[16,32,128]{2,1,0:T(8,128)}, u32[]{:S(2)}) copy-start(f32[16,32,128]{2,1,0:T(8,128)} %u_ref.1) | copy-start | bytes 786436
  8.7 9.2 %copy-start.3 = (f32[16,32,128]{2,1,0:T(8,128)S(1)}, f32[16,32,128]{2,1,0:T(8,128)}, u32[]{:S(2)}) copy-start(f32[16,32,128]{2,1,0:T(8,128)} %v_ref.1) | copy-start | bytes 786436
  8.7 9.2 %copy-start.4 = (s32[16,32,128]{2,1,0:T(8,128)S(1)}, s32[16,32,128]{2,1,0:T(8,128)}, u32[]{:S(2)}) copy-start(s32[16,32,128]{2,1,0:T(8,128)} %wet_ref.1) | copy-start | bytes 786436
  10.2 7.7 %copy-start.5 = (f32[32,128]{1,0:T(8,128)S(1)}, f32[32,128]{1,0:T(8,128)}, u32[]{:S(2)}) copy-start(f32[32,128]{1,0:T(8,128)} %ps_ref.3) | copy-start | bytes 49156
  10.4 11.1 %collective-permute-start.2 = (f32[160,128]{1,0:T(8,128)S(1)}, f32[160,128]{1,0:T(8,128)S(1)}, u32[]{:S(2)}, u32[]{:S(2)}) collective-permute-start(f32[160,128]{1,0:T(8,128)S(1)} %get-tuple-element.27), channel_id=1, source_target_pairs={{0,8},{8,0},{16,24},{24,16},{32,40},{40,32},{48,56},{56,48},{64,72... | collective-permute-start | bytes 245768 | tf_op jit(solution)/shard_map/ppermute | solution.py:541
  10.8 10.7 %collective-permute-start.3 = (f32[160,128]{1,0:T(8,128)S(1)}, f32[160,128]{1,0:T(8,128)S(1)}, u32[]{:S(2)}, u32[]{:S(2)}) collective-permute-start(f32[160,128]{1,0:T(8,128)S(1)} %get-tuple-element.28), channel_id=1, source_target_pairs={{0,1},{8,9},{16,17},{24,25},{32,33},{40,41},{48,49},{56,57},{64,65... | collective-permute-start | bytes 245768 | tf_op jit(solution)/shard_map/ppermute | solution.py:541
